TPU v7x, 256 devices: a whole 4x4x8 slice. The times are simulated.
256 devices in a mesh: sec: 32 (over x, z), term: 8 (over y, core).
Axes of the slice: x: 4, y: 4, z: 8, core: 2. Of those that a mesh axis runs over, the one named last changes fastest.
Arguments:
- psi_blocks: float32 [256, 256, 256], P('sec'), may hold values from -6 to 6
- left_env: float32 [16, 256, 256, 256], P('term', 'sec'), may hold values from -0.1875 to 0.1875
- right_env: float32 [16, 256, 256, 256], P('term', 'sec'), may hold values from -0.75 to 0.75
- left_sizes: int32 [256], P('sec'), may hold values from 1 to 256, 16384 in all
- right_sizes: int32 [256], P('sec'), may hold values from 1 to 256, 16384 in all
- dest_sector: int32 [16, 256], P('term', 'sec'), may hold values from 0 to 255, as said below
Outputs:
- sigma_blocks: float32 [256, 256, 256], P('sec')
Inputs may be any that keep to these rules, and one draw needn't show every extreme that they name: `left_sizes`: the entries sum to 16384, and the largest equals 256. `right_sizes`: the entries sum to 16384, and the largest equals 256. For every term t, dest_sector[t] is a permutation of the 256 sectors; sector s is held by index s // 8 of sec; of the 16 pairs (term, sector) held by one device, at most 1 reach sectors held by any one index of sec, and exactly 1 reach some index.
All inputs are finite; a program needn't handle non-finite values. No bound on the sum of `left_sizes` or of `right_sizes` on one device may be relied on, other than what follows from the above.
Results may differ from a plain program's by a relative error of at most 0.0001.
Values sent between devices are 32-bit elements; how exact they have to be, the bound alone decides.
No kernel may reach another device: no remote copies, remote signals or barrier semaphores. Data moves between devices by JAX's collectives and lax.ppermute only.
A program may use at most 128 MiB of HBM per device.

v0:
```python
import jax
import jax.numpy as jnp
from jax import lax
from jax.sharding import PartitionSpec as P


def sector_mask(left_sizes, right_sizes, block_size):
    positions = jnp.arange(block_size, dtype=jnp.int32)
    row_ok = positions[None, :, None] < left_sizes[:, None, None]
    col_ok = positions[None, None, :] < right_sizes[:, None, None]
    return (row_ok & col_ok).astype(jnp.float32)


def pack_blocks(outgoing, targets, term_ids, sector_local, capacity, slot_count):
    target_device = targets // sector_local
    target_place = targets % sector_local
    count_out = targets.shape[0]
    order_index = jnp.arange(count_out, dtype=jnp.int32)
    same_device = target_device[:, None] == target_device[None, :]
    earlier = order_index[None, :] < order_index[:, None]
    peer_rank = jnp.sum((same_device & earlier).astype(jnp.int32), axis=1)
    send_slot = target_device * capacity + peer_rank
    chosen = jnp.arange(slot_count, dtype=jnp.int32)[:, None] == send_slot[None, :]
    slot_source = jnp.sum(jnp.where(chosen, order_index[None, :], 0), axis=1)
    filled = jnp.any(chosen, axis=1)
    buffer = jnp.where(filled[:, None, None], outgoing[slot_source], 0.0)
    left_code = term_ids * sector_local + target_place
    meta_codes = jnp.where(filled, left_code[slot_source], -1)
    return (buffer, meta_codes)


def apply_left(received, meta_codes, flat_left, sector_local, live_count):
    slot_count = meta_codes.shape[0]
    is_valid = meta_codes >= 0
    live_rank = jnp.cumsum(is_valid.astype(jnp.int32)) - 1
    wanted = jnp.arange(live_count, dtype=jnp.int32)
    picked = (live_rank[None, :] == wanted[:, None]) & is_valid[None, :]
    slot_index = jnp.arange(slot_count, dtype=jnp.int32)
    source_slot = jnp.sum(jnp.where(picked, slot_index[None, :], 0), axis=1)
    compact_blocks = received[source_slot]
    compact_codes = meta_codes[source_slot]
    chosen_left = flat_left[compact_codes]
    landed = jnp.einsum(
        "pab,pbc->pac", chosen_left, compact_blocks, precision=lax.Precision.HIGHEST
    )
    target_place = compact_codes % sector_local
    onehot_place = target_place[:, None] == jnp.arange(sector_local, dtype=jnp.int32)[None, :]
    return jnp.einsum(
        "pk,pac->kac", onehot_place.astype(jnp.float32), landed, precision=lax.Precision.HIGHEST
    )


def per_device(psi_blocks, left_env, right_env, left_sizes, right_sizes, dest_sector):
    term_local = left_env.shape[0]
    sector_local = left_env.shape[1]
    block_size = left_env.shape[2]
    peers = lax.axis_size("sec")
    capacity = (term_local * sector_local + peers - 1) // peers
    slot_count = peers * capacity
    valid_mask = sector_mask(left_sizes, right_sizes, block_size)
    masked_psi = psi_blocks * valid_mask
    carried = jnp.einsum("sab,tsbc->tsac", masked_psi, right_env, precision=lax.Precision.HIGHEST)
    flat_left = left_env.reshape(term_local * sector_local, block_size, block_size)
    term_ids = jnp.repeat(jnp.arange(term_local, dtype=jnp.int32), sector_local)
    buffer, meta_codes = pack_blocks(
        carried.reshape(term_local * sector_local, block_size, block_size),
        dest_sector.reshape(term_local * sector_local),
        term_ids,
        sector_local,
        capacity,
        slot_count,
    )
    received, codes_in = (
        lax.all_to_all(buffer, "sec", split_axis=0, concat_axis=0, tiled=True),
        lax.all_to_all(meta_codes, "sec", split_axis=0, concat_axis=0, tiled=True),
    )
    partial_sum = apply_left(received, codes_in, flat_left, sector_local, term_local * sector_local)
    total = lax.psum(partial_sum, "term")
    return total * valid_mask


def solution(mesh):
    in_specs = (
        P("sec", None, None),
        P("term", "sec", None, None),
        P("term", "sec", None, None),
        P("sec"),
        P("sec"),
        P("term", "sec"),
    )
    out_specs = P("sec", None, None)
    return jax.shard_map(
        per_device, mesh=mesh, in_specs=in_specs, out_specs=out_specs, check_vma=False
    )
```

profile of v0, /device:TPU:1, one launch (start us, length us, event | category | flops | bytes accessed | tf_op | source)
XLA Modules:
  0.0 343.7 jit_solution(1306117525942289401)
XLA Ops:
  6.5 0.8 reshape.239
  7.3 0.1 mul.13
  7.4 0.2 convert_reduce_fusion
  7.6 0.1 fusion.9
  7.7 0.1 select_reduce_fusion.1
  7.8 0.7 gather_fusion
  8.5 0.7 copy.34
  9.2 11.9 %all-to-all-start = ((s32[32,1,1]{2,1,0:T(1,128)}), s32[32,1,1]{2,1,0:T(1,128)S(1)}, u32[]{:S(2)}, u32[]{:S(2)}) async-start(s32[32,1,1]{2,1,0:T(1,128)} %copy.34), calls=%async_computation | async-start | bytes 32768 | tf_op jit(solution)/shard_map/all_to_all | solution.py:75
  21.1 0.0 copy-start
  21.1 0.9 iota_compare_fusion.4
  22.0 0.9 iota_compare_fusion
  22.9 3.0 fusion.7
  25.9 0.0 copy-done
  25.9 4.3 %fusion.4 = f32[2,8,256,256]{3,2,0,1:T(8,128)S(1)} fusion(f32[2,8,256,256]{3,2,1,0:T(8,128)S(1)} %copy-done, f32[8,256,256,1]{2,0,1,3:T(8,128)S(1)} %fusion.7), kind=kOutput, calls=%fused_computation.12 | convolution fusion | flops 3221225472 | bytes 10485760 | tf_op jit(solution)/shard_map/sab,tsbc->tsac/dot_general | solution.py:62
  30.2 2.3 copy.39
  32.5 6.5 %gather_fusion.3 = f32[32,256,256]{2,1,0:T(8,128)} fusion(f32[16,256,256]{2,1,0:T(8,128)} %bitcast.26, s32[1024]{0:T(1024)S(1)} %pad_clamp_fusion.2), kind=kCustom, calls=%fused_computation.3 | custom fusion | bytes 16777344 | tf_op jit(solution)/shard_map/gather | solution.py:26
  38.9 7.8 %broadcast_select_fusion = f32[32,256,256]{2,1,0:T(8,128)} fusion(f32[32,256,256]{2,1,0:T(8,128)} %gather_fusion.3, pred[32]{0:T(512)(128)(4,1)S(1)} %fusion.9), kind=kLoop, calls=%fused_computation.9 | loop fusion | flops 2097152 | bytes 16777248 | tf_op jit(solution)/shard_map/jit(_where)/select_n | solution.py:26
  46.7 0.0 all-to-all-done
  46.8 9.4 %all-to-all-start.1 = ((f32[32,256,256]{2,1,0:T(8,128)}), f32[32,256,256]{2,1,0:T(8,128)}, u32[]{:S(2)}, u32[]{:S(2)}) async-start(f32[32,256,256]{2,1,0:T(8,128)} %broadcast_select_fusion), calls=%async_computation.1 | async-start | bytes 16777216 | tf_op jit(solution)/shard_map/all_to_all | solution.py:74
  56.1 0.2 all-reduce.2.cloned.1.call-start
  56.4 0.1 reduce-window.8
  56.4 0.7 reduce
  57.1 0.1 add_reduce_fusion
  57.2 0.1 select_reduce_fusion
  57.4 0.7 gather_fusion.1
  58.0 4.9 %gather_fusion.2 = f32[16,256,256]{2,1,0:T(8,128)} fusion(f32[16,256,256]{2,1,0:T(8,128)} %bitcast.27, s32[1024]{0:T(1024)S(1)} %pad_clamp_fusion), kind=kCustom, calls=%fused_computation.2 | custom fusion | bytes 8388672 | tf_op jit(solution)/shard_map/gather | solution.py:42
  63.0 176.4 %all-to-all-done.1 = f32[32,256,256]{2,1,0:T(8,128)} async-done(((f32[32,256,256]{2,1,0:T(8,128)}), f32[32,256,256]{2,1,0:T(8,128)}, u32[]{:S(2)}, u32[]{:S(2)}) %all-to-all-start.1) | async-done | bytes 8388640 | tf_op jit(solution)/shard_map/all_to_all | solution.py:74
  239.4 6.2 %gather_fusion.4 = f32[16,256,256]{2,1,0:T(8,128)} fusion(f32[32,256,256]{2,1,0:T(8,128)} %all-to-all-done.1, s32[1024]{0:T(1024)S(1)} %pad_clamp_fusion.1), kind=kCustom, calls=%fused_computation.4 | custom fusion | bytes 8388672 | tf_op jit(solution)/shard_map/gather | solution.py:40
  245.6 8.2 %fusion.20 = f32[16,256,256]{2,1,0:T(8,128)S(1)} fusion(f32[16,256,256]{2,1,0:T(8,128)} %gather_fusion.2, f32[16,256,256]{2,1,0:T(8,128)} %gather_fusion.4), kind=kOutput, calls=%fused_computation.53 | convolution fusion | flops 3221225472 | bytes 12582912 | tf_op jit(solution)/shard_map/pab,pbc->pac/dot_general | solution.py:43
  253.8 5.3 %fusion = f32[8,256,256]{2,0,1:T(8,128)} fusion(f32[16,256,256]{2,1,0:T(8,128)S(1)} %fusion.20, s32[16]{0:T(128)S(1)} %and_select_fusion.2), kind=kOutput, calls=%fused_computation.5 | convolution fusion | flops 100663424 | bytes 6291520 | tf_op jit(solution)/shard_map/pk,pac->kac/dot_general | solution.py:48
  259.1 0.0 all-reduce.2.cloned.1.call-update
  259.2 74.0 %all-reduce.2.cloned.1.call-done = f32[8,256,256]{2,0,1:T(8,128)} async-done(((f32[8,256,256]{2,0,1:T(8,128)}), f32[8,256,256]{2,0,1:T(8,128)}) %all-reduce.2.cloned.1.call-update) | async-done | bytes 2097168 | tf_op jit(solution)/shard_map/psum | solution.py:78
  333.1 1.8 and_select_fusion
  334.9 2.0 copy.41
  (13 shorter events, 0.1 us)
Async XLA Ops:
  9.2 37.6 %all-to-all-start = ((s32[32,1,1]{2,1,0:T(1,128)}), s32[32,1,1]{2,1,0:T(1,128)S(1)}, u32[]{:S(2)}, u32[]{:S(2)}) async-start(s32[32,1,1]{2,1,0:T(1,128)} %copy.34), calls=%async_computation | async-start | bytes 32768 | tf_op jit(solution)/shard_map/all_to_all | solution.py:75
  21.1 4.8 %copy-start = (f32[2,8,256,256]{3,2,1,0:T(8,128)S(1)}, f32[2,8,256,256]{3,2,1,0:T(8,128)}, u32[]{:S(2)}) copy-start(f32[2,8,256,256]{3,2,1,0:T(8,128)} %param.8) | copy-start | bytes 12582916
  46.8 192.7 %all-to-all-start.1 = ((f32[32,256,256]{2,1,0:T(8,128)}), f32[32,256,256]{2,1,0:T(8,128)}, u32[]{:S(2)}, u32[]{:S(2)}) async-start(f32[32,256,256]{2,1,0:T(8,128)} %broadcast_select_fusion), calls=%async_computation.1 | async-start | bytes 16777216 | tf_op jit(solution)/shard_map/all_to_all | solution.py:74
  56.1 277.0 %all-reduce.2.cloned.1.call-start = ((), (), s32[]{:S(2)}) async-start(), calls=%async_computation.2 | async-start | bytes 4194304 | tf_op jit(solution)/shard_map/psum | solution.py:78
Sparse Core Ops, SparseCore 0:
  259.3 73.7 all-reduce.1
where the time goes:
time: 345 us; the launch traced here: 344 us
  waiting for transfers between devices  250 us (72%)
  local copies, waits for them, and re-layouts  24.7 us (7%)
  starting transfers between devices  21.4 us (6%)
  matrix products  17.8 us (5%)
  other arithmetic  15.8 us (5%)
  between operations  13.5 us (4%)
    all_to_all x1, waiting for transfers between devices, per_device(): lax.all_to_all(buffer, 'sec', split_axis=0, concat_axis=0, tiled=True)  176 us
    psum x1, waiting for transfers between devices, per_device(): total = lax.psum(partial_sum, 'term')  74 us
    all_to_all x1, starting transfers between devices, per_device(): lax.all_to_all(meta_codes, 'sec', split_axis=0, concat_axis=0, tiled=True)  11.9 us
    all_to_all x1, starting transfers between devices, per_device(): lax.all_to_all(buffer, 'sec', split_axis=0, concat_axis=0, tiled=True)  9.35 us
    dot_general x1, matrix products, apply_left(): jnp.einsum('pab,pbc->pac', chosen_left, compact_blocks, precision=lax.Pre...  8.25 us
    select_n x1, other arithmetic, pack_blocks(): buffer = jnp.where(filled[:, None, None], outgoing[slot_source], 0.0)  7.81 us
  transfers between devices with their start and end apart: 3, of which 2 were waited for; matrix products, arithmetic and copies ran while one was open for 9% of the time, Pallas kernels for 0%

commit v1 on v0

--- a/solution.py
+++ b/solution.py
@@ -1,7 +1,22 @@
+import functools
 import jax
 import jax.numpy as jnp
 from jax import lax
+from jax.experimental import pallas as pl
+from jax.experimental.pallas import tpu as pltpu
 from jax.sharding import PartitionSpec as P
+
+BLK = 256
+LANES = 128
+ROWS = 8
+PEERS = 32
+MEMBERS = 8
+HELD = 8
+PAIRS = 16
+ROWS_OUT = 64
+ROWS_IN = 64
+PIECE = 32
+VMEM_BYTES = 40 * 1024 * 1024
 
 
 def sector_mask(left_sizes, right_sizes, block_size):
@@ -50,7 +65,7 @@
     )
 
 
-def per_device(psi_blocks, left_env, right_env, left_sizes, right_sizes, dest_sector):
+def dense_program(psi_blocks, left_env, right_env, left_sizes, right_sizes, dest_sector):
     term_local = left_env.shape[0]
     sector_local = left_env.shape[1]
     block_size = left_env.shape[2]
@@ -79,6 +94,426 @@
     return total * valid_mask
 
 
+def split3(a):
+    hi = a.astype(jnp.bfloat16)
+    lo = (a - hi.astype(jnp.float32)).astype(jnp.bfloat16)
+    return hi, lo
+
+
+def dot3(a, b, transposed=False):
+    dims = (((1,), (1 if transposed else 0,)), ((), ()))
+    a_hi, a_lo = split3(a)
+    b_hi, b_lo = split3(b)
+    mul = functools.partial(
+        lax.dot_general, dimension_numbers=dims, preferred_element_type=jnp.float32
+    )
+    return mul(a_hi, b_hi) + (mul(a_hi, b_lo) + mul(a_lo, b_hi))
+
+
+T_START, T_ROWS, T_NX, T_NY, T_LEFT, T_RIGHT, T_BASE = 0, 1, 2, 3, 4, 5, 6
+T_WIDTH = 10
+
+
+def tile_rows(stream, rows):
+    return (stream % 4) * (ROWS * rows) + stream // 4
+
+
+def send_kernel(tbl, psi_ref, right_ref, buf_ref, x_ref, y_ref):
+    row = lax.broadcasted_iota(jnp.int32, (BLK, BLK), 0)
+    col = lax.broadcasted_iota(jnp.int32, (BLK, BLK), 1)
+
+    def emit(src_ref, strip, first, rows):
+        room = jnp.maximum(jnp.minimum(rows, 4 * ROWS_OUT - first), 0)
+
+        def one(a, carry):
+            tile = src_ref[pl.ds(pl.multiple_of(a * ROWS, ROWS), ROWS), pl.ds(strip * LANES, LANES)]
+            buf_ref[pl.ds(tile_rows(first + a, ROWS_OUT), ROWS, stride=ROWS_OUT), :] = tile
+            return carry
+
+        lax.fori_loop(0, room, one, 0)
+
+    def pair(p, carry):
+        at = p * T_WIDTH
+        start, rows = tbl[at + T_START], tbl[at + T_ROWS]
+        nx, ny = tbl[at + T_NX], tbl[at + T_NY]
+        kept = (row < tbl[at + T_LEFT]) & (col < tbl[at + T_RIGHT])
+        psi = jnp.where(kept, psi_ref[p % HELD], 0.0)
+        factors = (nx > 0) & (ny > 0)
+
+        @pl.when(factors)
+        def _():
+            x_ref[...] = psi.T
+            y_ref[...] = right_ref[p]
+
+        @pl.when(nx == 0)
+        def _():
+            y_ref[...] = dot3(psi, right_ref[p])
+
+        @pl.when(ny == 0)
+        def _():
+            x_ref[...] = dot3(psi, right_ref[p]).T
+
+        for strip in range(2):
+            @pl.when(strip < nx)
+            def _():
+                emit(x_ref, strip, start + strip * rows, rows)
+
+        for strip in range(2):
+            @pl.when(strip < ny)
+            def _():
+                emit(y_ref, strip, start + (nx + strip) * rows, rows)
+
+        return carry
+
+    lax.fori_loop(0, PAIRS, pair, 0)
+
+
+def relay_kernel(idx, count, in_ref, out_ref):
+    def slot(peer, carry):
+        def some(i, inner):
+            at = peer * ROWS_IN + i * ROWS
+            for k in range(ROWS):
+                out_ref[pl.ds(at + k, 1), :] = in_ref[pl.ds(idx[at + k], 1), :]
+            return inner
+
+        lax.fori_loop(0, (count[peer] + ROWS - 1) // ROWS, some, 0)
+        return carry
+
+    lax.fori_loop(0, PEERS, slot, 0)
+
+
+def land_kernel(tbl, out_tbl, buf_ref, left_ref, keep_ref, send_ref, x_ref, y_ref, z_ref, acc_ref):
+    acc_ref[...] = jnp.zeros_like(acc_ref)
+
+    def take(dst_ref, strip, at, before, rows):
+        start = tbl[at + T_START]
+
+        def one(a, carry):
+            q = before + a
+            kind = (start + q) % 4
+            rank = jnp.minimum(tbl[at + T_BASE + kind] + q // 4, ROWS_IN - 1)
+            tile = buf_ref[pl.ds(kind * (ROWS * ROWS_IN) + rank, ROWS, stride=ROWS_IN), :]
+            dst_ref[pl.ds(pl.multiple_of(a * ROWS, ROWS), ROWS), pl.ds(strip * LANES, LANES)] = tile
+            return carry
+
+        lax.fori_loop(0, rows, one, 0)
+
+    def pair(u, carry):
+        at = u * T_WIDTH
+        rows, nx, ny = tbl[at + T_ROWS], tbl[at + T_NX], tbl[at + T_NY]
+
+        @pl.when(nx > 0)
+        def _():
+            x_ref[...] = jnp.zeros_like(x_ref)
+            for strip in range(2):
+                @pl.when(strip < nx)
+                def _():
+                    take(x_ref, strip, at, strip * rows, rows)
+            z_ref[...] = dot3(left_ref[u], x_ref[...], transposed=True)
+
+        @pl.when(nx == 0)
+        def _():
+            z_ref[...] = left_ref[u]
+
+        @pl.when(ny > 0)
+        def _():
+            y_ref[...] = jnp.zeros_like(y_ref)
+            for strip in range(2):
+                @pl.when(strip < ny)
+                def _():
+                    take(y_ref, strip, at, (nx + strip) * rows, rows)
+            acc_ref[u % HELD] += dot3(z_ref[...], y_ref[...])
+
+        @pl.when(ny == 0)
+        def _():
+            acc_ref[u % HELD] += z_ref[...]
+
+        return carry
+
+    lax.fori_loop(0, PAIRS, pair, 0)
+
+    half = 4 * PIECE
+    core, chip = out_tbl[O_CORE], out_tbl[O_CHIP]
+
+    def sector(d, carry):
+        first, rows, strips = out_tbl[3 * d], out_tbl[3 * d + 1], out_tbl[3 * d + 2]
+        for strip in range(2):
+            @pl.when(strip < strips)
+            def _():
+                begin = first + strip * rows
+                room = jnp.maximum(jnp.minimum(rows, 2 * half - 1 - begin), 0)
+
+                def one(a, inner):
+                    s = begin + a
+                    place = ((s % half) // PIECE ^ chip) * PIECE + s % PIECE
+                    tile = acc_ref[
+                        d,
+                        pl.ds(pl.multiple_of(a * ROWS, ROWS), ROWS),
+                        pl.ds(strip * LANES, LANES),
+                    ]
+
+                    @pl.when(s // half == core)
+                    def _():
+                        keep_ref[place] = tile
+
+                    @pl.when(s // half != core)
+                    def _():
+                        send_ref[place] = tile
+
+                    return inner
+
+                lax.fori_loop(0, room, one, 0)
+        return carry
+
+    lax.fori_loop(0, HELD, sector, 0)
+    flag = jnp.full((ROWS, LANES), out_tbl[O_FLAG], jnp.int32).astype(jnp.float32)
+    last = (3 ^ chip) * PIECE + PIECE - 1
+
+    @pl.when(core == 1)
+    def _():
+        keep_ref[last] = flag
+
+    @pl.when(core != 1)
+    def _():
+        send_ref[last] = flag
+
+
+def spread_kernel(out_tbl, sizes, own_ref, other_ref, out_ref):
+    out_ref[...] = jnp.zeros_like(out_ref)
+    half = 4 * PIECE
+    core, chip = out_tbl[O_CORE], out_tbl[O_CHIP]
+    row = lax.broadcasted_iota(jnp.int32, (ROWS, LANES), 0)
+    col = lax.broadcasted_iota(jnp.int32, (ROWS, LANES), 1)
+
+    def sector(d, carry):
+        first, rows, strips = out_tbl[3 * d], out_tbl[3 * d + 1], out_tbl[3 * d + 2]
+        height, width = sizes[d], sizes[HELD + d]
+        for strip in range(2):
+            @pl.when(strip < strips)
+            def _():
+                begin = first + strip * rows
+                col_ok = col + strip * LANES < width
+
+                def one(a, inner):
+                    s = begin + a
+                    place = ((s % half) // PIECE ^ chip) * PIECE + s % PIECE
+                    kept = col_ok & (row + a * ROWS < height)
+                    at = (
+                        d,
+                        pl.ds(pl.multiple_of(a * ROWS, ROWS), ROWS),
+                        pl.ds(strip * LANES, LANES),
+                    )
+
+                    @pl.when(s // half == core)
+                    def _():
+                        out_ref[at] = jnp.where(kept, own_ref[place], 0.0)
+
+                    @pl.when(s // half != core)
+                    def _():
+                        out_ref[at] = jnp.where(kept, other_ref[place], 0.0)
+
+                    return inner
+
+                lax.fori_loop(0, rows, one, 0)
+        return carry
+
+    lax.fori_loop(0, HELD, sector, 0)
+
+
+O_CORE, O_CHIP, O_FLAG = 3 * HELD, 3 * HELD + 1, 3 * HELD + 2
+
+SMEM = pl.BlockSpec(memory_space=pltpu.SMEM)
+VMEM = pl.BlockSpec(memory_space=pltpu.VMEM)
+PARAMS = pltpu.CompilerParams(vmem_limit_bytes=VMEM_BYTES)
+
+
+def floats(*shape):
+    return jax.ShapeDtypeStruct(shape, jnp.float32)
+
+
+def scratch(*shape):
+    return pltpu.VMEM(shape, jnp.float32)
+
+
+def send_call(tbl, psi, right):
+    return pl.pallas_call(
+        send_kernel,
+        out_shape=floats(PEERS * ROWS_OUT, LANES),
+        in_specs=[SMEM, VMEM, VMEM],
+        out_specs=VMEM,
+        scratch_shapes=[scratch(BLK, BLK), scratch(BLK, BLK)],
+        compiler_params=PARAMS,
+    )(tbl, psi, right)
+
+
+def relay_call(idx, count, received):
+    return pl.pallas_call(
+        relay_kernel,
+        out_shape=floats(PEERS * ROWS_IN, LANES),
+        in_specs=[SMEM, SMEM, VMEM],
+        out_specs=VMEM,
+        compiler_params=PARAMS,
+    )(idx, count, received)
+
+
+def land_call(tbl, out_tbl, received, left):
+    return pl.pallas_call(
+        land_kernel,
+        out_shape=[floats(4 * PIECE, ROWS, LANES)] * 2,
+        in_specs=[SMEM, SMEM, VMEM, VMEM],
+        out_specs=[VMEM, VMEM],
+        scratch_shapes=[scratch(BLK, BLK)] * 3 + [scratch(HELD, BLK, BLK)],
+        compiler_params=PARAMS,
+    )(tbl, out_tbl, received, left)
+
+
+def spread_call(out_tbl, sizes, own, other):
+    return pl.pallas_call(
+        spread_kernel,
+        out_shape=floats(HELD, BLK, BLK),
+        in_specs=[SMEM, SMEM, VMEM, VMEM],
+        out_specs=VMEM,
+        compiler_params=PARAMS,
+    )(out_tbl, sizes, own, other)
+
+
+def up(value, unit):
+    return (value + (unit - 1)) // unit
+
+
+def before(values, axis):
+    n = values.shape[axis]
+    moved = jnp.moveaxis(values, axis, -1)
+    lower = jnp.arange(n)[:, None] > jnp.arange(n)[None, :]
+    total = jnp.sum(jnp.where(lower, moved[..., None, :], 0), axis=-1)
+    return jnp.moveaxis(total, -1, axis)
+
+
+def per_device(psi_blocks, left_env, right_env, left_sizes, right_sizes, dest_sector):
+    me = lax.axis_index("sec")
+    member = lax.axis_index("term")
+    core, chip = member % 2, member // 2
+    mine = jnp.concatenate([left_sizes, right_sizes, dest_sector.reshape(PAIRS)])
+    facts = lax.all_to_all(
+        jnp.broadcast_to(mine[None, :], (PEERS, 4 * HELD)), "sec", 0, 0, tiled=True
+    )
+    size_l, size_r, dest = facts[:, :HELD], facts[:, HELD : 2 * HELD], facts[:, 2 * HELD :]
+
+    ls = jnp.concatenate([size_l, size_l], axis=1)
+    rs = jnp.concatenate([size_r, size_r], axis=1)
+    to_dev, to_place = dest // HELD, dest % HELD
+    hit_dev = to_dev[:, :, None] == jnp.arange(PEERS)[None, None, :]
+    hit_place = to_place[:, :, None] == jnp.arange(HELD)[None, None, :]
+    rd = jnp.sum(
+        jnp.where(hit_dev[:, :, :, None] & hit_place[:, :, None, :], size_r[None, None], 0),
+        axis=(2, 3),
+    )
+    nl, nr = up(ls, LANES), up(rd, LANES)
+    cost_c = up(ls, ROWS) * nr
+    cost_ct = up(rd, ROWS) * nl
+    cost_f = up(rs, ROWS) * (nl + nr)
+    is_f = (cost_f < cost_c) & (cost_f < cost_ct)
+    is_ct = ~is_f & (cost_ct < cost_c)
+    rows = up(jnp.where(is_f, rs, jnp.where(is_ct, rd, ls)), ROWS)
+    nx = jnp.where(is_f | is_ct, nl, 0)
+    ny = jnp.where(is_ct, 0, nr)
+    tiles = rows * (nx + ny)
+    start = before(tiles, 1)
+    total = jnp.sum(tiles, axis=1)
+
+    kinds = jnp.arange(4)[:, None, None]
+    lag = (kinds - start) % 4
+    share = (tiles + 3 - lag) // 4
+    first_row = (start + lag) // 4
+    onto = jnp.sum(jnp.where(hit_dev[None], share[..., None], 0), axis=2)
+    base = before(onto, 1)
+    filled = jnp.sum(onto, axis=1)
+
+    out_rows, out_strips = up(size_l, ROWS), up(size_r, LANES)
+    out_tiles = out_rows * out_strips
+    out_first = before(out_tiles, 1)
+    spilled = (
+        jnp.any(total > 4 * ROWS_OUT)
+        | jnp.any(filled > ROWS_IN)
+        | jnp.any(jnp.sum(out_tiles, axis=1) > MEMBERS * PIECE - 1)
+    )
+
+    def own(values, axis=0):
+        return lax.dynamic_index_in_dim(values, me, axis, keepdims=False)
+
+    zero = jnp.zeros((PAIRS,), jnp.int32)
+    send_tbl = jnp.stack(
+        [own(start), own(rows), own(nx), own(ny), own(ls), own(rs)] + [zero] * 4, axis=1
+    ).reshape(-1)
+
+    kind = me // ROWS
+    onto_k = lax.dynamic_index_in_dim(onto, kind, 0, keepdims=False)
+    base_k = lax.dynamic_index_in_dim(base, kind, 0, keepdims=False)
+    first_k = lax.dynamic_index_in_dim(first_row, kind, 0, keepdims=False)
+    filled_k = lax.dynamic_index_in_dim(filled, kind, 0, keepdims=False)
+    first_to = jnp.sum(jnp.where(hit_dev, first_k[:, :, None], 0), axis=1)
+    rank = jnp.arange(ROWS_IN)[None, None, :]
+    here = (rank >= base_k[:, :, None]) & (rank < (base_k + onto_k)[:, :, None])
+    origin = jnp.arange(PEERS)[:, None] * ROWS_OUT + first_to - base_k
+    relay_idx = jnp.sum(jnp.where(here, origin[:, :, None] + rank, 0), axis=0)
+    relay_idx = jnp.clip(relay_idx, 0, PEERS * ROWS_OUT - 1).reshape(-1)
+    relay_count = jnp.minimum(filled_k, ROWS_IN)
+
+    unit = jnp.arange(PAIRS)[:, None, None]
+    reach = (dest[None] == me * HELD + unit % HELD) & (
+        (jnp.arange(PAIRS) // HELD)[None, None, :] == unit // HELD
+    )
+
+    def reached(values):
+        return jnp.sum(jnp.where(reach, values[None], 0), axis=(1, 2))
+
+    base_me = lax.dynamic_index_in_dim(base, me, 2, keepdims=False)
+    land_tbl = jnp.stack(
+        [reached(start), reached(rows), reached(nx), reached(ny), reached(ls), reached(rs)]
+        + [reached(jnp.broadcast_to(base_me[g][:, None], (PEERS, PAIRS))) for g in range(4)],
+        axis=1,
+    ).reshape(-1)
+
+    out_tbl = jnp.concatenate(
+        [
+            jnp.stack([own(out_first), own(out_rows), own(out_strips)], axis=1).reshape(-1),
+            jnp.stack([core, chip, spilled.astype(jnp.int32)]).astype(jnp.int32),
+        ]
+    )
+    sizes = jnp.concatenate([left_sizes, right_sizes])
+
+    sent = send_call(send_tbl, psi_blocks, right_env.reshape(PAIRS, BLK, BLK))
+    hop = lax.all_to_all(sent.reshape(PEERS, ROWS_OUT, LANES), "sec", 0, 0, tiled=True)
+    passed = relay_call(relay_idx, relay_count, hop.reshape(PEERS * ROWS_OUT, LANES))
+    hop = lax.all_to_all(passed.reshape(PEERS, ROWS_IN, LANES), "sec", 0, 0, tiled=True)
+    keep, give = land_call(
+        land_tbl,
+        out_tbl,
+        hop.reshape(PEERS * ROWS_IN, LANES),
+        left_env.reshape(PAIRS, BLK, BLK),
+    )
+
+    def swap(values, bits):
+        return lax.ppermute(values, "term", [(i, i ^ bits) for i in range(MEMBERS)])
+
+    half = (keep + swap(give, 1)).reshape(4, PIECE, ROWS, LANES)
+    piece = half[0] + swap(half[1], 2) + swap(half[2], 4) + swap(half[3], 6)
+    whole = jnp.concatenate([piece, swap(piece, 2), swap(piece, 4), swap(piece, 6)])
+    other = swap(whole, 1)
+
+    last = (3 ^ chip) * PIECE + PIECE - 1
+    flag_own = lax.dynamic_slice(whole, (last, 0, 0), (1, 1, 1))
+    flag_other = lax.dynamic_slice(other, (last, 0, 0), (1, 1, 1))
+    flag = jnp.where(core == 1, flag_own, flag_other).reshape(())
+    return lax.cond(
+        flag > 0.5,
+        lambda: dense_program(
+            psi_blocks, left_env, right_env, left_sizes, right_sizes, dest_sector
+        ),
+        lambda: spread_call(out_tbl, sizes, whole, other),
+    )
+
+
 def solution(mesh):
     in_specs = (
         P("sec", None, None),

time: 345 us -> 173 us (0.50)
  waiting for transfers between devices: 250 us -> 56.7 us
  Pallas kernels: 0 us -> 26.5 us
  starting transfers between devices: 21.4 us -> 42 us
  local copies, waits for them, and re-layouts: 24.7 us -> 5.79 us
  matrix products: 17.8 us -> 0 us
  other arithmetic: 15.8 us -> 22.5 us
    all_to_all x2 -> x3, waiting for transfers between devices: 176 us -> 43.4 us  [the longest x1 20 us: per_device(): lax.all_to_all(sent.reshape(PEERS, ROWS_OUT, LANES), 'sec', 0, 0, tiled=T...]
    psum x1 -> x0, waiting for transfers between devices: 74 us -> none  [per_device(): total = lax.psum(partial_sum, 'term')]
    pallas_call x0 -> x4, Pallas kernels: none -> 26.5 us  [the longest x1 11.2 us: land_call(): pl.pallas_call(land_kernel, out_shape=[floats(4 * PIECE, ROWS, LANES)] *...]
    gather x5 -> x0, local copies, waits for them, and re-layouts: 18.9 us -> none  [the longest x1 6.48 us: pack_blocks(): buffer = jnp.where(filled[:, None, None], outgoing[slot_source], 0.0)]
    ppermute x0 -> x8, starting transfers between devices: none -> 18.3 us  [swap(): return lax.ppermute(values, 'term', [(i, i ^ bits) for i in range(MEMBERS)])]
    dot_general x3 -> x0, matrix products: 17.8 us -> none  [the longest x1 8.25 us: apply_left(): jnp.einsum('pab,pbc->pac', chosen_left, compact_blocks, precision=lax.Pre...]
    reduce_sum x3 -> x10, other arithmetic: 0.39 us -> 17.3 us  [the longest x1 10.1 us: per_device(): jnp.sum(jnp.where(hit_dev[:, :, :, None] & hit_place[:, :, None, :], size...]
    ppermute x0 -> x8, waiting for transfers between devices: none -> 13.3 us  [swap(): return lax.ppermute(values, 'term', [(i, i ^ bits) for i in range(MEMBERS)])]
  transfers between devices with their start and end apart: 3 -> 11, of which waited for: 2 -> 10; matrix products, arithmetic and copies ran while one was open for 9% -> 6% of each run, Pallas kernels for 0% -> 0%
where the time goes in v1:
time: 173 us; the launch traced here: 170 us
  waiting for transfers between devices  56.7 us (33%)
  starting transfers between devices  42 us (24%)
  Pallas kernels  26.5 us (15%)
  other arithmetic  22.5 us (13%)
  between operations  16.3 us (9%)
  local copies, waits for them, and re-layouts  5.79 us (3%)
    all_to_all x1, waiting for transfers between devices, per_device(): lax.all_to_all(sent.reshape(PEERS, ROWS_OUT, LANES), 'sec', 0, 0, tiled=T...  20 us
    ppermute x8, starting transfers between devices, swap(): return lax.ppermute(values, 'term', [(i, i ^ bits) for i in range(MEMBERS)])  18.3 us
    all_to_all x1, waiting for transfers between devices, per_device(): lax.all_to_all(passed.reshape(PEERS, ROWS_IN, LANES), 'sec', 0, 0, tiled=...  14.8 us
    ppermute x8, waiting for transfers between devices, swap(): return lax.ppermute(values, 'term', [(i, i ^ bits) for i in range(MEMBERS)])  13.3 us
    all_to_all x1, starting transfers between devices, per_device(): lax.all_to_all(jnp.broadcast_to(mine[None, :], (PEERS, 4 * HELD)), 'sec',...  11.9 us
    pallas_call x1, Pallas kernels, land_call(): pl.pallas_call(land_kernel, out_shape=[floats(4 * PIECE, ROWS, LANES)] *...  11.2 us
    reduce_sum x1, other arithmetic, per_device(): jnp.sum(jnp.where(hit_dev[:, :, :, None] & hit_place[:, :, None, :], size...  10.1 us
    pallas_call x1, Pallas kernels, send_call(): pl.pallas_call(send_kernel, out_shape=floats(PEERS * ROWS_OUT, LANES), in...  9.98 us
  transfers between devices with their start and end apart: 11, of which 10 were waited for; matrix products, arithmetic and copies ran while one was open for 6% of the time, Pallas kernels for 0%

profile of v1, /device:TPU:1, one launch (start us, length us, event | category | flops | bytes accessed | tf_op | source)
XLA Modules:
  0.0 170.1 jit_solution(6723584742360637502)
XLA Ops:
  6.5 0.8 reshape.971
  7.3 0.7 pad_add_fusion.3
  8.0 0.6 broadcast_in_dim.277
  8.7 11.9 %all-to-all-start.2 = ((s32[32,1,32]{2,1,0:T(1,128)}), s32[32,1,32]{2,1,0:T(1,128)S(1)}, u32[]{:S(2)}, u32[]{:S(2)}) async-start(s32[32,1,32]{2,1,0:T(1,128)} %broadcast_in_dim.277), calls=%async_computation.2 | async-start | bytes 32768 | tf_op jit(solution)/shard_map/all_to_all | solution.py:397
  20.6 8.5 %all-to-all-done.2 = s32[32,1,32]{2,1,0:T(1,128)S(1)} async-done(((s32[32,1,32]{2,1,0:T(1,128)}), s32[32,1,32]{2,1,0:T(1,128)S(1)}, u32[]{:S(2)}, u32[]{:S(2)}) %all-to-all-start.2) | async-done | bytes 4128 | tf_op jit(solution)/shard_map/all_to_all | solution.py:397
  29.2 0.2 fusion.73
  29.4 0.1 iota_compare_fusion.9
  29.5 0.1 iota_compare_fusion.8
  29.7 10.1 %select_reduce_fusion.3 = s32[32,16]{1,0:T(8,128)S(1)} fusion(s32[32,8]{0,1:T(8,128)S(1)} %copy.122, pred[32,16,8]{2,1,0:T(8,128)(4,1)S(1)} %iota_compare_fusion.8, pred[32,16,32]{2,1,0:T(8,128)(4,1)S(1)} %iota_compare_fusion.9), kind=kLoop, calls=%fused_computation.54 | loop fusion | flops 392704 | bytes 23552 | tf_op jit(solution)/shard_map/reduce_sum | solution.py:407
  39.9 0.1 compare_and_fusion.1
  40.0 0.2 fusion.75
  40.4 0.1 select_reduce_fusion.18
  41.3 10.0 %shard_map.66 = f32[2048,128]{1,0:T(8,128)} custom-call(s32[160]{0:T(256)S(1)} %reshape.974.tbl, f32[8,256,256]{2,1,0:T(8,128)} %psi_ref.1, f32[16,256,256]{2,1,0:T(8,128)} %bitcast.88), custom_call_target="tpu_custom_call" | custom-call | tf_op jit(solution)/shard_map/pallas_call | solution.py:339
  51.2 4.2 %all-to-all-start.3 = ((f32[32,64,128]{2,1,0:T(8,128)}), f32[32,64,128]{2,1,0:T(8,128)S(1)}, u32[]{:S(2)}, u32[]{:S(2)}) async-start(f32[32,64,128]{2,1,0:T(8,128)} %bitcast.48), calls=%async_computation.3 | async-start | bytes 2097152 | tf_op jit(solution)/shard_map/all_to_all | solution.py:486
  55.6 0.2 select_reduce_fusion.7
  55.9 0.4 select_reduce_fusion.4
  56.5 2.2 %select_reduce_fusion.2 = s32[4,32,32]{2,1,0:T(8,128)S(1)} fusion(s32[4,32,32]{2,1,0:T(8,128)S(1)} %copy.130, pred[32,32]{1,0:T(8,128)(4,1)S(1)} %iota_compare_fusion.10), kind=kLoop, calls=%fused_computation.53 | loop fusion | flops 258048 | bytes 33792 | tf_op jit(solution)/shard_map/reduce_sum | solution.py:388
  58.9 0.6 select_reduce_fusion.6
  59.6 20.0 %all-to-all-done.3 = f32[32,64,128]{2,1,0:T(8,128)S(1)} async-done(((f32[32,64,128]{2,1,0:T(8,128)}), f32[32,64,128]{2,1,0:T(8,128)S(1)}, u32[]{:S(2)}, u32[]{:S(2)}) %all-to-all-start.3) | async-done | bytes 1048608 | tf_op jit(solution)/shard_map/all_to_all | solution.py:486
  79.7 3.2 %shard_map.67 = f32[2048,128]{1,0:T(8,128)} custom-call(s32[2048]{0:T(1024)S(1)} %min.18.idx, s32[32]{0:T(128)S(1)} %fusion.61.count, f32[2048,128]{1,0:T(8,128)S(1)} %bitcast.85), custom_call_target="tpu_custom_call" | custom-call | tf_op jit(solution)/shard_map/pallas_call | solution.py:350
  82.9 7.7 %all-to-all-start.4 = ((f32[32,64,128]{2,1,0:T(8,128)}), f32[32,64,128]{2,1,0:T(8,128)S(1)}, u32[]{:S(2)}, u32[]{:S(2)}) async-start(f32[32,64,128]{2,1,0:T(8,128)} %bitcast.50), calls=%async_computation.4 | async-start | bytes 2097152 | tf_op jit(solution)/shard_map/all_to_all | solution.py:488
  91.0 0.1 select_reduce_fusion.19
  91.1 0.2 fusion.54
  91.7 0.7 compare_reduce_fusion.2
  92.3 0.7 compare_reduce_fusion.1
  94.3 0.7 compare_reduce_fusion
  95.6 3.1 %select_reduce_fusion.8 = (s32[16]{0:T(128)S(1)}, s32[16]{0:T(128)S(1)}, s32[16]{0:T(128)S(1)}, s32[16]{0:T(128)S(1)}, s32[16]{0:T(128)S(1)}, /*index=5*/s32[16]...) fusion(s32[32]{0:T(128)S(1)} %get-tuple-element.117, s32[32,16]{0,1:T(8,128)S(1)} %copy.121, ...), kind=kLoop, calls=%fused_computation.68 | loop fusion | flops 180064 | bytes 15808 | tf_op jit(solution)/shard_map/reduce_sum | solution.py:468
  98.9 0.1 reshape.972.tbl
  99.0 14.8 %all-to-all-done.4 = f32[32,64,128]{2,1,0:T(8,128)S(1)} async-done(((f32[32,64,128]{2,1,0:T(8,128)}), f32[32,64,128]{2,1,0:T(8,128)S(1)}, u32[]{:S(2)}, u32[]{:S(2)}) %all-to-all-start.4) | async-done | bytes 1048608 | tf_op jit(solution)/shard_map/all_to_all | solution.py:488
  113.9 11.2 %shard_map.68 = (f32[128,8,128]{2,1,0:T(8,128)S(1)}, f32[128,8,128]{2,1,0:T(8,128)S(1)}) custom-call(s32[160]{0:T(256)S(1)} %reshape.972.tbl, s32[27]{0:T(128)S(1)} %pad_add_fusion.4.out_tbl, f32[2048,128]{1,0:T(8,128)S(1)} %bitcast.86, f32[16,256,256]{2,1,0:T(8,128)} %bitcast.89), custom_call_target="tpu_custom_call" | custom-call | tf_op jit(solution)/shard_map/pallas_call | solution.py:360
  125.1 7.5 %collective-permute-start = (f32[128,8,128]{2,1,0:T(8,128)S(1)}, f32[128,8,128]{2,1,0:T(8,128)S(1)}, u32[]{:S(2)}, u32[]{:S(2)}) collective-permute-start(f32[128,8,128]{2,1,0:T(8,128)S(1)} %get-tuple-element.41), channel_id=1, source_target_pairs={{0,1},{1,0},{2,3},{3,2},{4,5},{5,4},{6,7},{7,6},{8,9},{9,8},{10,11... | collective-permute-start | bytes 1572872 | tf_op jit(solution)/shard_map/ppermute | solution.py:497
  132.7 1.5 collective-permute-done
  134.3 0.1 collective-permute-start.1
  134.4 3.1 %collective-permute-start.3 = (f32[32,8,128]{2,1,0:T(8,128)S(1)}, f32[32,8,128]{2,1,0:T(8,128)S(1)}, u32[]{:S(2)}, u32[]{:S(2)}) collective-permute-start(f32[32,8,128]{2,1,0:T(8,128)S(1)} %get-tuple-element.112), channel_id=1, source_target_pairs={{0,6},{1,7},{2,4},{3,5},{4,2},{5,3},{6,0},{7,1},{8,14},{9,15},{10,... | collective-permute-start | bytes 393224 | tf_op jit(solution)/shard_map/ppermute | solution.py:497
  137.5 0.3 collective-permute-start.2
  137.8 1.3 collective-permute-done.1
  139.1 3.7 %collective-permute-done.3 = f32[32,8,128]{2,1,0:T(8,128)S(1)} collective-permute-done((f32[32,8,128]{2,1,0:T(8,128)S(1)}, f32[32,8,128]{2,1,0:T(8,128)S(1)}, u32[]{:S(2)}, u32[]{:S(2)}) %collective-permute-start.3) | collective-permute-done | bytes 131104 | tf_op jit(solution)/shard_map/ppermute | solution.py:497
  142.8 0.6 collective-permute-done.2
  143.4 3.0 %collective-permute-start.6 = (f32[32,8,128]{2,1,0:T(8,128)S(1)}, f32[32,8,128]{2,1,0:T(8,128)S(1)}, u32[]{:S(2)}, u32[]{:S(2)}) collective-permute-start(f32[32,8,128]{2,1,0:T(8,128)S(1)} %fusion.22), channel_id=1, source_target_pairs={{0,6},{1,7},{2,4},{3,5},{4,2},{5,3},{6,0},{7,1},{8,14},{9,15},{10,... | collective-permute-start | bytes 393224 | tf_op jit(solution)/shard_map/ppermute | solution.py:497
  146.5 0.7 collective-permute-start.4
  147.1 4.7 %collective-permute-done.6 = f32[32,8,128]{2,1,0:T(8,128)S(1)} collective-permute-done((f32[32,8,128]{2,1,0:T(8,128)S(1)}, f32[32,8,128]{2,1,0:T(8,128)S(1)}, u32[]{:S(2)}, u32[]{:S(2)}) %collective-permute-start.6) | collective-permute-done | bytes 131104 | tf_op jit(solution)/shard_map/ppermute | solution.py:497
  152.0 3.5 %collective-permute-start.7 = (f32[128,8,128]{2,1,0:T(8,128)S(1)}, f32[128,8,128]{2,1,0:T(8,128)S(1)}, u32[]{:S(2)}, u32[]{:S(2)}) collective-permute-start(f32[128,8,128]{2,1,0:T(8,128)S(1)} %pad_maximum_fusion), channel_id=1, source_target_pairs={{0,1},{1,0},{2,3},{3,2},{4,5},{5,4},{6,7},{7,6},{8,9},{9,8},{10,11... | collective-permute-start | bytes 1572872 | tf_op jit(solution)/shard_map/ppermute | solution.py:497
  155.5 1.5 collective-permute-done.7
  157.0 0.6 constant_dynamic-slice_fusion.2
  157.6 1.3 fusion.78
  159.6 2.4 %conditional.1 = (f32[8,256,256]{2,1,0:T(8,128)S(1)}) conditional(s32[]{:T(128)} %bitcast.53, (s32[27]{0:T(128)S(1)}, s32[16]{0:T(128)S(1)}, f32[128,8,128]{2,1,0:T(8,128)S(1)}, f32[128,8,128]{2,1,0:T(8,128)S(1)}) %tuple.11, (s32[8]{0:T(128)S(1)}, s32[8]{0:T(128)S(1)}, s32[2,8]{1,0:T(2,128)S(1)}, f32[2,8,256,256]{3,2,1,0:T(8,128)}, ...), branch_computations={%region_23.24_spmd, %region_24.31_spmd} | conditional | flops 6547847168 | bytes 155251904 | solution.py:508
  159.6 2.1 %branch_0_fun.1 = f32[8,256,256]{2,1,0:T(8,128)S(1)} custom-call(s32[27]{0:T(128)S(1)} %get-tuple-element.28.out_tbl, s32[16]{0:T(128)S(1)} %get-tuple-element.29.sizes, f32[128,8,128]{2,1,0:T(8,128)S(1)} %get-tuple-element.30.own_ref, f32[128,8,128]{2,1,0:T(8,128)S(1)} %get-tuple-element.31.other_ref), custom_call_target="tpu_custom_call" | custom-call | tf_op jit(solution)/shard_map/cond/branch_0_fun/pallas_call | solution.py:371
  162.0 1.3 copy-done.2
  (70 shorter events, 3.0 us)
Async XLA Ops:
  8.7 20.4 %all-to-all-start.2 = ((s32[32,1,32]{2,1,0:T(1,128)}), s32[32,1,32]{2,1,0:T(1,128)S(1)}, u32[]{:S(2)}, u32[]{:S(2)}) async-start(s32[32,1,32]{2,1,0:T(1,128)} %broadcast_in_dim.277), calls=%async_computation.2 | async-start | bytes 32768 | tf_op jit(solution)/shard_map/all_to_all | solution.py:397
  51.2 28.4 %all-to-all-start.3 = ((f32[32,64,128]{2,1,0:T(8,128)}), f32[32,64,128]{2,1,0:T(8,128)S(1)}, u32[]{:S(2)}, u32[]{:S(2)}) async-start(f32[32,64,128]{2,1,0:T(8,128)} %bitcast.48), calls=%async_computation.3 | async-start | bytes 2097152 | tf_op jit(solution)/shard_map/all_to_all | solution.py:486
  82.9 31.0 %all-to-all-start.4 = ((f32[32,64,128]{2,1,0:T(8,128)}), f32[32,64,128]{2,1,0:T(8,128)S(1)}, u32[]{:S(2)}, u32[]{:S(2)}) async-start(f32[32,64,128]{2,1,0:T(8,128)} %bitcast.50), calls=%async_computation.4 | async-start | bytes 2097152 | tf_op jit(solution)/shard_map/all_to_all | solution.py:488
  113.9 41.6 %copy-start.3 = (s32[8]{0:T(128)S(1)}, s32[8]{0:T(128)}, u32[]{:S(2)}) copy-start(s32[8]{0:T(128)} %param.11) | copy-start | bytes 100
  113.9 41.6 %copy-start.4 = (s32[8]{0:T(128)S(1)}, s32[8]{0:T(128)}, u32[]{:S(2)}) copy-start(s32[8]{0:T(128)} %param.12) | copy-start | bytes 100
  113.9 45.7 %copy-start.1 = (f32[8,256,256]{2,1,0:T(8,128)S(1)}, f32[8,256,256]{2,1,0:T(8,128)}, u32[]{:S(2)}) copy-start(f32[8,256,256]{2,1,0:T(8,128)} %psi_ref.1) | copy-start | bytes 6291460
  113.9 45.7 %copy-start.5 = (s32[2,8]{1,0:T(2,128)S(1)}, s32[2,8]{1,0:T(2,128)}, u32[]{:S(2)}) copy-start(s32[2,8]{1,0:T(2,128)} %param.13) | copy-start | bytes 196
  125.1 9.1 %collective-permute-start = (f32[128,8,128]{2,1,0:T(8,128)S(1)}, f32[128,8,128]{2,1,0:T(8,128)S(1)}, u32[]{:S(2)}, u32[]{:S(2)}) collective-permute-start(f32[128,8,128]{2,1,0:T(8,128)S(1)} %get-tuple-element.41), channel_id=1, source_target_pairs={{0,1},{1,0},{2,3},{3,2},{4,5},{5,4},{6,7},{7,6},{8,9},{9,8},{10,11... | collective-permute-start | bytes 1572872 | tf_op jit(solution)/shard_map/ppermute | solution.py:497
  134.3 4.8 %collective-permute-start.1 = (f32[32,8,128]{2,1,0:T(8,128)S(1)}, f32[32,8,128]{2,1,0:T(8,128)S(1)}, u32[]{:S(2)}, u32[]{:S(2)}) collective-permute-start(f32[32,8,128]{2,1,0:T(8,128)S(1)} %get-tuple-element.111), channel_id=1, source_target_pairs={{0,2},{1,3},{2,0},{3,1},{4,6},{5,7},{6,4},{7,5},{8,10},{9,11},{10,... | collective-permute-start | bytes 393224 | tf_op jit(solution)/shard_map/ppermute | solution.py:497
  134.4 8.4 %collective-permute-start.3 = (f32[32,8,128]{2,1,0:T(8,128)S(1)}, f32[32,8,128]{2,1,0:T(8,128)S(1)}, u32[]{:S(2)}, u32[]{:S(2)}) collective-permute-start(f32[32,8,128]{2,1,0:T(8,128)S(1)} %get-tuple-element.112), channel_id=1, source_target_pairs={{0,6},{1,7},{2,4},{3,5},{4,2},{5,3},{6,0},{7,1},{8,14},{9,15},{10,... | collective-permute-start | bytes 393224 | tf_op jit(solution)/shard_map/ppermute | solution.py:497
  137.5 5.8 %collective-permute-start.2 = (f32[32,8,128]{2,1,0:T(8,128)S(1)}, f32[32,8,128]{2,1,0:T(8,128)S(1)}, u32[]{:S(2)}, u32[]{:S(2)}) collective-permute-start(f32[32,8,128]{2,1,0:T(8,128)S(1)} %get-tuple-element.113), channel_id=1, source_target_pairs={{0,4},{1,5},{2,6},{3,7},{4,0},{5,1},{6,2},{7,3},{8,12},{9,13},{10,... | collective-permute-start | bytes 393224 | tf_op jit(solution)/shard_map/ppermute | solution.py:497
  143.4 8.5 %collective-permute-start.6 = (f32[32,8,128]{2,1,0:T(8,128)S(1)}, f32[32,8,128]{2,1,0:T(8,128)S(1)}, u32[]{:S(2)}, u32[]{:S(2)}) collective-permute-start(f32[32,8,128]{2,1,0:T(8,128)S(1)} %fusion.22), channel_id=1, source_target_pairs={{0,6},{1,7},{2,4},{3,5},{4,2},{5,3},{6,0},{7,1},{8,14},{9,15},{10,... | collective-permute-start | bytes 393224 | tf_op jit(solution)/shard_map/ppermute | solution.py:497
  146.5 5.4 %collective-permute-start.5 = (f32[32,8,128]{2,1,0:T(8,128)S(1)}, f32[32,8,128]{2,1,0:T(8,128)S(1)}, u32[]{:S(2)}, u32[]{:S(2)}) collective-permute-start(f32[32,8,128]{2,1,0:T(8,128)S(1)} %fusion.22), channel_id=1, source_target_pairs={{0,4},{1,5},{2,6},{3,7},{4,0},{5,1},{6,2},{7,3},{8,12},{9,13},{10,... | collective-permute-start | bytes 393224 | tf_op jit(solution)/shard_map/ppermute | solution.py:497
  146.5 5.5 %collective-permute-start.4 = (f32[32,8,128]{2,1,0:T(8,128)S(1)}, f32[32,8,128]{2,1,0:T(8,128)S(1)}, u32[]{:S(2)}, u32[]{:S(2)}) collective-permute-start(f32[32,8,128]{2,1,0:T(8,128)S(1)} %fusion.22), channel_id=1, source_target_pairs={{0,2},{1,3},{2,0},{3,1},{4,6},{5,7},{6,4},{7,5},{8,10},{9,11},{10,... | collective-permute-start | bytes 393224 | tf_op jit(solution)/shard_map/ppermute | solution.py:497
  152.0 5.0 %collective-permute-start.7 = (f32[128,8,128]{2,1,0:T(8,128)S(1)}, f32[128,8,128]{2,1,0:T(8,128)S(1)}, u32[]{:S(2)}, u32[]{:S(2)}) collective-permute-start(f32[128,8,128]{2,1,0:T(8,128)S(1)} %pad_maximum_fusion), channel_id=1, source_target_pairs={{0,1},{1,0},{2,3},{3,2},{4,5},{5,4},{6,7},{7,6},{8,9},{9,8},{10,11... | collective-permute-start | bytes 1572872 | tf_op jit(solution)/shard_map/ppermute | solution.py:497
  162.0 1.3 copy-start.2

commit v2 on v1

v2 whole, which is shorter than its diff:
```python
import functools
import jax
import jax.numpy as jnp
from jax import lax
from jax.experimental import pallas as pl
from jax.experimental.pallas import tpu as pltpu
from jax.sharding import PartitionSpec as P

BLK = 256
LANES = 128
ROWS = 8
PEERS = 32
MEMBERS = 8
HELD = 8
PAIRS = 16
ROWS_OUT = 64
ROWS_IN = 64
PIECE = 32
VMEM_BYTES = 24 * 1024 * 1024
WIDE_BYTES = 56 * 1024 * 1024


def sector_mask(left_sizes, right_sizes, block_size):
    positions = jnp.arange(block_size, dtype=jnp.int32)
    row_ok = positions[None, :, None] < left_sizes[:, None, None]
    col_ok = positions[None, None, :] < right_sizes[:, None, None]
    return (row_ok & col_ok).astype(jnp.float32)


def pack_blocks(outgoing, targets, term_ids, sector_local, capacity, slot_count):
    target_device = targets // sector_local
    target_place = targets % sector_local
    count_out = targets.shape[0]
    order_index = jnp.arange(count_out, dtype=jnp.int32)
    same_device = target_device[:, None] == target_device[None, :]
    earlier = order_index[None, :] < order_index[:, None]
    peer_rank = jnp.sum((same_device & earlier).astype(jnp.int32), axis=1)
    send_slot = target_device * capacity + peer_rank
    chosen = jnp.arange(slot_count, dtype=jnp.int32)[:, None] == send_slot[None, :]
    slot_source = jnp.sum(jnp.where(chosen, order_index[None, :], 0), axis=1)
    filled = jnp.any(chosen, axis=1)
    buffer = jnp.where(filled[:, None, None], outgoing[slot_source], 0.0)
    left_code = term_ids * sector_local + target_place
    meta_codes = jnp.where(filled, left_code[slot_source], -1)
    return (buffer, meta_codes)


def apply_left(received, meta_codes, flat_left, sector_local, live_count):
    slot_count = meta_codes.shape[0]
    is_valid = meta_codes >= 0
    live_rank = jnp.cumsum(is_valid.astype(jnp.int32)) - 1
    wanted = jnp.arange(live_count, dtype=jnp.int32)
    picked = (live_rank[None, :] == wanted[:, None]) & is_valid[None, :]
    slot_index = jnp.arange(slot_count, dtype=jnp.int32)
    source_slot = jnp.sum(jnp.where(picked, slot_index[None, :], 0), axis=1)
    compact_blocks = received[source_slot]
    compact_codes = meta_codes[source_slot]
    chosen_left = flat_left[compact_codes]
    landed = jnp.einsum(
        "pab,pbc->pac", chosen_left, compact_blocks, precision=lax.Precision.HIGHEST
    )
    target_place = compact_codes % sector_local
    onehot_place = target_place[:, None] == jnp.arange(sector_local, dtype=jnp.int32)[None, :]
    return jnp.einsum(
        "pk,pac->kac", onehot_place.astype(jnp.float32), landed, precision=lax.Precision.HIGHEST
    )


def dense_program(psi_blocks, left_env, right_env, left_sizes, right_sizes, dest_sector):
    term_local = left_env.shape[0]
    sector_local = left_env.shape[1]
    block_size = left_env.shape[2]
    peers = lax.axis_size("sec")
    capacity = (term_local * sector_local + peers - 1) // peers
    slot_count = peers * capacity
    valid_mask = sector_mask(left_sizes, right_sizes, block_size)
    masked_psi = psi_blocks * valid_mask
    carried = jnp.einsum("sab,tsbc->tsac", masked_psi, right_env, precision=lax.Precision.HIGHEST)
    flat_left = left_env.reshape(term_local * sector_local, block_size, block_size)
    term_ids = jnp.repeat(jnp.arange(term_local, dtype=jnp.int32), sector_local)
    buffer, meta_codes = pack_blocks(
        carried.reshape(term_local * sector_local, block_size, block_size),
        dest_sector.reshape(term_local * sector_local),
        term_ids,
        sector_local,
        capacity,
        slot_count,
    )
    received, codes_in = (
        lax.all_to_all(buffer, "sec", split_axis=0, concat_axis=0, tiled=True),
        lax.all_to_all(meta_codes, "sec", split_axis=0, concat_axis=0, tiled=True),
    )
    partial_sum = apply_left(received, codes_in, flat_left, sector_local, term_local * sector_local)
    total = lax.psum(partial_sum, "term")
    return total * valid_mask


def split3(a):
    hi = a.astype(jnp.bfloat16)
    lo = (a - hi.astype(jnp.float32)).astype(jnp.bfloat16)
    return hi, lo


def dot3(a, b, transposed=False):
    dims = (((1,), (1 if transposed else 0,)), ((), ()))
    mul = functools.partial(
        lax.dot_general, dimension_numbers=dims, preferred_element_type=jnp.float32
    )
    return mul(a[0], b[0]) + (mul(a[0], b[1]) + mul(a[1], b[0]))


T_START, T_ROWS, T_NX, T_NY, T_LEFT, T_RIGHT, T_BASE = 0, 1, 2, 3, 4, 5, 6
T_WIDTH = 10


def tile_rows(stream, rows):
    return (stream % 4) * (ROWS * rows) + jnp.minimum(stream // 4, rows - 1)


def tile_at(a):
    return pl.ds(pl.multiple_of(a * ROWS, ROWS), ROWS)


def strip_at(strip):
    return pl.ds(strip * LANES, LANES)


def block_at(i):
    return pl.ds(pl.multiple_of(i * LANES, LANES), LANES)


def variants(k_blocks, n_blocks, body):
    for k in (1, 2):
        for n in (1, 2):
            @pl.when((k_blocks == k) & (n_blocks == n))
            def _():
                body(k * LANES, n * LANES)


S_PSI, S_PROD, S_TURN, S_RIGHT, STRIPS = 0, 2, 6, 10, 14
TOGETHER = 2


def carry_kernel(sizes, psi_ref, right_ref, strip_ref):
    row = lax.broadcasted_iota(jnp.int32, (BLK, BLK), 0)
    col = lax.broadcasted_iota(jnp.int32, (BLK, BLK), 1)

    def put(i, first, block):
        for strip in range(2):
            strip_ref[i, first + strip] = block[:, strip * LANES : (strip + 1) * LANES]

    for i in range(TOGETHER):
        d = pl.program_id(0) * TOGETHER + i
        kept = (row < sizes[d]) & (col < sizes[HELD + d])
        psi = jnp.where(kept, psi_ref[i], 0.0)
        parts = split3(psi)
        put(i, S_PSI, psi.T)
        for t in range(PAIRS // HELD):
            right = right_ref[t, i]
            product = dot3(parts, split3(right))
            put(i, S_RIGHT + 2 * t, right)
            put(i, S_PROD + 2 * t, product)
            put(i, S_TURN + 2 * t, product.T)


def send_kernel(tbl, strip_ref, buf_ref, held_ref, sems):
    def copy(e):
        return pltpu.make_async_copy(strip_ref.at[tbl[3 * e]], held_ref.at[e], sems.at[e])

    for e in range(4 * PAIRS):
        @pl.when(tbl[3 * e + 1] > 0)
        def _():
            copy(e).start()

    for e in range(4 * PAIRS):
        rows, first = tbl[3 * e + 1], tbl[3 * e + 2]

        @pl.when(rows > 0)
        def _():
            copy(e).wait()

            def four(i, inner):
                for k in range(4):
                    a = i * 4 + k
                    at = tile_rows(first + a, ROWS_OUT)
                    buf_ref[pl.ds(at, ROWS, stride=ROWS_OUT), :] = held_ref[e, tile_at(a), :]
                return inner

            lax.fori_loop(0, (rows + 3) // 4, four, 0)


def relay_kernel(idx, count, in_ref, out_ref):
    def slot(peer, carry):
        def some(i, inner):
            at = peer * ROWS_IN + i * ROWS
            for k in range(ROWS):
                out_ref[pl.ds(at + k, 1), :] = in_ref[pl.ds(idx[at + k], 1), :]
            return inner

        lax.fori_loop(0, (count[peer] + ROWS - 1) // ROWS, some, 0)
        return carry

    lax.fori_loop(0, PEERS, slot, 0)


STREAM = MEMBERS * PIECE


def piece_at(place, core, chip):
    piece = ((place // 4) ^ core) * 4 + ((place % 4) ^ chip)
    return pl.ds(pl.multiple_of(piece * PIECE, PIECE), PIECE)


def land_kernel(
    tbl, out_tbl, buf_ref, left_ref, keep_ref, send_ref, x_ref, y_ref, z_ref, sum_ref, stream_ref
):
    z_ref[...] = jnp.zeros_like(z_ref)

    def take(dst_ref, u, strip, before, rows):
        at = u * T_WIDTH
        start = tbl[at + T_START] + before
        begin = []
        for k in range(4):
            kind = (start + k) % 4
            rank = tbl[at + T_BASE + kind] + (before + k) // 4
            begin.append((kind * (ROWS * ROWS_IN), rank))

        def four(i, carry):
            for k in range(4):
                first, rank = begin[k]
                row = first + jnp.minimum(rank + i, ROWS_IN - 1)
                dst_ref[u, tile_at(i * 4 + k), strip_at(strip)] = buf_ref[
                    pl.ds(row, ROWS, stride=ROWS_IN), :
                ]
            return carry

        lax.fori_loop(0, (rows + 3) // 4, four, 0)

    def unpack(u, carry):
        at = u * T_WIDTH
        rows, nx, ny = tbl[at + T_ROWS], tbl[at + T_NX], tbl[at + T_NY]
        for strip in range(2):
            @pl.when(strip < nx)
            def _():
                take(x_ref, u, strip, strip * rows, rows)

            @pl.when(strip < ny)
            def _():
                take(y_ref, u, strip, (nx + strip) * rows, rows)

        return carry

    lax.fori_loop(0, PAIRS, unpack, 0)

    def blocks(rows):
        return (rows * ROWS + LANES - 1) // LANES

    def sector(d, carry):
        first, out_rows, strips = out_tbl[3 * d], out_tbl[3 * d + 1], out_tbl[3 * d + 2]
        units = [d + t * HELD for t in range(PAIRS // HELD)]
        rows = [tbl[u * T_WIDTH + T_ROWS] for u in units]
        nx = [tbl[u * T_WIDTH + T_NX] for u in units]
        ny = [tbl[u * T_WIDTH + T_NY] for u in units]
        m_blocks = blocks(out_rows)

        def masked(ref, t, height, width, count):
            row = lax.broadcasted_iota(jnp.int32, (height, width), 0)
            col = lax.broadcasted_iota(jnp.int32, (height, width), 1)
            kept = (row < rows[t] * ROWS) & (col < count * LANES)
            return jnp.where(kept, ref[units[t], :height, :width], 0.0)

        def turned(k, n):
            mats = [split3(masked(x_ref, t, n, k, nx[t])) for t in range(2)]

            def some(i, inner):
                for t in range(2):
                    z_ref[t, block_at(i), :n] = dot3(
                        split3(left_ref[units[t], block_at(i), :k]), mats[t], transposed=True
                    )
                return inner

            lax.fori_loop(0, m_blocks, some, 0)

        inner_x = [jnp.where(nx[t] > 0, blocks(rows[t]), 0) for t in range(2)]
        variants(jnp.maximum(nx[0], nx[1]), jnp.maximum(inner_x[0], inner_x[1]), turned)

        def added(k, n):
            mats = [split3(masked(y_ref, t, k, n, ny[t])) for t in range(2)]

            def some(i, inner):
                total = None
                for t in range(2):
                    a = jnp.where(
                        nx[t] > 0, z_ref[t, block_at(i), :k], left_ref[units[t], block_at(i), :k]
                    )
                    part = dot3(split3(a), mats[t]) + jnp.where(
                        ny[t] > 0, 0.0, z_ref[t, block_at(i), :n]
                    )
                    total = part if total is None else total + part
                sum_ref[block_at(i), :n] = total
                return inner

            lax.fori_loop(0, m_blocks, some, 0)

        inner_y = [jnp.where(ny[t] > 0, blocks(rows[t]), 1) for t in range(2)]
        variants(jnp.maximum(inner_y[0], inner_y[1]), strips, added)

        for strip in range(2):
            @pl.when(strip < strips)
            def _():
                begin = first + strip * out_rows

                def four(i, inner):
                    at = jnp.minimum(begin + i * 4, STREAM)
                    for k in range(4):
                        stream_ref[at + k] = sum_ref[tile_at(i * 4 + k), strip_at(strip)]
                    return inner

                lax.fori_loop(0, (out_rows + 3) // 4, four, 0)
        return carry

    lax.fori_loop(0, HELD, sector, 0)
    core, chip = out_tbl[O_CORE], out_tbl[O_CHIP]
    flag = jnp.full((ROWS, LANES), out_tbl[O_FLAG], jnp.int32).astype(jnp.float32)
    stream_ref[STREAM - 1] = flag
    for place in range(4):
        into = pl.ds(place * PIECE, PIECE)
        keep_ref[into] = stream_ref[piece_at(place, core, chip)]
        send_ref[into] = stream_ref[piece_at(place + 4, core, chip)]


def spread_kernel(out_tbl, sizes, own_ref, other_ref, out_ref, flag_ref, stream_ref):
    d = pl.program_id(0)

    @pl.when(d == 0)
    def _():
        core, chip = out_tbl[O_CORE], out_tbl[O_CHIP]
        for place in range(4):
            part = pl.ds(place * PIECE, PIECE)
            stream_ref[piece_at(place, core, chip)] = own_ref[part]
            stream_ref[piece_at(place + 4, core, chip)] = other_ref[part]
        flag_ref[0] = jnp.max(stream_ref[STREAM - 1])

    row = lax.broadcasted_iota(jnp.int32, (ROWS, LANES), 0)
    col = lax.broadcasted_iota(jnp.int32, (ROWS, LANES), 1)
    out_ref[...] = jnp.zeros_like(out_ref)
    first, rows, strips = out_tbl[3 * d], out_tbl[3 * d + 1], out_tbl[3 * d + 2]
    height, width = sizes[d], sizes[HELD + d]
    for strip in range(2):
        @pl.when(strip < strips)
        def _():
            begin = first + strip * rows
            col_ok = col + strip * LANES < width

            def four(i, inner):
                at = jnp.minimum(begin + i * 4, STREAM)
                for k in range(4):
                    a = i * 4 + k
                    kept = col_ok & (row + a * ROWS < height)
                    tile = jnp.where(kept, stream_ref[at + k], 0.0)
                    out_ref[0, tile_at(a), strip_at(strip)] = tile
                return inner

            lax.fori_loop(0, (rows + 3) // 4, four, 0)


O_CORE, O_CHIP, O_FLAG = 3 * HELD, 3 * HELD + 1, 3 * HELD + 2

SMEM = pl.BlockSpec(memory_space=pltpu.SMEM)
VMEM = pl.BlockSpec(memory_space=pltpu.VMEM)
PARAMS = pltpu.CompilerParams(vmem_limit_bytes=VMEM_BYTES)
WIDE = pltpu.CompilerParams(vmem_limit_bytes=WIDE_BYTES)


def floats(*shape):
    return jax.ShapeDtypeStruct(shape, jnp.float32)


def scratch(*shape):
    return pltpu.VMEM(shape, jnp.float32)


def carry_call(sizes, psi, right):
    return pl.pallas_call(
        carry_kernel,
        grid=(HELD // TOGETHER,),
        out_shape=floats(HELD, STRIPS, BLK, LANES),
        in_specs=[
            SMEM,
            pl.BlockSpec((TOGETHER, BLK, BLK), lambda d: (d, 0, 0)),
            pl.BlockSpec((PAIRS // HELD, TOGETHER, BLK, BLK), lambda d: (0, d, 0, 0)),
        ],
        out_specs=pl.BlockSpec((TOGETHER, STRIPS, BLK, LANES), lambda d: (d, 0, 0, 0)),
        cost_estimate=pl.CostEstimate(
            flops=6 * PAIRS * BLK**3, bytes_accessed=24 * 2**20, transcendentals=0
        ),
        compiler_params=WIDE,
    )(sizes, psi, right)


def send_call(tbl, strips):
    return pl.pallas_call(
        send_kernel,
        out_shape=floats(PEERS * ROWS_OUT, LANES),
        in_specs=[SMEM, pl.BlockSpec(memory_space=pl.ANY)],
        out_specs=VMEM,
        scratch_shapes=[
            scratch(4 * PAIRS, BLK, LANES),
            pltpu.SemaphoreType.DMA((4 * PAIRS,)),
        ],
        compiler_params=WIDE,
    )(tbl, strips)


def relay_call(idx, count, received):
    return pl.pallas_call(
        relay_kernel,
        out_shape=floats(PEERS * ROWS_IN, LANES),
        in_specs=[SMEM, SMEM, VMEM],
        out_specs=VMEM,
        compiler_params=PARAMS,
    )(idx, count, received)


def land_call(tbl, out_tbl, received, left):
    return pl.pallas_call(
        land_kernel,
        out_shape=[floats(4 * PIECE, ROWS, LANES)] * 2,
        in_specs=[SMEM, SMEM, VMEM, VMEM],
        out_specs=[VMEM, VMEM],
        scratch_shapes=[
            scratch(PAIRS, BLK, BLK),
            scratch(PAIRS, BLK, BLK),
            scratch(PAIRS // HELD, BLK, BLK),
            scratch(BLK, BLK),
            scratch(STREAM + ROWS, ROWS, LANES),
        ],
        compiler_params=PARAMS,
    )(tbl, out_tbl, received, left)


def spread_call(out_tbl, sizes, own, other):
    return pl.pallas_call(
        spread_kernel,
        grid=(HELD,),
        out_shape=[floats(HELD, BLK, BLK), floats(1)],
        in_specs=[SMEM, SMEM, VMEM, VMEM],
        out_specs=[pl.BlockSpec((1, BLK, BLK), lambda d: (d, 0, 0)), SMEM],
        scratch_shapes=[scratch(STREAM + ROWS, ROWS, LANES)],
        compiler_params=WIDE,
    )(out_tbl, sizes, own, other)


def up(value, unit):
    return (value + (unit - 1)) // unit


def before(values, axis):
    n = values.shape[axis]
    moved = jnp.moveaxis(values, axis, -1)
    lower = jnp.arange(n)[:, None] > jnp.arange(n)[None, :]
    total = jnp.sum(jnp.where(lower, moved[..., None, :], 0), axis=-1)
    return jnp.moveaxis(total, -1, axis)


def make_tables(facts, me, core, chip):
    size_l, size_r = facts[:, 0], facts[:, 1]
    dest = facts[:, 2:].reshape(PEERS, PAIRS)

    ls = jnp.concatenate([size_l, size_l], axis=1)
    rs = jnp.concatenate([size_r, size_r], axis=1)
    to_dev = dest // HELD
    hit_dev = to_dev[:, :, None] == jnp.arange(PEERS)[None, None, :]
    sector = jnp.arange(PEERS * HELD)[:, None]
    rd = jnp.sum(
        jnp.where(dest.reshape(1, -1) == sector, size_r.reshape(-1)[:, None], 0), axis=0
    ).reshape(PEERS, PAIRS)
    nl, nr = up(ls, LANES), up(rd, LANES)
    cost_c = up(ls, ROWS) * nr
    cost_ct = up(rd, ROWS) * nl
    cost_f = up(rs, ROWS) * (nl + nr)
    is_f = (cost_f < cost_c) & (cost_f < cost_ct)
    is_ct = ~is_f & (cost_ct < cost_c)
    rows = up(jnp.where(is_f, rs, jnp.where(is_ct, rd, ls)), ROWS)
    nx = jnp.where(is_f | is_ct, nl, 0)
    ny = jnp.where(is_ct, 0, nr)
    tiles = rows * (nx + ny)
    start = before(tiles, 1)
    total = jnp.sum(tiles, axis=1)

    kinds = jnp.arange(4)[:, None, None]
    lag = (kinds - start) % 4
    share = (tiles + 3 - lag) // 4
    first_row = (start + lag) // 4
    onto = jnp.sum(jnp.where(hit_dev[None], share[..., None], 0), axis=2)
    base = before(onto, 1)
    filled = jnp.sum(onto, axis=1)

    out_rows, out_strips = up(size_l, ROWS), up(size_r, LANES)
    out_tiles = out_rows * out_strips
    out_first = before(out_tiles, 1)
    spilled = (
        jnp.any(total > 4 * (ROWS_OUT - 1))
        | jnp.any(filled > ROWS_IN)
        | jnp.any(jnp.sum(out_tiles, axis=1) > MEMBERS * PIECE - 1)
    )

    def own(values, axis=0):
        return lax.dynamic_index_in_dim(values, me, axis, keepdims=False)

    pair, place = jnp.arange(PAIRS)[:, None], jnp.arange(4)[None, :]
    own_nx, own_ny, own_rows = own(nx)[:, None], own(ny)[:, None], own(rows)[:, None]
    both = (own_nx > 0) & (own_ny > 0)
    term, held = pair // HELD, pair % HELD
    source = jnp.where(
        place < 2,
        jnp.where(both, S_PSI, S_TURN + 2 * term),
        jnp.where(both, S_RIGHT, S_PROD) + 2 * term,
    )
    source = held * STRIPS + source + place % 2
    used = jnp.where(place < 2, place < own_nx, place - 2 < own_ny)
    index = jnp.where(place < 2, place, own_nx + place - 2)
    send_tbl = jnp.stack(
        [source, jnp.where(used, own_rows, 0), own(start)[:, None] + index * own_rows], axis=2
    ).reshape(-1)

    kind = me // ROWS
    onto_k = lax.dynamic_index_in_dim(onto, kind, 0, keepdims=False)
    base_k = lax.dynamic_index_in_dim(base, kind, 0, keepdims=False)
    first_k = lax.dynamic_index_in_dim(first_row, kind, 0, keepdims=False)
    filled_k = lax.dynamic_index_in_dim(filled, kind, 0, keepdims=False)
    first_to = jnp.sum(jnp.where(hit_dev, first_k[:, :, None], 0), axis=1)
    rank = jnp.arange(ROWS_IN)[None, None, :]
    here = (rank >= base_k[:, :, None]) & (rank < (base_k + onto_k)[:, :, None])
    origin = jnp.arange(PEERS)[:, None] * ROWS_OUT + first_to - base_k
    relay_idx = jnp.sum(jnp.where(here, origin[:, :, None] + rank, 0), axis=0)
    relay_idx = jnp.clip(relay_idx, 0, PEERS * ROWS_OUT - 1).reshape(-1)
    relay_count = jnp.minimum(filled_k, ROWS_IN)

    unit = jnp.arange(PAIRS)[:, None, None]
    reach = (dest[None] == me * HELD + unit % HELD) & (
        (jnp.arange(PAIRS) // HELD)[None, None, :] == unit // HELD
    )

    def reached(values):
        return jnp.sum(jnp.where(reach, values[None], 0), axis=(1, 2))

    base_me = lax.dynamic_index_in_dim(base, me, 2, keepdims=False)
    land_tbl = jnp.stack(
        [reached(start), reached(rows), reached(nx), reached(ny), reached(ls), reached(rs)]
        + [reached(jnp.broadcast_to(base_me[g][:, None], (PEERS, PAIRS))) for g in range(4)],
        axis=1,
    ).reshape(-1)

    out_tbl = jnp.concatenate(
        [
            jnp.stack([own(out_first), own(out_rows), own(out_strips)], axis=1).reshape(-1),
            jnp.stack([core, chip, spilled.astype(jnp.int32)]).astype(jnp.int32),
        ]
    )
    return send_tbl, relay_idx, relay_count, land_tbl, out_tbl


def per_device(psi_blocks, left_env, right_env, left_sizes, right_sizes, dest_sector):
    me = lax.axis_index("sec")
    member = lax.axis_index("term")
    core, chip = member % 2, member // 2
    sizes = jnp.concatenate([left_sizes, right_sizes])
    strips = carry_call(sizes, psi_blocks, right_env).reshape(HELD * STRIPS, BLK, LANES)
    mine = jnp.concatenate([left_sizes[None], right_sizes[None], dest_sector])
    facts = lax.all_to_all(
        jnp.broadcast_to(mine[None], (PEERS, 4, HELD)), "sec", 0, 0, tiled=True
    )
    tables = make_tables(facts, me, core, chip)
    send_tbl, relay_idx, relay_count, land_tbl, out_tbl = tables

    sent = send_call(send_tbl, strips)
    hop = lax.all_to_all(sent.reshape(PEERS, ROWS_OUT, LANES), "sec", 0, 0, tiled=True)
    passed = relay_call(relay_idx, relay_count, hop.reshape(PEERS * ROWS_OUT, LANES))
    hop = lax.all_to_all(passed.reshape(PEERS, ROWS_IN, LANES), "sec", 0, 0, tiled=True)
    keep, give = land_call(
        land_tbl,
        out_tbl,
        hop.reshape(PEERS * ROWS_IN, LANES),
        left_env.reshape(PAIRS, BLK, BLK),
    )

    def swap(values, bits):
        return lax.ppermute(values, "term", [(i, i ^ bits) for i in range(MEMBERS)])

    half = (keep + swap(give, 1)).reshape(4, PIECE, ROWS, LANES)
    piece = half[0] + swap(half[1], 2) + swap(half[2], 4) + swap(half[3], 6)
    whole = jnp.concatenate([piece, swap(piece, 2), swap(piece, 4), swap(piece, 6)])
    other = swap(whole, 1)

    packed, flag = spread_call(out_tbl, sizes, whole, other)
    return lax.cond(
        flag[0] > 0.5,
        lambda: dense_program(
            psi_blocks, left_env, right_env, left_sizes, right_sizes, dest_sector
        ),
        lambda: packed,
    )


def solution(mesh):
    in_specs = (
        P("sec", None, None),
        P("term", "sec", None, None),
        P("term", "sec", None, None),
        P("sec"),
        P("sec"),
        P("term", "sec"),
    )
    out_specs = P("sec", None, None)
    return jax.shard_map(
        per_device, mesh=mesh, in_specs=in_specs, out_specs=out_specs, check_vma=False
    )
```

time: 173 us -> 161 us (0.931)
  other arithmetic: 22.5 us -> 12.2 us
  waiting for transfers between devices: 56.7 us -> 50 us
  starting transfers between devices: 42 us -> 45.4 us
  Pallas kernels: 26.5 us -> 29.7 us
    reduce_sum x6 -> x5, other arithmetic: 11.7 us -> 1.45 us  [the longest x1 0.57 us: make_tables(): relay_idx = jnp.sum(jnp.where(here, origin[:, :, None] + rank, 0), axis=0)]
    pallas_call x1 -> x2, Pallas kernels: 2.09 us -> 12 us  [the longest x1 9.42 us: carry_call(): pl.pallas_call(carry_kernel, grid=(HELD // TOGETHER,), out_shape=floats(H...]
    all_to_all x1, waiting for transfers between devices: 8.5 us -> 0.01 us  [per_device(): lax.all_to_all(jnp.broadcast_to(mine[None], (PEERS, 4, HELD)), 'sec', 0,...]
    all_to_all x1, starting transfers between devices: 4.16 us -> 9.9 us  [per_device(): lax.all_to_all(sent.reshape(PEERS, ROWS_OUT, LANES), 'sec', 0, 0, tiled=T...]
    pallas_call x1, Pallas kernels: 9.98 us -> 4.48 us  [send_call(): pl.pallas_call(send_kernel, out_shape=floats(PEERS * ROWS_OUT, LANES), in...]
    ppermute x8, starting transfers between devices: 18.3 us -> 14.9 us  [swap(): return lax.ppermute(values, 'term', [(i, i ^ bits) for i in range(MEMBERS)])]
  transfers between devices with their start and end apart: 11 -> 11, of which waited for: 10 -> 10; matrix products, arithmetic and copies ran while one was open for 6% -> 8% of each run, Pallas kernels for 0% -> 6%
where the time goes in v2:
time: 161 us; the launch traced here: 160 us
  waiting for transfers between devices  50 us (31%)
  starting transfers between devices  45.4 us (28%)
  Pallas kernels  29.7 us (18%)
  between operations  16.3 us (10%)
  other arithmetic  12.2 us (8%)
  local copies, waits for them, and re-layouts  5.95 us (4%)
    all_to_all x1, waiting for transfers between devices, per_device(): lax.all_to_all(sent.reshape(PEERS, ROWS_OUT, LANES), 'sec', 0, 0, tiled=T...  20.1 us
    all_to_all x1, waiting for transfers between devices, per_device(): lax.all_to_all(passed.reshape(PEERS, ROWS_IN, LANES), 'sec', 0, 0, tiled=...  15.9 us
    ppermute x8, starting transfers between devices, swap(): return lax.ppermute(values, 'term', [(i, i ^ bits) for i in range(MEMBERS)])  14.9 us
    ppermute x8, waiting for transfers between devices, swap(): return lax.ppermute(values, 'term', [(i, i ^ bits) for i in range(MEMBERS)])  14 us
    all_to_all x1, starting transfers between devices, per_device(): lax.all_to_all(jnp.broadcast_to(mine[None], (PEERS, 4, HELD)), 'sec', 0,...  11.9 us
    pallas_call x1, Pallas kernels, land_call(): pl.pallas_call(land_kernel, out_shape=[floats(4 * PIECE, ROWS, LANES)] *...  9.92 us
    all_to_all x1, starting transfers between devices, per_device(): lax.all_to_all(sent.reshape(PEERS, ROWS_OUT, LANES), 'sec', 0, 0, tiled=T...  9.9 us
    pallas_call x1, Pallas kernels, carry_call(): pl.pallas_call(carry_kernel, grid=(HELD // TOGETHER,), out_shape=floats(H...  9.42 us
  transfers between devices with their start and end apart: 11, of which 10 were waited for; matrix products, arithmetic and copies ran while one was open for 8% of the time, Pallas kernels for 6%

profile of v2, /device:TPU:1, one launch (start us, length us, event | category | flops | bytes accessed | tf_op | source)
XLA Modules:
  0.0 159.7 jit_solution(13573021313161081415)
XLA Ops:
  6.5 0.7 pad_add_fusion.3
  7.2 0.6 broadcast_in_dim.363
  7.9 11.9 %all-to-all-start.2 = ((s32[32,4,8]{2,1,0:T(4,128)}), s32[32,4,8]{2,1,0:T(4,128)S(1)}, u32[]{:S(2)}, u32[]{:S(2)}) async-start(s32[32,4,8]{2,1,0:T(4,128)} %broadcast_in_dim.363), calls=%async_computation.2 | async-start | bytes 131072 | tf_op jit(solution)/shard_map/all_to_all | solution.py:571
  19.8 1.3 and_select_fusion.6
  21.1 9.4 %shard_map.66 = f32[8,14,256,128]{3,2,1,0:T(8,128)} custom-call(s32[16]{0:T(128)} %get-tuple-element.120.sizes, f32[8,256,256]{2,1,0:T(8,128)} %psi_ref.1, f32[2,8,256,256]{3,2,1,0:T(8,128)} %right_ref.1), custom_call_target="tpu_custom_call" | custom-call | flops 1610612736 | bytes 25165824 | tf_op jit(solution)/shard_map/pallas_call | solution.py:384
  30.8 0.1 select_reduce_fusion.6
  31.0 0.1 compare_and_fusion.1
  31.4 0.1 select_reduce_fusion.18
  31.6 0.2 dynamic-slice_reduce_fusion
  32.0 0.7 reshape.1520.tbl
  32.7 4.5 %shard_map.67 = f32[2048,128]{1,0:T(8,128)} custom-call(s32[192]{0:T(256)} %reshape.1520.tbl, f32[112,256,128]{2,1,0:T(8,128)} %bitcast.94), custom_call_target="tpu_custom_call" | custom-call | tf_op jit(solution)/shard_map/pallas_call | solution.py:402
  37.2 9.9 %all-to-all-start.3 = ((f32[32,64,128]{2,1,0:T(8,128)}), f32[32,64,128]{2,1,0:T(8,128)S(1)}, u32[]{:S(2)}, u32[]{:S(2)}) async-start(f32[32,64,128]{2,1,0:T(8,128)} %bitcast.98), calls=%async_computation.3 | async-start | bytes 2097152 | tf_op jit(solution)/shard_map/all_to_all | solution.py:578
  47.4 0.2 select_reduce_fusion.7
  47.7 0.1 iota_compare_fusion.9
  47.9 0.4 select_reduce_fusion.3
  48.5 2.2 %select_reduce_fusion.2 = s32[4,32,32]{2,1,0:T(8,128)S(1)} fusion(s32[4,32,32]{2,1,0:T(8,128)S(1)} %copy.141, pred[32,32]{1,0:T(8,128)(4,1)S(1)} %iota_compare_fusion.10), kind=kLoop, calls=%fused_computation.53 | loop fusion | flops 258048 | bytes 33792 | tf_op jit(solution)/shard_map/reduce_sum | solution.py:462
  50.9 0.6 select_reduce_fusion.5
  51.6 20.1 %all-to-all-done.3 = f32[32,64,128]{2,1,0:T(8,128)S(1)} async-done(((f32[32,64,128]{2,1,0:T(8,128)}), f32[32,64,128]{2,1,0:T(8,128)S(1)}, u32[]{:S(2)}, u32[]{:S(2)}) %all-to-all-start.3) | async-done | bytes 1048608 | tf_op jit(solution)/shard_map/all_to_all | solution.py:578
  71.7 3.3 %shard_map.68 = f32[2048,128]{1,0:T(8,128)} custom-call(s32[2048]{0:T(1024)S(1)} %min.18.idx, s32[32]{0:T(128)S(1)} %fusion.70.count, f32[2048,128]{1,0:T(8,128)S(1)} %bitcast.92), custom_call_target="tpu_custom_call" | custom-call | tf_op jit(solution)/shard_map/pallas_call | solution.py:416
  75.0 8.7 %all-to-all-start.4 = ((f32[32,64,128]{2,1,0:T(8,128)}), f32[32,64,128]{2,1,0:T(8,128)S(1)}, u32[]{:S(2)}, u32[]{:S(2)}) async-start(f32[32,64,128]{2,1,0:T(8,128)} %bitcast.51), calls=%async_computation.4 | async-start | bytes 2097152 | tf_op jit(solution)/shard_map/all_to_all | solution.py:580
  83.8 0.1 reduce_sum.213
  84.4 0.2 fusion.60
  84.6 0.1 add_select_fusion.11
  85.0 0.7 compare_reduce_fusion.2
  85.7 0.7 compare_reduce_fusion.1
  87.7 0.7 compare_reduce_fusion
  89.0 3.1 %select_reduce_fusion.8 = (s32[16]{0:T(128)S(1)}, s32[16]{0:T(128)S(1)}, s32[16]{0:T(128)S(1)}, s32[16]{0:T(128)S(1)}, s32[16]{0:T(128)S(1)}, /*index=5*/s32[16]...) fusion(s32[32]{0:T(128)S(1)} %get-tuple-element.105, s32[32,16]{0,1:T(8,128)S(1)} %bitcast.110, ...), kind=kLoop, calls=%fused_computation.68 | loop fusion | flops 180064 | bytes 15808 | tf_op jit(solution)/shard_map/reduce_sum | solution.py:546
  92.4 15.9 %all-to-all-done.4 = f32[32,64,128]{2,1,0:T(8,128)S(1)} async-done(((f32[32,64,128]{2,1,0:T(8,128)}), f32[32,64,128]{2,1,0:T(8,128)S(1)}, u32[]{:S(2)}, u32[]{:S(2)}) %all-to-all-start.4) | async-done | bytes 1048608 | tf_op jit(solution)/shard_map/all_to_all | solution.py:580
  108.3 9.9 %shard_map.69 = (f32[128,8,128]{2,1,0:T(8,128)S(1)}, f32[128,8,128]{2,1,0:T(8,128)S(1)}) custom-call(s32[160]{0:T(256)S(1)} %reshape.1519.tbl, s32[27]{0:T(128)S(1)} %pad_add_fusion.5.out_tbl, f32[2048,128]{1,0:T(8,128)S(1)} %bitcast.93, f32[16,256,256]{2,1,0:T(8,128)} %bitcast.96), custom_call_target="tpu_custom_call" | custom-call | tf_op jit(solution)/shard_map/pallas_call | solution.py:426
  118.3 5.4 %collective-permute-start = (f32[128,8,128]{2,1,0:T(8,128)S(1)}, f32[128,8,128]{2,1,0:T(8,128)S(1)}, u32[]{:S(2)}, u32[]{:S(2)}) collective-permute-start(f32[128,8,128]{2,1,0:T(8,128)S(1)} %get-tuple-element.32), channel_id=1, source_target_pairs={{0,1},{1,0},{2,3},{3,2},{4,5},{5,4},{6,7},{7,6},{8,9},{9,8},{10,11... | collective-permute-start | bytes 1572872 | tf_op jit(solution)/shard_map/ppermute | solution.py:589
  123.7 1.5 collective-permute-done
  125.3 0.7 collective-permute-start.1
  126.0 1.9 %collective-permute-start.3 = (f32[32,8,128]{2,1,0:T(8,128)S(1)}, f32[32,8,128]{2,1,0:T(8,128)S(1)}, u32[]{:S(2)}, u32[]{:S(2)}) collective-permute-start(f32[32,8,128]{2,1,0:T(8,128)S(1)} %get-tuple-element.100), channel_id=1, source_target_pairs={{0,6},{1,7},{2,4},{3,5},{4,2},{5,3},{6,0},{7,1},{8,14},{9,15},{10,... | collective-permute-start | bytes 393224 | tf_op jit(solution)/shard_map/ppermute | solution.py:589
  127.9 1.1 collective-permute-start.2
  128.9 1.1 collective-permute-done.1
  130.1 1.5 collective-permute-done.3
  131.6 3.4 %collective-permute-done.2 = f32[32,8,128]{2,1,0:T(8,128)S(1)} collective-permute-done((f32[32,8,128]{2,1,0:T(8,128)S(1)}, f32[32,8,128]{2,1,0:T(8,128)S(1)}, u32[]{:S(2)}, u32[]{:S(2)}) %collective-permute-start.2) | collective-permute-done | bytes 131104 | tf_op jit(solution)/shard_map/ppermute | solution.py:589
  135.0 1.4 collective-permute-start.6
  136.5 1.9 %collective-permute-start.4 = (f32[32,8,128]{2,1,0:T(8,128)S(1)}, f32[32,8,128]{2,1,0:T(8,128)S(1)}, u32[]{:S(2)}, u32[]{:S(2)}) collective-permute-start(f32[32,8,128]{2,1,0:T(8,128)S(1)} %fusion.22), channel_id=1, source_target_pairs={{0,2},{1,3},{2,0},{3,1},{4,6},{5,7},{6,4},{7,5},{8,10},{9,11},{10,... | collective-permute-start | bytes 393224 | tf_op jit(solution)/shard_map/ppermute | solution.py:589
  138.4 1.8 %collective-permute-done.6 = f32[32,8,128]{2,1,0:T(8,128)S(1)} collective-permute-done((f32[32,8,128]{2,1,0:T(8,128)S(1)}, f32[32,8,128]{2,1,0:T(8,128)S(1)}, u32[]{:S(2)}, u32[]{:S(2)}) %collective-permute-start.6) | collective-permute-done | bytes 131104 | tf_op jit(solution)/shard_map/ppermute | solution.py:589
  140.1 1.7 %collective-permute-done.5 = f32[32,8,128]{2,1,0:T(8,128)S(1)} collective-permute-done((f32[32,8,128]{2,1,0:T(8,128)S(1)}, f32[32,8,128]{2,1,0:T(8,128)S(1)}, u32[]{:S(2)}, u32[]{:S(2)}) %collective-permute-start.5) | collective-permute-done | bytes 131104 | tf_op jit(solution)/shard_map/ppermute | solution.py:589
  141.9 1.3 collective-permute-done.4
  143.3 2.5 %collective-permute-start.7 = (f32[128,8,128]{2,1,0:T(8,128)S(1)}, f32[128,8,128]{2,1,0:T(8,128)S(1)}, u32[]{:S(2)}, u32[]{:S(2)}) collective-permute-start(f32[128,8,128]{2,1,0:T(8,128)S(1)} %pad_maximum_fusion.own_ref), channel_id=1, source_target_pairs={{0,1},{1,0},{2,3},{3,2},{4,5},{5,4},{6,7},{7,6},{8,9},{9,8},{10,11... | collective-permute-start | bytes 1572872 | tf_op jit(solution)/shard_map/ppermute | solution.py:589
  145.8 1.5 collective-permute-done.7.other_ref
  147.3 0.8 copy-done.4
  148.1 2.6 %shard_map.70 = (f32[8,256,256]{2,1,0:T(8,128)S(1)}, f32[1]{0:T(128)}) custom-call(s32[27]{0:T(128)} %copy-done, s32[16]{0:T(128)} %get-tuple-element.120.sizes, f32[128,8,128]{2,1,0:T(8,128)} %copy-done.3, f32[128,8,128]{2,1,0:T(8,128)} %copy-done.4), custom_call_target="tpu_custom_call" | custom-call | tf_op jit(solution)/shard_map/pallas_call | solution.py:443
  151.3 0.3 conditional.1
  151.6 1.3 copy-done.8
  (77 shorter events, 3.0 us)
Async XLA Ops:
  7.9 22.7 %all-to-all-start.2 = ((s32[32,4,8]{2,1,0:T(4,128)}), s32[32,4,8]{2,1,0:T(4,128)S(1)}, u32[]{:S(2)}, u32[]{:S(2)}) async-start(s32[32,4,8]{2,1,0:T(4,128)} %broadcast_in_dim.363), calls=%async_computation.2 | async-start | bytes 131072 | tf_op jit(solution)/shard_map/all_to_all | solution.py:571
  37.2 34.5 %all-to-all-start.3 = ((f32[32,64,128]{2,1,0:T(8,128)}), f32[32,64,128]{2,1,0:T(8,128)S(1)}, u32[]{:S(2)}, u32[]{:S(2)}) async-start(f32[32,64,128]{2,1,0:T(8,128)} %bitcast.98), calls=%async_computation.3 | async-start | bytes 2097152 | tf_op jit(solution)/shard_map/all_to_all | solution.py:578
  75.0 33.3 %all-to-all-start.4 = ((f32[32,64,128]{2,1,0:T(8,128)}), f32[32,64,128]{2,1,0:T(8,128)S(1)}, u32[]{:S(2)}, u32[]{:S(2)}) async-start(f32[32,64,128]{2,1,0:T(8,128)} %bitcast.51), calls=%async_computation.4 | async-start | bytes 2097152 | tf_op jit(solution)/shard_map/all_to_all | solution.py:580
  92.4 50.9 %copy-start = (s32[27]{0:T(128)}, s32[27]{0:T(128)S(1)}, u32[]{:S(2)}) copy-start(s32[27]{0:T(128)S(1)} %pad_add_fusion.5.out_tbl) | copy-start | bytes 328
  108.3 42.9 %copy-start.2 = (f32[8,256,256]{2,1,0:T(8,128)S(1)}, f32[8,256,256]{2,1,0:T(8,128)}, u32[]{:S(2)}) copy-start(f32[8,256,256]{2,1,0:T(8,128)} %psi_ref.1) | copy-start | bytes 6291460
  108.3 42.9 %copy-start.5 = (s32[8]{0:T(128)S(1)}, s32[8]{0:T(128)}, u32[]{:S(2)}) copy-start(s32[8]{0:T(128)} %param.11) | copy-start | bytes 100
  108.3 43.0 %copy-start.6 = (s32[8]{0:T(128)S(1)}, s32[8]{0:T(128)}, u32[]{:S(2)}) copy-start(s32[8]{0:T(128)} %param.12) | copy-start | bytes 100
  108.3 43.0 %copy-start.7 = (s32[2,8]{1,0:T(2,128)S(1)}, s32[2,8]{1,0:T(2,128)}, u32[]{:S(2)}) copy-start(s32[2,8]{1,0:T(2,128)} %param.13) | copy-start | bytes 196
  118.3 6.9 %collective-permute-start = (f32[128,8,128]{2,1,0:T(8,128)S(1)}, f32[128,8,128]{2,1,0:T(8,128)S(1)}, u32[]{:S(2)}, u32[]{:S(2)}) collective-permute-start(f32[128,8,128]{2,1,0:T(8,128)S(1)} %get-tuple-element.32), channel_id=1, source_target_pairs={{0,1},{1,0},{2,3},{3,2},{4,5},{5,4},{6,7},{7,6},{8,9},{9,8},{10,11... | collective-permute-start | bytes 1572872 | tf_op jit(solution)/shard_map/ppermute | solution.py:589
  125.3 4.8 %collective-permute-start.1 = (f32[32,8,128]{2,1,0:T(8,128)S(1)}, f32[32,8,128]{2,1,0:T(8,128)S(1)}, u32[]{:S(2)}, u32[]{:S(2)}) collective-permute-start(f32[32,8,128]{2,1,0:T(8,128)S(1)} %get-tuple-element.99), channel_id=1, source_target_pairs={{0,2},{1,3},{2,0},{3,1},{4,6},{5,7},{6,4},{7,5},{8,10},{9,11},{10,... | collective-permute-start | bytes 393224 | tf_op jit(solution)/shard_map/ppermute | solution.py:589
  126.0 5.6 %collective-permute-start.3 = (f32[32,8,128]{2,1,0:T(8,128)S(1)}, f32[32,8,128]{2,1,0:T(8,128)S(1)}, u32[]{:S(2)}, u32[]{:S(2)}) collective-permute-start(f32[32,8,128]{2,1,0:T(8,128)S(1)} %get-tuple-element.100), channel_id=1, source_target_pairs={{0,6},{1,7},{2,4},{3,5},{4,2},{5,3},{6,0},{7,1},{8,14},{9,15},{10,... | collective-permute-start | bytes 393224 | tf_op jit(solution)/shard_map/ppermute | solution.py:589
  127.9 7.1 %collective-permute-start.2 = (f32[32,8,128]{2,1,0:T(8,128)S(1)}, f32[32,8,128]{2,1,0:T(8,128)S(1)}, u32[]{:S(2)}, u32[]{:S(2)}) collective-permute-start(f32[32,8,128]{2,1,0:T(8,128)S(1)} %get-tuple-element.101), channel_id=1, source_target_pairs={{0,4},{1,5},{2,6},{3,7},{4,0},{5,1},{6,2},{7,3},{8,12},{9,13},{10,... | collective-permute-start | bytes 393224 | tf_op jit(solution)/shard_map/ppermute | solution.py:589
  135.0 5.1 %collective-permute-start.6 = (f32[32,8,128]{2,1,0:T(8,128)S(1)}, f32[32,8,128]{2,1,0:T(8,128)S(1)}, u32[]{:S(2)}, u32[]{:S(2)}) collective-permute-start(f32[32,8,128]{2,1,0:T(8,128)S(1)} %fusion.22), channel_id=1, source_target_pairs={{0,6},{1,7},{2,4},{3,5},{4,2},{5,3},{6,0},{7,1},{8,14},{9,15},{10,... | collective-permute-start | bytes 393224 | tf_op jit(solution)/shard_map/ppermute | solution.py:589
  136.5 5.4 %collective-permute-start.5 = (f32[32,8,128]{2,1,0:T(8,128)S(1)}, f32[32,8,128]{2,1,0:T(8,128)S(1)}, u32[]{:S(2)}, u32[]{:S(2)}) collective-permute-start(f32[32,8,128]{2,1,0:T(8,128)S(1)} %fusion.22), channel_id=1, source_target_pairs={{0,4},{1,5},{2,6},{3,7},{4,0},{5,1},{6,2},{7,3},{8,12},{9,13},{10,... | collective-permute-start | bytes 393224 | tf_op jit(solution)/shard_map/ppermute | solution.py:589
  136.5 6.8 %collective-permute-start.4 = (f32[32,8,128]{2,1,0:T(8,128)S(1)}, f32[32,8,128]{2,1,0:T(8,128)S(1)}, u32[]{:S(2)}, u32[]{:S(2)}) collective-permute-start(f32[32,8,128]{2,1,0:T(8,128)S(1)} %fusion.22), channel_id=1, source_target_pairs={{0,2},{1,3},{2,0},{3,1},{4,6},{5,7},{6,4},{7,5},{8,10},{9,11},{10,... | collective-permute-start | bytes 393224 | tf_op jit(solution)/shard_map/ppermute | solution.py:589
  143.3 4.0 %copy-start.3 = (f32[128,8,128]{2,1,0:T(8,128)}, f32[128,8,128]{2,1,0:T(8,128)S(1)}, u32[]{:S(2)}) copy-start(f32[128,8,128]{2,1,0:T(8,128)S(1)} %pad_maximum_fusion.own_ref) | copy-start | bytes 1572868
  143.3 4.0 %collective-permute-start.7 = (f32[128,8,128]{2,1,0:T(8,128)S(1)}, f32[128,8,128]{2,1,0:T(8,128)S(1)}, u32[]{:S(2)}, u32[]{:S(2)}) collective-permute-start(f32[128,8,128]{2,1,0:T(8,128)S(1)} %pad_maximum_fusion.own_ref), channel_id=1, source_target_pairs={{0,1},{1,0},{2,3},{3,2},{4,5},{5,4},{6,7},{7,6},{8,9},{9,8},{10,11... | collective-permute-start | bytes 1572872 | tf_op jit(solution)/shard_map/ppermute | solution.py:589
  147.3 0.8 copy-start.4
  151.6 1.3 copy-start.8

commit v3 on v2

--- a/solution.py
+++ b/solution.py
@@ -1,6 +1,7 @@
 import functools
 import jax
 import jax.numpy as jnp
+import numpy as np
 from jax import lax
 from jax.experimental import pallas as pl
 from jax.experimental.pallas import tpu as pltpu
@@ -18,6 +19,7 @@
 PIECE = 32
 VMEM_BYTES = 24 * 1024 * 1024
 WIDE_BYTES = 56 * 1024 * 1024
+WIDEST_BYTES = 62 * 1024 * 1024
 
 
 def sector_mask(left_sizes, right_sizes, block_size):
@@ -114,7 +116,7 @@
 
 
 def tile_rows(stream, rows):
-    return (stream % 4) * (ROWS * rows) + jnp.minimum(stream // 4, rows - 1)
+    return (stream & 3) * (ROWS * rows) + jnp.minimum(stream >> 2, rows - 1)
 
 
 def tile_at(a):
@@ -129,19 +131,21 @@
     return pl.ds(pl.multiple_of(i * LANES, LANES), LANES)
 
 
-def variants(k_blocks, n_blocks, body):
-    for k in (1, 2):
-        for n in (1, 2):
-            @pl.when((k_blocks == k) & (n_blocks == n))
-            def _():
-                body(k * LANES, n * LANES)
+def variants(m_blocks, k_blocks, n_blocks, body):
+    code = m_blocks * 4 + k_blocks * 2 + n_blocks - 7
+    for m in (1, 2):
+        for k in (1, 2):
+            for n in (1, 2):
+                @pl.when((code == m * 4 + k * 2 + n - 7) & (k_blocks > 0))
+                def _():
+                    body(m * LANES, k * LANES, n * LANES)
 
 
 S_PSI, S_PROD, S_TURN, S_RIGHT, STRIPS = 0, 2, 6, 10, 14
 TOGETHER = 2
 
 
-def carry_kernel(sizes, psi_ref, right_ref, strip_ref):
+def carry_kernel(left_sizes, right_sizes, psi_ref, right_ref, strip_ref):
     row = lax.broadcasted_iota(jnp.int32, (BLK, BLK), 0)
     col = lax.broadcasted_iota(jnp.int32, (BLK, BLK), 1)
 
@@ -151,7 +155,7 @@
 
     for i in range(TOGETHER):
         d = pl.program_id(0) * TOGETHER + i
-        kept = (row < sizes[d]) & (col < sizes[HELD + d])
+        kept = (row < left_sizes[d]) & (col < right_sizes[d])
         psi = jnp.where(kept, psi_ref[i], 0.0)
         parts = split3(psi)
         put(i, S_PSI, psi.T)
@@ -163,30 +167,32 @@
             put(i, S_TURN + 2 * t, product.T)
 
 
-def send_kernel(tbl, strip_ref, buf_ref, held_ref, sems):
-    def copy(e):
-        return pltpu.make_async_copy(strip_ref.at[tbl[3 * e]], held_ref.at[e], sems.at[e])
-
-    for e in range(4 * PAIRS):
-        @pl.when(tbl[3 * e + 1] > 0)
+def send_kernel(source, rows, first, strip_ref, buf_ref, held_ref, sems):
+    def copy(p, c):
+        e = 4 * p + c
+        return pltpu.make_async_copy(strip_ref.at[source[p, c]], held_ref.at[e], sems.at[e])
+
+    places = [(p, c) for p in range(PAIRS) for c in range(4)]
+    for p, c in places:
+        @pl.when(rows[p, c] > 0)
         def _():
-            copy(e).start()
-
-    for e in range(4 * PAIRS):
-        rows, first = tbl[3 * e + 1], tbl[3 * e + 2]
-
-        @pl.when(rows > 0)
+            copy(p, c).start()
+
+    for p, c in places:
+        @pl.when(rows[p, c] > 0)
         def _():
-            copy(e).wait()
+            copy(p, c).wait()
+            begin = first[p, c]
 
             def four(i, inner):
                 for k in range(4):
                     a = i * 4 + k
-                    at = tile_rows(first + a, ROWS_OUT)
-                    buf_ref[pl.ds(at, ROWS, stride=ROWS_OUT), :] = held_ref[e, tile_at(a), :]
+                    at = tile_rows(begin + a, ROWS_OUT)
+                    tile = held_ref[4 * p + c, tile_at(a), :]
+                    buf_ref[pl.ds(at, ROWS, stride=ROWS_OUT), :] = tile
                 return inner
 
-            lax.fori_loop(0, (rows + 3) // 4, four, 0)
+            lax.fori_loop(0, (rows[p, c] + 3) >> 2, four, 0)
 
 
 def relay_kernel(idx, count, in_ref, out_ref):
@@ -197,17 +203,18 @@
                 out_ref[pl.ds(at + k, 1), :] = in_ref[pl.ds(idx[at + k], 1), :]
             return inner
 
-        lax.fori_loop(0, (count[peer] + ROWS - 1) // ROWS, some, 0)
+        lax.fori_loop(0, (count[peer] + ROWS - 1) >> 3, some, 0)
         return carry
 
     lax.fori_loop(0, PEERS, slot, 0)
 
 
 STREAM = MEMBERS * PIECE
+SENT = PIECE + 1
 
 
 def piece_at(place, core, chip):
-    piece = ((place // 4) ^ core) * 4 + ((place % 4) ^ chip)
+    piece = ((place >> 2) ^ core) * 4 + ((place & 3) ^ chip)
     return pl.ds(pl.multiple_of(piece * PIECE, PIECE), PIECE)
 
 
@@ -221,8 +228,8 @@
         start = tbl[at + T_START] + before
         begin = []
         for k in range(4):
-            kind = (start + k) % 4
-            rank = tbl[at + T_BASE + kind] + (before + k) // 4
+            kind = (start + k) & 3
+            rank = tbl[at + T_BASE + kind] + ((before + k) >> 2)
             begin.append((kind * (ROWS * ROWS_IN), rank))
 
         def four(i, carry):
@@ -234,7 +241,7 @@
                 ]
             return carry
 
-        lax.fori_loop(0, (rows + 3) // 4, four, 0)
+        lax.fori_loop(0, (rows + 3) >> 2, four, 0)
 
     def unpack(u, carry):
         at = u * T_WIDTH
@@ -253,7 +260,7 @@
     lax.fori_loop(0, PAIRS, unpack, 0)
 
     def blocks(rows):
-        return (rows * ROWS + LANES - 1) // LANES
+        return (rows * ROWS + LANES - 1) >> 7
 
     def sector(d, carry):
         first, out_rows, strips = out_tbl[3 * d], out_tbl[3 * d + 1], out_tbl[3 * d + 2]
@@ -269,41 +276,30 @@
             kept = (row < rows[t] * ROWS) & (col < count * LANES)
             return jnp.where(kept, ref[units[t], :height, :width], 0.0)
 
-        def turned(k, n):
-            mats = [split3(masked(x_ref, t, n, k, nx[t])) for t in range(2)]
-
-            def some(i, inner):
-                for t in range(2):
-                    z_ref[t, block_at(i), :n] = dot3(
-                        split3(left_ref[units[t], block_at(i), :k]), mats[t], transposed=True
-                    )
-                return inner
-
-            lax.fori_loop(0, m_blocks, some, 0)
+        def turned(m, k, n):
+            for t in range(2):
+                z_ref[t, :m, :n] = dot3(
+                    split3(left_ref[units[t], :m, :k]),
+                    split3(masked(x_ref, t, n, k, nx[t])),
+                    transposed=True,
+                )
 
         inner_x = [jnp.where(nx[t] > 0, blocks(rows[t]), 0) for t in range(2)]
-        variants(jnp.maximum(nx[0], nx[1]), jnp.maximum(inner_x[0], inner_x[1]), turned)
-
-        def added(k, n):
-            mats = [split3(masked(y_ref, t, k, n, ny[t])) for t in range(2)]
-
-            def some(i, inner):
-                total = None
-                for t in range(2):
-                    a = jnp.where(
-                        nx[t] > 0, z_ref[t, block_at(i), :k], left_ref[units[t], block_at(i), :k]
-                    )
-                    part = dot3(split3(a), mats[t]) + jnp.where(
-                        ny[t] > 0, 0.0, z_ref[t, block_at(i), :n]
-                    )
-                    total = part if total is None else total + part
-                sum_ref[block_at(i), :n] = total
-                return inner
-
-            lax.fori_loop(0, m_blocks, some, 0)
+        variants(
+            m_blocks, jnp.maximum(nx[0], nx[1]), jnp.maximum(inner_x[0], inner_x[1]), turned
+        )
+
+        def added(m, k, n):
+            total = None
+            for t in range(2):
+                a = jnp.where(nx[t] > 0, z_ref[t, :m, :k], left_ref[units[t], :m, :k])
+                part = dot3(split3(a), split3(masked(y_ref, t, k, n, ny[t])))
+                part = part + jnp.where(ny[t] > 0, 0.0, z_ref[t, :m, :n])
+                total = part if total is None else total + part
+            sum_ref[:m, :n] = total
 
         inner_y = [jnp.where(ny[t] > 0, blocks(rows[t]), 1) for t in range(2)]
-        variants(jnp.maximum(inner_y[0], inner_y[1]), strips, added)
+        variants(m_blocks, jnp.maximum(inner_y[0], inner_y[1]), strips, added)
 
         for strip in range(2):
             @pl.when(strip < strips)
@@ -316,52 +312,57 @@
                         stream_ref[at + k] = sum_ref[tile_at(i * 4 + k), strip_at(strip)]
                     return inner
 
-                lax.fori_loop(0, (out_rows + 3) // 4, four, 0)
+                lax.fori_loop(0, (out_rows + 3) >> 2, four, 0)
         return carry
 
     lax.fori_loop(0, HELD, sector, 0)
     core, chip = out_tbl[O_CORE], out_tbl[O_CHIP]
     flag = jnp.full((ROWS, LANES), out_tbl[O_FLAG], jnp.int32).astype(jnp.float32)
-    stream_ref[STREAM - 1] = flag
     for place in range(4):
-        into = pl.ds(place * PIECE, PIECE)
+        into = pl.ds(place * SENT, PIECE)
         keep_ref[into] = stream_ref[piece_at(place, core, chip)]
         send_ref[into] = stream_ref[piece_at(place + 4, core, chip)]
-
-
-def spread_kernel(out_tbl, sizes, own_ref, other_ref, out_ref, flag_ref, stream_ref):
-    d = pl.program_id(0)
-
-    @pl.when(d == 0)
-    def _():
-        core, chip = out_tbl[O_CORE], out_tbl[O_CHIP]
-        for place in range(4):
-            part = pl.ds(place * PIECE, PIECE)
-            stream_ref[piece_at(place, core, chip)] = own_ref[part]
-            stream_ref[piece_at(place + 4, core, chip)] = other_ref[part]
-        flag_ref[0] = jnp.max(stream_ref[STREAM - 1])
+        keep_ref[place * SENT + PIECE] = flag
+        send_ref[place * SENT + PIECE] = flag
+
+
+def spread_kernel(
+    out_tbl, left_sizes, right_sizes, own_ref, other_ref, out_ref, stream_ref, block_ref, sems
+):
+    core, chip = out_tbl[O_CORE], out_tbl[O_CHIP]
+    for place in range(4):
+        part = pl.ds(place * SENT, PIECE)
+        stream_ref[piece_at(place, core, chip)] = own_ref[part]
+        stream_ref[piece_at(place + 4, core, chip)] = other_ref[part]
 
     row = lax.broadcasted_iota(jnp.int32, (ROWS, LANES), 0)
     col = lax.broadcasted_iota(jnp.int32, (ROWS, LANES), 1)
-    out_ref[...] = jnp.zeros_like(out_ref)
-    first, rows, strips = out_tbl[3 * d], out_tbl[3 * d + 1], out_tbl[3 * d + 2]
-    height, width = sizes[d], sizes[HELD + d]
-    for strip in range(2):
-        @pl.when(strip < strips)
-        def _():
-            begin = first + strip * rows
-            col_ok = col + strip * LANES < width
-
-            def four(i, inner):
-                at = jnp.minimum(begin + i * 4, STREAM)
-                for k in range(4):
-                    a = i * 4 + k
-                    kept = col_ok & (row + a * ROWS < height)
-                    tile = jnp.where(kept, stream_ref[at + k], 0.0)
-                    out_ref[0, tile_at(a), strip_at(strip)] = tile
-                return inner
-
-            lax.fori_loop(0, (rows + 3) // 4, four, 0)
+    copies = []
+    for d in range(HELD):
+        block_ref[d] = jnp.zeros((BLK, BLK), jnp.float32)
+        first, rows, strips = out_tbl[3 * d], out_tbl[3 * d + 1], out_tbl[3 * d + 2]
+        height, width = left_sizes[d], right_sizes[d]
+        for strip in range(2):
+            @pl.when(strip < strips)
+            def _():
+                begin = first + strip * rows
+                col_ok = col + strip * LANES < width
+
+                def four(i, inner):
+                    at = jnp.minimum(begin + i * 4, STREAM)
+                    for k in range(4):
+                        a = i * 4 + k
+                        kept = col_ok & (row + a * ROWS < height)
+                        tile = jnp.where(kept, stream_ref[at + k], 0.0)
+                        block_ref[d, tile_at(a), strip_at(strip)] = tile
+                    return inner
+
+                lax.fori_loop(0, (rows + 3) >> 2, four, 0)
+
+        copies.append(pltpu.make_async_copy(block_ref.at[d], out_ref.at[d], sems.at[d]))
+        copies[-1].start()
+    for copy in copies:
+        copy.wait()
 
 
 O_CORE, O_CHIP, O_FLAG = 3 * HELD, 3 * HELD + 1, 3 * HELD + 2
@@ -369,6 +370,7 @@
 SMEM = pl.BlockSpec(memory_space=pltpu.SMEM)
 VMEM = pl.BlockSpec(memory_space=pltpu.VMEM)
 PARAMS = pltpu.CompilerParams(vmem_limit_bytes=VMEM_BYTES)
+WIDEST = pltpu.CompilerParams(vmem_limit_bytes=WIDEST_BYTES)
 WIDE = pltpu.CompilerParams(vmem_limit_bytes=WIDE_BYTES)
 
 
@@ -380,12 +382,13 @@
     return pltpu.VMEM(shape, jnp.float32)
 
 
-def carry_call(sizes, psi, right):
+def carry_call(left_sizes, right_sizes, psi, right):
     return pl.pallas_call(
         carry_kernel,
         grid=(HELD // TOGETHER,),
         out_shape=floats(HELD, STRIPS, BLK, LANES),
         in_specs=[
+            SMEM,
             SMEM,
             pl.BlockSpec((TOGETHER, BLK, BLK), lambda d: (d, 0, 0)),
             pl.BlockSpec((PAIRS // HELD, TOGETHER, BLK, BLK), lambda d: (0, d, 0, 0)),
@@ -395,21 +398,21 @@
             flops=6 * PAIRS * BLK**3, bytes_accessed=24 * 2**20, transcendentals=0
         ),
         compiler_params=WIDE,
-    )(sizes, psi, right)
-
-
-def send_call(tbl, strips):
+    )(left_sizes, right_sizes, psi, right)
+
+
+def send_call(tables, strips):
     return pl.pallas_call(
         send_kernel,
         out_shape=floats(PEERS * ROWS_OUT, LANES),
-        in_specs=[SMEM, pl.BlockSpec(memory_space=pl.ANY)],
+        in_specs=[SMEM, SMEM, SMEM, pl.BlockSpec(memory_space=pl.ANY)],
         out_specs=VMEM,
         scratch_shapes=[
             scratch(4 * PAIRS, BLK, LANES),
             pltpu.SemaphoreType.DMA((4 * PAIRS,)),
         ],
         compiler_params=WIDE,
-    )(tbl, strips)
+    )(*tables, strips)
 
 
 def relay_call(idx, count, received):
@@ -425,7 +428,7 @@
 def land_call(tbl, out_tbl, received, left):
     return pl.pallas_call(
         land_kernel,
-        out_shape=[floats(4 * PIECE, ROWS, LANES)] * 2,
+        out_shape=[floats(4 * SENT, ROWS, LANES)] * 2,
         in_specs=[SMEM, SMEM, VMEM, VMEM],
         out_specs=[VMEM, VMEM],
         scratch_shapes=[
@@ -439,26 +442,29 @@
     )(tbl, out_tbl, received, left)
 
 
-def spread_call(out_tbl, sizes, own, other):
+def spread_call(out_tbl, left_sizes, right_sizes, own, other):
     return pl.pallas_call(
         spread_kernel,
-        grid=(HELD,),
-        out_shape=[floats(HELD, BLK, BLK), floats(1)],
-        in_specs=[SMEM, SMEM, VMEM, VMEM],
-        out_specs=[pl.BlockSpec((1, BLK, BLK), lambda d: (d, 0, 0)), SMEM],
-        scratch_shapes=[scratch(STREAM + ROWS, ROWS, LANES)],
-        compiler_params=WIDE,
-    )(out_tbl, sizes, own, other)
+        out_shape=floats(HELD, BLK, BLK),
+        in_specs=[SMEM, SMEM, SMEM, VMEM, VMEM],
+        out_specs=pl.BlockSpec(memory_space=pl.ANY),
+        scratch_shapes=[
+            scratch(STREAM + ROWS, ROWS, LANES),
+            scratch(HELD, BLK, BLK),
+            pltpu.SemaphoreType.DMA((HELD,)),
+        ],
+        compiler_params=WIDEST,
+    )(out_tbl, left_sizes, right_sizes, own, other)
 
 
 def up(value, unit):
-    return (value + (unit - 1)) // unit
+    return (value + (unit - 1)) >> (unit.bit_length() - 1)
 
 
 def before(values, axis):
     n = values.shape[axis]
     moved = jnp.moveaxis(values, axis, -1)
-    lower = jnp.arange(n)[:, None] > jnp.arange(n)[None, :]
+    lower = np.arange(n)[:, None] > np.arange(n)[None, :]
     total = jnp.sum(jnp.where(lower, moved[..., None, :], 0), axis=-1)
     return jnp.moveaxis(total, -1, axis)
 
@@ -469,9 +475,9 @@
 
     ls = jnp.concatenate([size_l, size_l], axis=1)
     rs = jnp.concatenate([size_r, size_r], axis=1)
-    to_dev = dest // HELD
-    hit_dev = to_dev[:, :, None] == jnp.arange(PEERS)[None, None, :]
-    sector = jnp.arange(PEERS * HELD)[:, None]
+    to_dev = dest >> 3
+    hit_dev = to_dev[:, :, None] == np.arange(PEERS, dtype=np.int32)[None, None, :]
+    sector = np.arange(PEERS * HELD, dtype=np.int32)[:, None]
     rd = jnp.sum(
         jnp.where(dest.reshape(1, -1) == sector, size_r.reshape(-1)[:, None], 0), axis=0
     ).reshape(PEERS, PAIRS)
@@ -488,10 +494,10 @@
     start = before(tiles, 1)
     total = jnp.sum(tiles, axis=1)
 
-    kinds = jnp.arange(4)[:, None, None]
-    lag = (kinds - start) % 4
-    share = (tiles + 3 - lag) // 4
-    first_row = (start + lag) // 4
+    kinds = np.arange(4, dtype=np.int32)[:, None, None]
+    lag = (kinds - start) & 3
+    share = (tiles + 3 - lag) >> 2
+    first_row = (start + lag) >> 2
     onto = jnp.sum(jnp.where(hit_dev[None], share[..., None], 0), axis=2)
     base = before(onto, 1)
     filled = jnp.sum(onto, axis=1)
@@ -502,13 +508,14 @@
     spilled = (
         jnp.any(total > 4 * (ROWS_OUT - 1))
         | jnp.any(filled > ROWS_IN)
-        | jnp.any(jnp.sum(out_tiles, axis=1) > MEMBERS * PIECE - 1)
+        | jnp.any(jnp.sum(out_tiles, axis=1) > MEMBERS * PIECE)
     )
 
     def own(values, axis=0):
         return lax.dynamic_index_in_dim(values, me, axis, keepdims=False)
 
-    pair, place = jnp.arange(PAIRS)[:, None], jnp.arange(4)[None, :]
+    pair = np.arange(PAIRS, dtype=np.int32)[:, None]
+    place = np.arange(4, dtype=np.int32)[None, :]
     own_nx, own_ny, own_rows = own(nx)[:, None], own(ny)[:, None], own(rows)[:, None]
     both = (own_nx > 0) & (own_ny > 0)
     term, held = pair // HELD, pair % HELD
@@ -520,26 +527,28 @@
     source = held * STRIPS + source + place % 2
     used = jnp.where(place < 2, place < own_nx, place - 2 < own_ny)
     index = jnp.where(place < 2, place, own_nx + place - 2)
-    send_tbl = jnp.stack(
-        [source, jnp.where(used, own_rows, 0), own(start)[:, None] + index * own_rows], axis=2
-    ).reshape(-1)
-
-    kind = me // ROWS
+    send_tbl = (
+        source,
+        jnp.where(used, own_rows, 0),
+        own(start)[:, None] + index * own_rows,
+    )
+
+    kind = me >> 3
     onto_k = lax.dynamic_index_in_dim(onto, kind, 0, keepdims=False)
     base_k = lax.dynamic_index_in_dim(base, kind, 0, keepdims=False)
     first_k = lax.dynamic_index_in_dim(first_row, kind, 0, keepdims=False)
     filled_k = lax.dynamic_index_in_dim(filled, kind, 0, keepdims=False)
     first_to = jnp.sum(jnp.where(hit_dev, first_k[:, :, None], 0), axis=1)
-    rank = jnp.arange(ROWS_IN)[None, None, :]
+    rank = np.arange(ROWS_IN, dtype=np.int32)[None, None, :]
     here = (rank >= base_k[:, :, None]) & (rank < (base_k + onto_k)[:, :, None])
-    origin = jnp.arange(PEERS)[:, None] * ROWS_OUT + first_to - base_k
+    origin = np.arange(PEERS, dtype=np.int32)[:, None] * ROWS_OUT + first_to - base_k
     relay_idx = jnp.sum(jnp.where(here, origin[:, :, None] + rank, 0), axis=0)
     relay_idx = jnp.clip(relay_idx, 0, PEERS * ROWS_OUT - 1).reshape(-1)
     relay_count = jnp.minimum(filled_k, ROWS_IN)
 
-    unit = jnp.arange(PAIRS)[:, None, None]
+    unit = np.arange(PAIRS, dtype=np.int32)[:, None, None]
     reach = (dest[None] == me * HELD + unit % HELD) & (
-        (jnp.arange(PAIRS) // HELD)[None, None, :] == unit // HELD
+        (np.arange(PAIRS, dtype=np.int32) // HELD)[None, None, :] == unit // HELD
     )
 
     def reached(values):
@@ -564,13 +573,12 @@
 def per_device(psi_blocks, left_env, right_env, left_sizes, right_sizes, dest_sector):
     me = lax.axis_index("sec")
     member = lax.axis_index("term")
-    core, chip = member % 2, member // 2
-    sizes = jnp.concatenate([left_sizes, right_sizes])
-    strips = carry_call(sizes, psi_blocks, right_env).reshape(HELD * STRIPS, BLK, LANES)
+    core, chip = member & 1, member >> 1
+    strips = carry_call(left_sizes, right_sizes, psi_blocks, right_env)
+    strips = strips.reshape(HELD * STRIPS, BLK, LANES)
     mine = jnp.concatenate([left_sizes[None], right_sizes[None], dest_sector])
-    facts = lax.all_to_all(
-        jnp.broadcast_to(mine[None], (PEERS, 4, HELD)), "sec", 0, 0, tiled=True
-    )
+    mine = jnp.broadcast_to(mine[None], (PEERS, 4, HELD))
+    facts = lax.all_to_all(mine, "sec", 0, 0, tiled=True)
     tables = make_tables(facts, me, core, chip)
     send_tbl, relay_idx, relay_count, land_tbl, out_tbl = tables
 
@@ -588,18 +596,17 @@
     def swap(values, bits):
         return lax.ppermute(values, "term", [(i, i ^ bits) for i in range(MEMBERS)])
 
-    half = (keep + swap(give, 1)).reshape(4, PIECE, ROWS, LANES)
+    half = (keep + swap(give, 1)).reshape(4, SENT, ROWS, LANES)
     piece = half[0] + swap(half[1], 2) + swap(half[2], 4) + swap(half[3], 6)
     whole = jnp.concatenate([piece, swap(piece, 2), swap(piece, 4), swap(piece, 6)])
     other = swap(whole, 1)
 
-    packed, flag = spread_call(out_tbl, sizes, whole, other)
     return lax.cond(
-        flag[0] > 0.5,
+        piece[PIECE, 0, 0] > 0.5,
         lambda: dense_program(
             psi_blocks, left_env, right_env, left_sizes, right_sizes, dest_sector
         ),
-        lambda: packed,
+        lambda: spread_call(out_tbl, left_sizes, right_sizes, whole, other),
     )
 
 

time: 161 us -> 155 us (0.963); the launches traced: 160 us -> 156 us
  local copies, waits for them, and re-layouts: 5.95 us -> 3.81 us
    unnamed x17 -> x31, local copies, waits for them, and re-layouts: 2.2 us -> 0.28 us
  transfers between devices with their start and end apart: 11 -> 11, of which waited for: 10 -> 10; matrix products, arithmetic and copies ran while one was open for 8% -> 7% of each run, Pallas kernels for 6% -> 6%
where the time goes in v3:
time: 155 us; the launch traced here: 156 us
  waiting for transfers between devices  49.8 us (32%)
  starting transfers between devices  45.6 us (29%)
  Pallas kernels  28.7 us (19%)
  between operations  16.4 us (11%)
  other arithmetic  11 us (7%)
  local copies, waits for them, and re-layouts  3.81 us (2%)
    all_to_all x1, waiting for transfers between devices, per_device(): lax.all_to_all(sent.reshape(PEERS, ROWS_OUT, LANES), 'sec', 0, 0, tiled=T...  20.4 us
    all_to_all x1, waiting for transfers between devices, per_device(): lax.all_to_all(passed.reshape(PEERS, ROWS_IN, LANES), 'sec', 0, 0, tiled=...  16.4 us
    ppermute x8, starting transfers between devices, swap(): return lax.ppermute(values, 'term', [(i, i ^ bits) for i in range(MEMBERS)])  15.8 us
    ppermute x8, waiting for transfers between devices, swap(): return lax.ppermute(values, 'term', [(i, i ^ bits) for i in range(MEMBERS)])  13 us
    all_to_all x1, starting transfers between devices, per_device(): facts = lax.all_to_all(mine, 'sec', 0, 0, tiled=True)  11.9 us
    pallas_call x1, Pallas kernels, carry_call(): pl.pallas_call(carry_kernel, grid=(HELD // TOGETHER,), out_shape=floats(H...  9.42 us
    pallas_call x1, Pallas kernels, land_call(): pl.pallas_call(land_kernel, out_shape=[floats(4 * SENT, ROWS, LANES)] * 2...  9.25 us
    all_to_all x1, starting transfers between devices, per_device(): lax.all_to_all(sent.reshape(PEERS, ROWS_OUT, LANES), 'sec', 0, 0, tiled=T...  9.23 us
  transfers between devices with their start and end apart: 11, of which 10 were waited for; matrix products, arithmetic and copies ran while one was open for 7% of the time, Pallas kernels for 6%

profile of v3, /device:TPU:1, one launch (start us, length us, event | category | flops | bytes accessed | tf_op | source)
XLA Modules:
  0.0 155.5 jit_solution(5862474573973351835)
XLA Ops:
  6.5 0.7 pad_add_fusion.2
  7.2 0.6 broadcast_in_dim.357
  7.9 11.9 %all-to-all-start.2 = ((s32[32,4,8]{2,1,0:T(4,128)}), s32[32,4,8]{2,1,0:T(4,128)S(1)}, u32[]{:S(2)}, u32[]{:S(2)}) async-start(s32[32,4,8]{2,1,0:T(4,128)} %broadcast_in_dim.357), calls=%async_computation.2 | async-start | bytes 131072 | tf_op jit(solution)/shard_map/all_to_all | solution.py:581
  19.8 9.4 %shard_map.240 = f32[8,14,256,128]{3,2,1,0:T(8,128)} custom-call(s32[8]{0:T(128)} %left_sizes.1, s32[8]{0:T(128)} %right_sizes.1, f32[8,256,256]{2,1,0:T(8,128)} %psi_ref.1, f32[2,8,256,256]{3,2,1,0:T(8,128)} %right_ref.1), custom_call_target="tpu_custom_call" | custom-call | flops 1610612736 | bytes 25165824 | tf_op jit(solution)/shard_map/pallas_call | solution.py:386
  29.3 0.1 eq.113
  29.8 0.1 select_reduce_fusion.5
  30.1 0.1 select_reduce_fusion.17
  30.3 0.2 dynamic-slice_reduce_fusion
  30.6 0.2 dynamic-slice_reduce_fusion.2
  30.8 0.2 select_reduce_fusion.19
  31.1 0.7 fusion.30
  31.8 4.8 %shard_map.241 = f32[2048,128]{1,0:T(8,128)} custom-call(s32[16,4]{1,0:T(8,128)} %get-tuple-element.138.source, s32[16,4]{1,0:T(8,128)} %get-tuple-element.137.rows, s32[16,4]{1,0:T(8,128)} %get-tuple-element.136.first, f32[112,256,128]{2,1,0:T(8,128)} %bitcast.88), custom_call_target="tpu_custom_call" | custom-call | tf_op jit(solution)/shard_map/pallas_call | solution.py:405
  36.6 9.2 %all-to-all-start.3 = ((f32[32,64,128]{2,1,0:T(8,128)}), f32[32,64,128]{2,1,0:T(8,128)S(1)}, u32[]{:S(2)}, u32[]{:S(2)}) async-start(f32[32,64,128]{2,1,0:T(8,128)} %bitcast.92), calls=%async_computation.3 | async-start | bytes 2097152 | tf_op jit(solution)/shard_map/all_to_all | solution.py:586
  46.0 0.2 select_reduce_fusion.6
  46.3 0.1 iota_compare_fusion.9
  46.4 0.4 select_reduce_fusion.3
  47.0 2.2 %select_reduce_fusion.2 = s32[4,32,32]{2,1,0:T(8,128)S(1)} fusion(s32[4,32,32]{2,1,0:T(8,128)S(1)} %copy.202, pred[32,32]{1,0:T(8,128)(4,1)S(1)} %bitcast.102), kind=kLoop, calls=%fused_computation.53 | loop fusion | flops 258048 | bytes 33792 | tf_op jit(solution)/shard_map/reduce_sum | solution.py:468
  49.5 0.6 fusion.21
  50.2 20.4 %all-to-all-done.3 = f32[32,64,128]{2,1,0:T(8,128)S(1)} async-done(((f32[32,64,128]{2,1,0:T(8,128)}), f32[32,64,128]{2,1,0:T(8,128)S(1)}, u32[]{:S(2)}, u32[]{:S(2)}) %all-to-all-start.3) | async-done | bytes 1048608 | tf_op jit(solution)/shard_map/all_to_all | solution.py:586
  70.6 3.0 %shard_map.242 = f32[2048,128]{1,0:T(8,128)} custom-call(s32[2048]{0:T(1024)S(1)} %min.20.idx, s32[32]{0:T(128)S(1)} %fusion.39.count, f32[2048,128]{1,0:T(8,128)S(1)} %bitcast.86), custom_call_target="tpu_custom_call" | custom-call | tf_op jit(solution)/shard_map/pallas_call | solution.py:419
  73.6 8.7 %all-to-all-start.4 = ((f32[32,64,128]{2,1,0:T(8,128)}), f32[32,64,128]{2,1,0:T(8,128)S(1)}, u32[]{:S(2)}, u32[]{:S(2)}) async-start(f32[32,64,128]{2,1,0:T(8,128)} %bitcast.47), calls=%async_computation.4 | async-start | bytes 2097152 | tf_op jit(solution)/shard_map/all_to_all | solution.py:588
  82.4 0.2 dynamic-slice_reduce_fusion.6
  82.6 0.2 dynamic-slice_reduce_fusion.4
  83.0 0.7 compare_reduce_fusion.2
  83.7 0.7 compare_reduce_fusion.1
  85.7 0.7 compare_reduce_fusion
  87.0 3.1 %select_reduce_fusion.7 = (s32[16]{0:T(128)S(1)}, s32[16]{0:T(128)S(1)}, s32[16]{0:T(128)S(1)}, s32[16]{0:T(128)S(1)}, s32[16]{0:T(128)S(1)}, /*index=5*/s32[16]...) fusion(s32[32]{0:T(128)S(1)} %get-tuple-element.122, s32[32,16]{0,1:T(8,128)S(1)} %bitcast.98, ...), kind=kLoop, calls=%fused_computation.70 | loop fusion | flops 180064 | bytes 15808 | tf_op jit(solution)/shard_map/reduce_sum | solution.py:555
  90.3 0.1 reshape.770.tbl
  90.4 16.4 %all-to-all-done.4 = f32[32,64,128]{2,1,0:T(8,128)S(1)} async-done(((f32[32,64,128]{2,1,0:T(8,128)}), f32[32,64,128]{2,1,0:T(8,128)S(1)}, u32[]{:S(2)}, u32[]{:S(2)}) %all-to-all-start.4) | async-done | bytes 1048608 | tf_op jit(solution)/shard_map/all_to_all | solution.py:588
  106.8 9.3 %shard_map.243 = (f32[132,8,128]{2,1,0:T(8,128)S(1)}, f32[132,8,128]{2,1,0:T(8,128)S(1)}) custom-call(s32[160]{0:T(256)S(1)} %reshape.770.tbl, s32[27]{0:T(128)S(1)} %pad_add_fusion.4.out_tbl, f32[2048,128]{1,0:T(8,128)S(1)} %bitcast.87, f32[16,256,256]{2,1,0:T(8,128)} %bitcast.90), custom_call_target="tpu_custom_call" | custom-call | tf_op jit(solution)/shard_map/pallas_call | solution.py:429
  116.1 5.9 %collective-permute-start = (f32[132,8,128]{2,1,0:T(8,128)S(1)}, f32[132,8,128]{2,1,0:T(8,128)S(1)}, u32[]{:S(2)}, u32[]{:S(2)}) collective-permute-start(f32[132,8,128]{2,1,0:T(8,128)S(1)} %get-tuple-element.44), channel_id=1, source_target_pairs={{0,1},{1,0},{2,3},{3,2},{4,5},{5,4},{6,7},{7,6},{8,9},{9,8},{10,11... | collective-permute-start | bytes 1622024 | tf_op jit(solution)/shard_map/ppermute | solution.py:597
  122.0 1.6 %collective-permute-done = f32[132,8,128]{2,1,0:T(8,128)S(1)} collective-permute-done((f32[132,8,128]{2,1,0:T(8,128)S(1)}, f32[132,8,128]{2,1,0:T(8,128)S(1)}, u32[]{:S(2)}, u32[]{:S(2)}) %collective-permute-start) | collective-permute-done | bytes 540704 | tf_op jit(solution)/shard_map/ppermute | solution.py:597
  123.6 1.4 collective-permute-start.1
  125.0 1.3 collective-permute-start.3
  126.3 1.1 collective-permute-start.2
  127.4 1.1 collective-permute-done.1
  128.5 2.2 %collective-permute-done.3 = f32[33,8,128]{2,1,0:T(8,128)S(1)} collective-permute-done((f32[33,8,128]{2,1,0:T(8,128)S(1)}, f32[33,8,128]{2,1,0:T(8,128)S(1)}, u32[]{:S(2)}, u32[]{:S(2)}) %collective-permute-start.3) | collective-permute-done | bytes 135200 | tf_op jit(solution)/shard_map/ppermute | solution.py:597
  130.7 3.0 %collective-permute-done.2 = f32[33,8,128]{2,1,0:T(8,128)S(1)} collective-permute-done((f32[33,8,128]{2,1,0:T(8,128)S(1)}, f32[33,8,128]{2,1,0:T(8,128)S(1)}, u32[]{:S(2)}, u32[]{:S(2)}) %collective-permute-start.2) | collective-permute-done | bytes 135200 | tf_op jit(solution)/shard_map/ppermute | solution.py:597
  133.7 1.6 %collective-permute-start.6 = (f32[33,8,128]{2,1,0:T(8,128)S(1)}, f32[33,8,128]{2,1,0:T(8,128)S(1)}, u32[]{:S(2)}, u32[]{:S(2)}) collective-permute-start(f32[33,8,128]{2,1,0:T(8,128)S(1)} %fusion.24), channel_id=1, source_target_pairs={{0,6},{1,7},{2,4},{3,5},{4,2},{5,3},{6,0},{7,1},{8,14},{9,15},{10,... | collective-permute-start | bytes 405512 | tf_op jit(solution)/shard_map/ppermute | solution.py:597
  135.4 1.7 %collective-permute-start.4 = (f32[33,8,128]{2,1,0:T(8,128)S(1)}, f32[33,8,128]{2,1,0:T(8,128)S(1)}, u32[]{:S(2)}, u32[]{:S(2)}) collective-permute-start(f32[33,8,128]{2,1,0:T(8,128)S(1)} %fusion.24), channel_id=1, source_target_pairs={{0,2},{1,3},{2,0},{3,1},{4,6},{5,7},{6,4},{7,5},{8,10},{9,11},{10,... | collective-permute-start | bytes 405512 | tf_op jit(solution)/shard_map/ppermute | solution.py:597
  137.1 1.8 %collective-permute-done.6 = f32[33,8,128]{2,1,0:T(8,128)S(1)} collective-permute-done((f32[33,8,128]{2,1,0:T(8,128)S(1)}, f32[33,8,128]{2,1,0:T(8,128)S(1)}, u32[]{:S(2)}, u32[]{:S(2)}) %collective-permute-start.6) | collective-permute-done | bytes 135200 | tf_op jit(solution)/shard_map/ppermute | solution.py:597
  138.9 2.0 %collective-permute-done.5 = f32[33,8,128]{2,1,0:T(8,128)S(1)} collective-permute-done((f32[33,8,128]{2,1,0:T(8,128)S(1)}, f32[33,8,128]{2,1,0:T(8,128)S(1)}, u32[]{:S(2)}, u32[]{:S(2)}) %collective-permute-start.5) | collective-permute-done | bytes 135200 | tf_op jit(solution)/shard_map/ppermute | solution.py:597
  140.8 1.0 collective-permute-done.4
  141.8 2.8 %collective-permute-start.7 = (f32[132,8,128]{2,1,0:T(8,128)S(1)}, f32[132,8,128]{2,1,0:T(8,128)S(1)}, u32[]{:S(2)}, u32[]{:S(2)}) collective-permute-start(f32[132,8,128]{2,1,0:T(8,128)S(1)} %pad_maximum_fusion), channel_id=1, source_target_pairs={{0,1},{1,0},{2,3},{3,2},{4,5},{5,4},{6,7},{7,6},{8,9},{9,8},{10,11... | collective-permute-start | bytes 1622024 | tf_op jit(solution)/shard_map/ppermute | solution.py:597
  144.6 0.5 slice.77
  145.8 0.4 collective-permute-done.7
  146.2 2.5 %conditional.1 = (f32[8,256,256]{2,1,0:T(8,128)}) conditional(s32[]{:T(128)} %bitcast.50, (s32[27]{0:T(128)S(1)}, s32[8]{0:T(128)S(1)}, s32[8]{0:T(128)S(1)}, f32[132,8,128]{2,1,0:T(8,128)S(1)}, f32[132,8,128]{2,1,0:T(8,128)S(1)}) %tuple.71, (s32[8]{0:T(128)S(1)}, s32[8]{0:T(128)S(1)}, s32[2,8]{1,0:T(2,128)S(1)}, f32[2,8,256,256]{3,2,1,0:T(8,128)}, ...), branch_computations={%region_23.24_spmd, %region_24.31_spmd} | conditional | flops 6547847168 | bytes 155251904 | solution.py:604
  146.2 2.2 %branch_0_fun.1 = f32[8,256,256]{2,1,0:T(8,128)} custom-call(s32[27]{0:T(128)S(1)} %get-tuple-element.30.out_tbl, s32[8]{0:T(128)S(1)} %get-tuple-element.31.left_sizes, s32[8]{0:T(128)S(1)} %get-tuple-element.32.right_sizes, f32[132,8,128]{2,1,0:T(8,128)S(1)} %get-tuple-element.33.own_ref, f32[132,8,128]{2,1,0:T(8,128)S(1)} %get-tuple-element.34.other_ref), custom_call_target="tpu_custom_call" | custom-call | tf_op jit(solution)/shard_map/cond/branch_0_fun/pallas_call | solution.py:446
  (75 shorter events, 2.2 us)
Async XLA Ops:
  7.9 21.4 %all-to-all-start.2 = ((s32[32,4,8]{2,1,0:T(4,128)}), s32[32,4,8]{2,1,0:T(4,128)S(1)}, u32[]{:S(2)}, u32[]{:S(2)}) async-start(s32[32,4,8]{2,1,0:T(4,128)} %broadcast_in_dim.357), calls=%async_computation.2 | async-start | bytes 131072 | tf_op jit(solution)/shard_map/all_to_all | solution.py:581
  19.8 10.4 %copy-start.7 = (pred[16,16]{1,0:T(8,128)(4,1)S(1)}, pred[16,16]{1,0:T(8,128)(4,1)}, u32[]{:S(2)}) copy-start(pred[16,16]{1,0:T(8,128)(4,1)} %constant.177.clone) | copy-start | bytes 772
  19.8 11.0 %copy-start.3 = (s32[1,16]{0,1:T(8,128)S(1)}, s32[1,16]{0,1:T(8,128)}, u32[]{:S(2)}) copy-start(s32[1,16]{0,1:T(8,128)} %constant.211) | copy-start | bytes 196
  19.8 11.0 %copy-start.4 = (s32[1,16]{0,1:T(8,128)S(1)}, s32[1,16]{0,1:T(8,128)}, u32[]{:S(2)}) copy-start(s32[1,16]{0,1:T(8,128)} %constant.210) | copy-start | bytes 196
  19.8 11.2 %copy-start.10 = (s32[4]{0:T(128)S(1)}, s32[4]{0:T(128)}, u32[]{:S(2)}) copy-start(s32[4]{0:T(128)} %constant.208) | copy-start | bytes 52
  19.8 11.2 %copy-start.11 = (s32[4]{0:T(128)S(1)}, s32[4]{0:T(128)}, u32[]{:S(2)}) copy-start(s32[4]{0:T(128)} %constant.206) | copy-start | bytes 52
  19.8 11.2 %copy-start.12 = (pred[4]{0:T(512)(128)(4,1)S(1)}, pred[4]{0:T(512)(128)(4,1)}, u32[]{:S(2)}) copy-start(pred[4]{0:T(512)(128)(4,1)} %constant.205) | copy-start | bytes 16
  19.8 11.2 %copy-start.13 = (s32[16]{0:T(128)S(1)}, s32[16]{0:T(128)}, u32[]{:S(2)}) copy-start(s32[16]{0:T(128)} %constant.204) | copy-start | bytes 196
  31.8 15.3 %copy-start.5 = (pred[32,32]{1,0:T(32,128)(4,1)S(1)}, pred[32,32]{1,0:T(32,128)(4,1)}, u32[]{:S(2)}) copy-start(pred[32,32]{1,0:T(32,128)(4,1)} %constant.179.clone) | copy-start | bytes 3076
  36.6 45.7 %copy-start.14 = (s32[16,1,1]{0,2,1:T(1,128)S(1)}, s32[16,1,1]{0,2,1:T(1,128)}, u32[]{:S(2)}) copy-start(s32[16,1,1]{0,2,1:T(1,128)} %constant.190.clone) | copy-start | bytes 196
  36.6 45.7 %copy-start.8 = (pred[8,8]{1,0:T(8,128)(4,1)S(1)}, pred[8,8]{1,0:T(8,128)(4,1)}, u32[]{:S(2)}) copy-start(pred[8,8]{1,0:T(8,128)(4,1)} %constant.180.clone) | copy-start | bytes 196
  36.6 50.4 %copy-start.6 = (pred[16,16]{1,0:T(8,128)(4,1)S(1)}, pred[16,16]{1,0:T(8,128)(4,1)}, u32[]{:S(2)}) copy-start(pred[16,16]{1,0:T(8,128)(4,1)} %constant.198) | copy-start | bytes 772
  36.6 34.0 %all-to-all-start.3 = ((f32[32,64,128]{2,1,0:T(8,128)}), f32[32,64,128]{2,1,0:T(8,128)S(1)}, u32[]{:S(2)}, u32[]{:S(2)}) async-start(f32[32,64,128]{2,1,0:T(8,128)} %bitcast.92), calls=%async_computation.3 | async-start | bytes 2097152 | tf_op jit(solution)/shard_map/all_to_all | solution.py:586
  73.6 33.2 %all-to-all-start.4 = ((f32[32,64,128]{2,1,0:T(8,128)}), f32[32,64,128]{2,1,0:T(8,128)S(1)}, u32[]{:S(2)}, u32[]{:S(2)}) async-start(f32[32,64,128]{2,1,0:T(8,128)} %bitcast.47), calls=%async_computation.4 | async-start | bytes 2097152 | tf_op jit(solution)/shard_map/all_to_all | solution.py:588
  106.8 39.4 %copy-start.1 = (s32[8]{0:T(128)S(1)}, s32[8]{0:T(128)}, u32[]{:S(2)}) copy-start(s32[8]{0:T(128)} %left_sizes.1) | copy-start | bytes 100
  106.8 39.4 %copy-start.2 = (s32[8]{0:T(128)S(1)}, s32[8]{0:T(128)}, u32[]{:S(2)}) copy-start(s32[8]{0:T(128)} %right_sizes.1) | copy-start | bytes 100
  106.8 39.4 %copy-start.9 = (s32[2,8]{1,0:T(2,128)S(1)}, s32[2,8]{1,0:T(2,128)}, u32[]{:S(2)}) copy-start(s32[2,8]{1,0:T(2,128)} %param.32) | copy-start | bytes 196
  116.1 7.5 %collective-permute-start = (f32[132,8,128]{2,1,0:T(8,128)S(1)}, f32[132,8,128]{2,1,0:T(8,128)S(1)}, u32[]{:S(2)}, u32[]{:S(2)}) collective-permute-start(f32[132,8,128]{2,1,0:T(8,128)S(1)} %get-tuple-element.44), channel_id=1, source_target_pairs={{0,1},{1,0},{2,3},{3,2},{4,5},{5,4},{6,7},{7,6},{8,9},{9,8},{10,11... | collective-permute-start | bytes 1622024 | tf_op jit(solution)/shard_map/ppermute | solution.py:597
  123.6 4.9 %collective-permute-start.1 = (f32[33,8,128]{2,1,0:T(8,128)S(1)}, f32[33,8,128]{2,1,0:T(8,128)S(1)}, u32[]{:S(2)}, u32[]{:S(2)}) collective-permute-start(f32[33,8,128]{2,1,0:T(8,128)S(1)} %get-tuple-element.116), channel_id=1, source_target_pairs={{0,2},{1,3},{2,0},{3,1},{4,6},{5,7},{6,4},{7,5},{8,10},{9,11},{10,... | collective-permute-start | bytes 405512 | tf_op jit(solution)/shard_map/ppermute | solution.py:597
  125.0 5.7 %collective-permute-start.3 = (f32[33,8,128]{2,1,0:T(8,128)S(1)}, f32[33,8,128]{2,1,0:T(8,128)S(1)}, u32[]{:S(2)}, u32[]{:S(2)}) collective-permute-start(f32[33,8,128]{2,1,0:T(8,128)S(1)} %get-tuple-element.117), channel_id=1, source_target_pairs={{0,6},{1,7},{2,4},{3,5},{4,2},{5,3},{6,0},{7,1},{8,14},{9,15},{10,... | collective-permute-start | bytes 405512 | tf_op jit(solution)/shard_map/ppermute | solution.py:597
  126.3 7.4 %collective-permute-start.2 = (f32[33,8,128]{2,1,0:T(8,128)S(1)}, f32[33,8,128]{2,1,0:T(8,128)S(1)}, u32[]{:S(2)}, u32[]{:S(2)}) collective-permute-start(f32[33,8,128]{2,1,0:T(8,128)S(1)} %get-tuple-element.118), channel_id=1, source_target_pairs={{0,4},{1,5},{2,6},{3,7},{4,0},{5,1},{6,2},{7,3},{8,12},{9,13},{10,... | collective-permute-start | bytes 405512 | tf_op jit(solution)/shard_map/ppermute | solution.py:597
  133.7 5.2 %collective-permute-start.6 = (f32[33,8,128]{2,1,0:T(8,128)S(1)}, f32[33,8,128]{2,1,0:T(8,128)S(1)}, u32[]{:S(2)}, u32[]{:S(2)}) collective-permute-start(f32[33,8,128]{2,1,0:T(8,128)S(1)} %fusion.24), channel_id=1, source_target_pairs={{0,6},{1,7},{2,4},{3,5},{4,2},{5,3},{6,0},{7,1},{8,14},{9,15},{10,... | collective-permute-start | bytes 405512 | tf_op jit(solution)/shard_map/ppermute | solution.py:597
  135.3 5.5 %collective-permute-start.5 = (f32[33,8,128]{2,1,0:T(8,128)S(1)}, f32[33,8,128]{2,1,0:T(8,128)S(1)}, u32[]{:S(2)}, u32[]{:S(2)}) collective-permute-start(f32[33,8,128]{2,1,0:T(8,128)S(1)} %fusion.24), channel_id=1, source_target_pairs={{0,4},{1,5},{2,6},{3,7},{4,0},{5,1},{6,2},{7,3},{8,12},{9,13},{10,... | collective-permute-start | bytes 405512 | tf_op jit(solution)/shard_map/ppermute | solution.py:597
  135.4 6.5 %collective-permute-start.4 = (f32[33,8,128]{2,1,0:T(8,128)S(1)}, f32[33,8,128]{2,1,0:T(8,128)S(1)}, u32[]{:S(2)}, u32[]{:S(2)}) collective-permute-start(f32[33,8,128]{2,1,0:T(8,128)S(1)} %fusion.24), channel_id=1, source_target_pairs={{0,2},{1,3},{2,0},{3,1},{4,6},{5,7},{6,4},{7,5},{8,10},{9,11},{10,... | collective-permute-start | bytes 405512 | tf_op jit(solution)/shard_map/ppermute | solution.py:597
  141.8 4.3 %collective-permute-start.7 = (f32[132,8,128]{2,1,0:T(8,128)S(1)}, f32[132,8,128]{2,1,0:T(8,128)S(1)}, u32[]{:S(2)}, u32[]{:S(2)}) collective-permute-start(f32[132,8,128]{2,1,0:T(8,128)S(1)} %pad_maximum_fusion), channel_id=1, source_target_pairs={{0,1},{1,0},{2,3},{3,2},{4,5},{5,4},{6,7},{7,6},{8,9},{9,8},{10,11... | collective-permute-start | bytes 1622024 | tf_op jit(solution)/shard_map/ppermute | solution.py:597

commit v4 on v3

--- a/solution.py
+++ b/solution.py
@@ -16,10 +16,11 @@
 PAIRS = 16
 ROWS_OUT = 64
 ROWS_IN = 64
-PIECE = 32
+PIECE = 24
 VMEM_BYTES = 24 * 1024 * 1024
 WIDE_BYTES = 56 * 1024 * 1024
 WIDEST_BYTES = 62 * 1024 * 1024
+SEND_BYTES = 50 * 1024 * 1024
 
 
 def sector_mask(left_sizes, right_sizes, block_size):
@@ -263,12 +264,11 @@
         return (rows * ROWS + LANES - 1) >> 7
 
     def sector(d, carry):
-        first, out_rows, strips = out_tbl[3 * d], out_tbl[3 * d + 1], out_tbl[3 * d + 2]
+        first, out_rows, strips, flip, m_blocks, n_blocks = (out_tbl[6 * d + i] for i in range(6))
         units = [d + t * HELD for t in range(PAIRS // HELD)]
         rows = [tbl[u * T_WIDTH + T_ROWS] for u in units]
         nx = [tbl[u * T_WIDTH + T_NX] for u in units]
         ny = [tbl[u * T_WIDTH + T_NY] for u in units]
-        m_blocks = blocks(out_rows)
 
         def masked(ref, t, height, width, count):
             row = lax.broadcasted_iota(jnp.int32, (height, width), 0)
@@ -296,10 +296,17 @@
                 part = dot3(split3(a), split3(masked(y_ref, t, k, n, ny[t])))
                 part = part + jnp.where(ny[t] > 0, 0.0, z_ref[t, :m, :n])
                 total = part if total is None else total + part
-            sum_ref[:m, :n] = total
+
+            @pl.when(flip == 0)
+            def _():
+                sum_ref[:m, :n] = total
+
+            @pl.when(flip != 0)
+            def _():
+                sum_ref[:n, :m] = total.T
 
         inner_y = [jnp.where(ny[t] > 0, blocks(rows[t]), 1) for t in range(2)]
-        variants(m_blocks, jnp.maximum(inner_y[0], inner_y[1]), strips, added)
+        variants(m_blocks, jnp.maximum(inner_y[0], inner_y[1]), n_blocks, added)
 
         for strip in range(2):
             @pl.when(strip < strips)
@@ -337,11 +344,14 @@
 
     row = lax.broadcasted_iota(jnp.int32, (ROWS, LANES), 0)
     col = lax.broadcasted_iota(jnp.int32, (ROWS, LANES), 1)
-    copies = []
-    for d in range(HELD):
+    def copy(d):
+        return pltpu.make_async_copy(block_ref.at[d], out_ref.at[d], sems.at[d])
+
+    def sector(d, carry):
+        first, rows, strips, flip, high, wide = (out_tbl[6 * d + i] for i in range(6))
+        height = jnp.where(flip > 0, right_sizes[d], left_sizes[d])
+        width = jnp.where(flip > 0, left_sizes[d], right_sizes[d])
         block_ref[d] = jnp.zeros((BLK, BLK), jnp.float32)
-        first, rows, strips = out_tbl[3 * d], out_tbl[3 * d + 1], out_tbl[3 * d + 2]
-        height, width = left_sizes[d], right_sizes[d]
         for strip in range(2):
             @pl.when(strip < strips)
             def _():
@@ -359,13 +369,30 @@
 
                 lax.fori_loop(0, (rows + 3) >> 2, four, 0)
 
-        copies.append(pltpu.make_async_copy(block_ref.at[d], out_ref.at[d], sems.at[d]))
-        copies[-1].start()
-    for copy in copies:
-        copy.wait()
-
-
-O_CORE, O_CHIP, O_FLAG = 3 * HELD, 3 * HELD + 1, 3 * HELD + 2
+        for n in (1, 2):
+            for m in (1, 2):
+                @pl.when((flip > 0) & (wide == n) & (high == m))
+                def _():
+                    rows, cols = n * LANES, m * LANES
+                    turned = block_ref[d, :rows, :cols].T
+                    if m < n:
+                        block_ref[d, cols:rows, :cols] = jnp.zeros((rows - cols, cols), jnp.float32)
+                    if n < m:
+                        block_ref[d, :rows, rows:cols] = jnp.zeros((rows, cols - rows), jnp.float32)
+                    block_ref[d, :cols, :rows] = turned
+
+        copy(d).start()
+        return carry
+
+    def finish(d, carry):
+        copy(d).wait()
+        return carry
+
+    lax.fori_loop(0, HELD, sector, 0)
+    lax.fori_loop(0, HELD, finish, 0)
+
+
+O_CORE, O_CHIP, O_FLAG = 6 * HELD, 6 * HELD + 1, 6 * HELD + 2
 
 SMEM = pl.BlockSpec(memory_space=pltpu.SMEM)
 VMEM = pl.BlockSpec(memory_space=pltpu.VMEM)
@@ -411,7 +438,7 @@
             scratch(4 * PAIRS, BLK, LANES),
             pltpu.SemaphoreType.DMA((4 * PAIRS,)),
         ],
-        compiler_params=WIDE,
+        compiler_params=pltpu.CompilerParams(vmem_limit_bytes=SEND_BYTES),
     )(*tables, strips)
 
 
@@ -502,7 +529,10 @@
     base = before(onto, 1)
     filled = jnp.sum(onto, axis=1)
 
-    out_rows, out_strips = up(size_l, ROWS), up(size_r, LANES)
+    high, wide = up(size_l, LANES), up(size_r, LANES)
+    flip = (up(size_r, ROWS) * high < up(size_l, ROWS) * wide).astype(jnp.int32)
+    out_rows = up(jnp.where(flip > 0, size_r, size_l), ROWS)
+    out_strips = jnp.where(flip > 0, high, wide)
     out_tiles = out_rows * out_strips
     out_first = before(out_tiles, 1)
     spilled = (
@@ -563,7 +593,9 @@
 
     out_tbl = jnp.concatenate(
         [
-            jnp.stack([own(out_first), own(out_rows), own(out_strips)], axis=1).reshape(-1),
+            jnp.stack(
+                [own(v) for v in (out_first, out_rows, out_strips, flip, high, wide)], axis=1
+            ).reshape(-1),
             jnp.stack([core, chip, spilled.astype(jnp.int32)]).astype(jnp.int32),
         ]
     )

time: 155 us -> 151 us (0.974)
  waiting for transfers between devices: 49.8 us -> 46.5 us
    ppermute x8, waiting for transfers between devices: 13 us -> 9.87 us  [swap(): return lax.ppermute(values, 'term', [(i, i ^ bits) for i in range(MEMBERS)])]
where the time goes in v4:
time: 151 us
  waiting for transfers between devices  46.5 us (31%)
  starting transfers between devices  45.7 us (30%)
  Pallas kernels  27.4 us (18%)
  between operations  16.4 us (11%)
  other arithmetic  10.4 us (7%)
  local copies, waits for them, and re-layouts  4.08 us (3%)
    all_to_all x1, waiting for transfers between devices, per_device(): lax.all_to_all(sent.reshape(PEERS, ROWS_OUT, LANES), 'sec', 0, 0, tiled=T...  20.5 us
    all_to_all x1, waiting for transfers between devices, per_device(): lax.all_to_all(passed.reshape(PEERS, ROWS_IN, LANES), 'sec', 0, 0, tiled=...  16.1 us
    ppermute x8, starting transfers between devices, swap(): return lax.ppermute(values, 'term', [(i, i ^ bits) for i in range(MEMBERS)])  15.8 us
    all_to_all x1, starting transfers between devices, per_device(): facts = lax.all_to_all(mine, 'sec', 0, 0, tiled=True)  11.9 us
    ppermute x8, waiting for transfers between devices, swap(): return lax.ppermute(values, 'term', [(i, i ^ bits) for i in range(MEMBERS)])  9.87 us
    all_to_all x1, starting transfers between devices, per_device(): lax.all_to_all(sent.reshape(PEERS, ROWS_OUT, LANES), 'sec', 0, 0, tiled=T...  9.45 us
    pallas_call x1, Pallas kernels, carry_call(): pl.pallas_call(carry_kernel, grid=(HELD // TOGETHER,), out_shape=floats(H...  9.42 us
    all_to_all x1, starting transfers between devices, per_device(): lax.all_to_all(passed.reshape(PEERS, ROWS_IN, LANES), 'sec', 0, 0, tiled=...  8.57 us
  transfers between devices with their start and end apart: 11, of which 10 were waited for; matrix products, arithmetic and copies ran while one was open for 7% of the time, Pallas kernels for 6%

profile of v4, /device:TPU:1, one launch (start us, length us, event | category | flops | bytes accessed | tf_op | source)
XLA Modules:
  0.0 150.7 jit_solution(17129958408784656296)
XLA Ops:
  6.5 0.7 pad_add_fusion.2
  7.2 0.6 broadcast_in_dim.357
  7.9 11.9 %all-to-all-start.2 = ((s32[32,4,8]{2,1,0:T(4,128)}), s32[32,4,8]{2,1,0:T(4,128)S(1)}, u32[]{:S(2)}, u32[]{:S(2)}) async-start(s32[32,4,8]{2,1,0:T(4,128)} %broadcast_in_dim.357), calls=%async_computation.2 | async-start | bytes 131072 | tf_op jit(solution)/shard_map/all_to_all | solution.py:613
  19.8 9.4 %shard_map.240 = f32[8,14,256,128]{3,2,1,0:T(8,128)} custom-call(s32[8]{0:T(128)} %left_sizes.1, s32[8]{0:T(128)} %right_sizes.1, f32[8,256,256]{2,1,0:T(8,128)} %psi_ref.1, f32[2,8,256,256]{3,2,1,0:T(8,128)} %right_ref.1), custom_call_target="tpu_custom_call" | custom-call | flops 1610612736 | bytes 25165824 | tf_op jit(solution)/shard_map/pallas_call | solution.py:413
  29.3 0.1 eq.113
  29.8 0.1 select_reduce_fusion.5
  30.1 0.1 select_reduce_fusion.17
  30.3 0.2 dynamic-slice_reduce_fusion
  30.6 0.2 dynamic-slice_reduce_fusion.2
  30.8 0.2 select_reduce_fusion.19
  31.2 4.5 %shard_map.241 = f32[2048,128]{1,0:T(8,128)} custom-call(s32[16,4]{1,0:T(8,128)S(1)} %get-tuple-element.140.source, s32[16,4]{1,0:T(8,128)S(1)} %get-tuple-element.139.rows, s32[16,4]{1,0:T(8,128)S(1)} %get-tuple-element.138.first, f32[112,256,128]{2,1,0:T(8,128)} %bitcast.105), custom_call_target="tpu_custom_call" | custom-call | tf_op jit(solution)/shard_map/pallas_call | solution.py:432
  35.7 9.4 %all-to-all-start.3 = ((f32[32,64,128]{2,1,0:T(8,128)}), f32[32,64,128]{2,1,0:T(8,128)S(1)}, u32[]{:S(2)}, u32[]{:S(2)}) async-start(f32[32,64,128]{2,1,0:T(8,128)} %bitcast.45), calls=%async_computation.3 | async-start | bytes 2097152 | tf_op jit(solution)/shard_map/all_to_all | solution.py:618
  45.3 0.2 select_reduce_fusion.6
  45.6 0.1 iota_compare_fusion.9
  45.7 0.4 select_reduce_fusion.3
  46.3 2.2 %select_reduce_fusion.2 = s32[4,32,32]{2,1,0:T(8,128)S(1)} fusion(s32[4,32,32]{2,1,0:T(8,128)S(1)} %copy.202, pred[32,32]{1,0:T(8,128)(4,1)S(1)} %bitcast.118), kind=kLoop, calls=%fused_computation.53 | loop fusion | flops 258048 | bytes 33792 | tf_op jit(solution)/shard_map/reduce_sum | solution.py:495
  48.8 0.6 fusion.21
  49.4 20.5 %all-to-all-done.3 = f32[32,64,128]{2,1,0:T(8,128)S(1)} async-done(((f32[32,64,128]{2,1,0:T(8,128)}), f32[32,64,128]{2,1,0:T(8,128)S(1)}, u32[]{:S(2)}, u32[]{:S(2)}) %all-to-all-start.3) | async-done | bytes 1048608 | tf_op jit(solution)/shard_map/all_to_all | solution.py:618
  69.9 3.0 %shard_map.242 = f32[2048,128]{1,0:T(8,128)} custom-call(s32[2048]{0:T(1024)S(1)} %min.20.idx, s32[32]{0:T(128)S(1)} %fusion.47.count, f32[2048,128]{1,0:T(8,128)S(1)} %bitcast.103), custom_call_target="tpu_custom_call" | custom-call | tf_op jit(solution)/shard_map/pallas_call | solution.py:446
  72.9 8.6 %all-to-all-start.4 = ((f32[32,64,128]{2,1,0:T(8,128)}), f32[32,64,128]{2,1,0:T(8,128)S(1)}, u32[]{:S(2)}, u32[]{:S(2)}) async-start(f32[32,64,128]{2,1,0:T(8,128)} %bitcast.47), calls=%async_computation.4 | async-start | bytes 2097152 | tf_op jit(solution)/shard_map/all_to_all | solution.py:620
  81.7 0.2 fusion.34
  81.9 0.2 fusion.36
  82.1 0.2 fusion.38
  82.6 0.7 compare_reduce_fusion.2
  83.2 0.7 compare_reduce_fusion.1
  85.2 0.7 compare_reduce_fusion
  86.5 3.1 %select_reduce_fusion.7 = (s32[16]{0:T(128)S(1)}, s32[16]{0:T(128)S(1)}, s32[16]{0:T(128)S(1)}, s32[16]{0:T(128)S(1)}, s32[16]{0:T(128)S(1)}, /*index=5*/s32[16]...) fusion(s32[32]{0:T(128)S(1)} %get-tuple-element.125, s32[32,16]{0,1:T(8,128)S(1)} %bitcast.114, ...), kind=kLoop, calls=%fused_computation.67 | loop fusion | flops 180064 | bytes 15808 | tf_op jit(solution)/shard_map/reduce_sum | solution.py:585
  90.0 16.1 %all-to-all-done.4 = f32[32,64,128]{2,1,0:T(8,128)S(1)} async-done(((f32[32,64,128]{2,1,0:T(8,128)}), f32[32,64,128]{2,1,0:T(8,128)S(1)}, u32[]{:S(2)}, u32[]{:S(2)}) %all-to-all-start.4) | async-done | bytes 1048608 | tf_op jit(solution)/shard_map/all_to_all | solution.py:620
  106.1 8.4 %shard_map.243 = (f32[100,8,128]{2,1,0:T(8,128)S(1)}, f32[100,8,128]{2,1,0:T(8,128)S(1)}) custom-call(s32[160]{0:T(256)S(1)} %reshape.773.tbl, s32[51]{0:T(128)S(1)} %pad_add_fusion.3.out_tbl, f32[2048,128]{1,0:T(8,128)S(1)} %bitcast.104, f32[16,256,256]{2,1,0:T(8,128)} %bitcast.107), custom_call_target="tpu_custom_call" | custom-call | tf_op jit(solution)/shard_map/pallas_call | solution.py:456
  114.4 5.4 %collective-permute-start = (f32[100,8,128]{2,1,0:T(8,128)S(1)}, f32[100,8,128]{2,1,0:T(8,128)S(1)}, u32[]{:S(2)}, u32[]{:S(2)}) collective-permute-start(f32[100,8,128]{2,1,0:T(8,128)S(1)} %get-tuple-element.44), channel_id=1, source_target_pairs={{0,1},{1,0},{2,3},{3,2},{4,5},{5,4},{6,7},{7,6},{8,9},{9,8},{10,11... | collective-permute-start | bytes 1228808 | tf_op jit(solution)/shard_map/ppermute | solution.py:629
  119.8 1.4 collective-permute-done
  121.3 1.7 %collective-permute-start.1 = (f32[25,8,128]{2,1,0:T(8,128)S(1)}, f32[25,8,128]{2,1,0:T(8,128)S(1)}, u32[]{:S(2)}, u32[]{:S(2)}) collective-permute-start(f32[25,8,128]{2,1,0:T(8,128)S(1)} %get-tuple-element.119), channel_id=1, source_target_pairs={{0,2},{1,3},{2,0},{3,1},{4,6},{5,7},{6,4},{7,5},{8,10},{9,11},{10,... | collective-permute-start | bytes 307208 | tf_op jit(solution)/shard_map/ppermute | solution.py:629
  123.0 1.6 %collective-permute-start.3 = (f32[25,8,128]{2,1,0:T(8,128)S(1)}, f32[25,8,128]{2,1,0:T(8,128)S(1)}, u32[]{:S(2)}, u32[]{:S(2)}) collective-permute-start(f32[25,8,128]{2,1,0:T(8,128)S(1)} %get-tuple-element.120), channel_id=1, source_target_pairs={{0,6},{1,7},{2,4},{3,5},{4,2},{5,3},{6,0},{7,1},{8,14},{9,15},{10,... | collective-permute-start | bytes 307208 | tf_op jit(solution)/shard_map/ppermute | solution.py:629
  124.6 0.3 collective-permute-start.2
  124.9 0.9 collective-permute-done.1
  125.8 1.9 %collective-permute-done.3 = f32[25,8,128]{2,1,0:T(8,128)S(1)} collective-permute-done((f32[25,8,128]{2,1,0:T(8,128)S(1)}, f32[25,8,128]{2,1,0:T(8,128)S(1)}, u32[]{:S(2)}, u32[]{:S(2)}) %collective-permute-start.3) | collective-permute-done | bytes 102432 | tf_op jit(solution)/shard_map/ppermute | solution.py:629
  127.7 2.0 %collective-permute-done.2 = f32[25,8,128]{2,1,0:T(8,128)S(1)} collective-permute-done((f32[25,8,128]{2,1,0:T(8,128)S(1)}, f32[25,8,128]{2,1,0:T(8,128)S(1)}, u32[]{:S(2)}, u32[]{:S(2)}) %collective-permute-start.2) | collective-permute-done | bytes 102432 | tf_op jit(solution)/shard_map/ppermute | solution.py:629
  129.8 1.1 collective-permute-start.6
  130.9 0.5 collective-permute-start.5
  131.4 1.7 %collective-permute-start.4 = (f32[25,8,128]{2,1,0:T(8,128)S(1)}, f32[25,8,128]{2,1,0:T(8,128)S(1)}, u32[]{:S(2)}, u32[]{:S(2)}) collective-permute-start(f32[25,8,128]{2,1,0:T(8,128)S(1)} %fusion.24), channel_id=1, source_target_pairs={{0,2},{1,3},{2,0},{3,1},{4,6},{5,7},{6,4},{7,5},{8,10},{9,11},{10,... | collective-permute-start | bytes 307208 | tf_op jit(solution)/shard_map/ppermute | solution.py:629
  133.1 1.5 collective-permute-done.6
  134.6 1.3 collective-permute-done.5
  135.9 0.6 collective-permute-done.4
  136.6 3.4 %collective-permute-start.7 = (f32[100,8,128]{2,1,0:T(8,128)S(1)}, f32[100,8,128]{2,1,0:T(8,128)S(1)}, u32[]{:S(2)}, u32[]{:S(2)}) collective-permute-start(f32[100,8,128]{2,1,0:T(8,128)S(1)} %pad_maximum_fusion), channel_id=1, source_target_pairs={{0,1},{1,0},{2,3},{3,2},{4,5},{5,4},{6,7},{7,6},{8,9},{9,8},{10,11... | collective-permute-start | bytes 1228808 | tf_op jit(solution)/shard_map/ppermute | solution.py:629
  140.0 0.5 slice.77
  141.2 0.2 collective-permute-done.7
  141.4 2.4 %conditional.1 = (f32[8,256,256]{2,1,0:T(8,128)}) conditional(s32[]{:T(128)} %bitcast.50, (s32[51]{0:T(128)S(1)}, s32[8]{0:T(128)S(1)}, s32[8]{0:T(128)S(1)}, f32[100,8,128]{2,1,0:T(8,128)S(1)}, f32[100,8,128]{2,1,0:T(8,128)S(1)}) %tuple.75, (s32[8]{0:T(128)S(1)}, s32[8]{0:T(128)S(1)}, s32[2,8]{1,0:T(2,128)S(1)}, f32[2,8,256,256]{3,2,1,0:T(8,128)}, ...), branch_computations={%region_23.24_spmd, %region_24.31_spmd} | conditional | flops 6547847168 | bytes 155251904 | solution.py:636
  141.4 2.2 %branch_0_fun.1 = f32[8,256,256]{2,1,0:T(8,128)} custom-call(s32[51]{0:T(128)S(1)} %get-tuple-element.30.out_tbl, s32[8]{0:T(128)S(1)} %get-tuple-element.31.left_sizes, s32[8]{0:T(128)S(1)} %get-tuple-element.32.right_sizes, f32[100,8,128]{2,1,0:T(8,128)S(1)} %get-tuple-element.33.own_ref, f32[100,8,128]{2,1,0:T(8,128)S(1)} %get-tuple-element.34.other_ref), custom_call_target="tpu_custom_call" | custom-call | tf_op jit(solution)/shard_map/cond/branch_0_fun/pallas_call | solution.py:473
  (77 shorter events, 2.3 us)
Async XLA Ops:
  7.9 21.4 %all-to-all-start.2 = ((s32[32,4,8]{2,1,0:T(4,128)}), s32[32,4,8]{2,1,0:T(4,128)S(1)}, u32[]{:S(2)}, u32[]{:S(2)}) async-start(s32[32,4,8]{2,1,0:T(4,128)} %broadcast_in_dim.357), calls=%async_computation.2 | async-start | bytes 131072 | tf_op jit(solution)/shard_map/all_to_all | solution.py:613
  19.8 10.4 %copy-start.7 = (pred[16,16]{1,0:T(8,128)(4,1)S(1)}, pred[16,16]{1,0:T(8,128)(4,1)}, u32[]{:S(2)}) copy-start(pred[16,16]{1,0:T(8,128)(4,1)} %constant.184.clone) | copy-start | bytes 772
  19.8 11.0 %copy-start.3 = (s32[1,16]{0,1:T(8,128)S(1)}, s32[1,16]{0,1:T(8,128)}, u32[]{:S(2)}) copy-start(s32[1,16]{0,1:T(8,128)} %constant.218) | copy-start | bytes 196
  19.8 11.0 %copy-start.4 = (s32[1,16]{0,1:T(8,128)S(1)}, s32[1,16]{0,1:T(8,128)}, u32[]{:S(2)}) copy-start(s32[1,16]{0,1:T(8,128)} %constant.217) | copy-start | bytes 196
  19.8 11.2 %copy-start.10 = (s32[4]{0:T(128)S(1)}, s32[4]{0:T(128)}, u32[]{:S(2)}) copy-start(s32[4]{0:T(128)} %constant.215) | copy-start | bytes 52
  19.8 11.2 %copy-start.11 = (s32[4]{0:T(128)S(1)}, s32[4]{0:T(128)}, u32[]{:S(2)}) copy-start(s32[4]{0:T(128)} %constant.213) | copy-start | bytes 52
  19.8 11.2 %copy-start.12 = (pred[4]{0:T(512)(128)(4,1)S(1)}, pred[4]{0:T(512)(128)(4,1)}, u32[]{:S(2)}) copy-start(pred[4]{0:T(512)(128)(4,1)} %constant.212) | copy-start | bytes 16
  19.8 11.2 %copy-start.13 = (s32[16]{0:T(128)S(1)}, s32[16]{0:T(128)}, u32[]{:S(2)}) copy-start(s32[16]{0:T(128)} %constant.211) | copy-start | bytes 196
  31.1 15.1 %copy-start.5 = (pred[32,32]{1,0:T(32,128)(4,1)S(1)}, pred[32,32]{1,0:T(32,128)(4,1)}, u32[]{:S(2)}) copy-start(pred[32,32]{1,0:T(32,128)(4,1)} %constant.186.clone) | copy-start | bytes 3076
  35.6 45.9 %copy-start.14 = (s32[16,1,1]{0,2,1:T(1,128)S(1)}, s32[16,1,1]{0,2,1:T(1,128)}, u32[]{:S(2)}) copy-start(s32[16,1,1]{0,2,1:T(1,128)} %constant.197.clone) | copy-start | bytes 196
  35.7 45.9 %copy-start.8 = (pred[8,8]{1,0:T(8,128)(4,1)S(1)}, pred[8,8]{1,0:T(8,128)(4,1)}, u32[]{:S(2)}) copy-start(pred[8,8]{1,0:T(8,128)(4,1)} %constant.187.clone) | copy-start | bytes 196
  35.7 50.9 %copy-start.6 = (pred[16,16]{1,0:T(8,128)(4,1)S(1)}, pred[16,16]{1,0:T(8,128)(4,1)}, u32[]{:S(2)}) copy-start(pred[16,16]{1,0:T(8,128)(4,1)} %constant.205) | copy-start | bytes 772
  35.7 34.3 %all-to-all-start.3 = ((f32[32,64,128]{2,1,0:T(8,128)}), f32[32,64,128]{2,1,0:T(8,128)S(1)}, u32[]{:S(2)}, u32[]{:S(2)}) async-start(f32[32,64,128]{2,1,0:T(8,128)} %bitcast.45), calls=%async_computation.3 | async-start | bytes 2097152 | tf_op jit(solution)/shard_map/all_to_all | solution.py:618
  72.9 33.1 %all-to-all-start.4 = ((f32[32,64,128]{2,1,0:T(8,128)}), f32[32,64,128]{2,1,0:T(8,128)S(1)}, u32[]{:S(2)}, u32[]{:S(2)}) async-start(f32[32,64,128]{2,1,0:T(8,128)} %bitcast.47), calls=%async_computation.4 | async-start | bytes 2097152 | tf_op jit(solution)/shard_map/all_to_all | solution.py:620
  106.1 35.3 %copy-start.1 = (s32[8]{0:T(128)S(1)}, s32[8]{0:T(128)}, u32[]{:S(2)}) copy-start(s32[8]{0:T(128)} %left_sizes.1) | copy-start | bytes 100
  106.1 35.3 %copy-start.2 = (s32[8]{0:T(128)S(1)}, s32[8]{0:T(128)}, u32[]{:S(2)}) copy-start(s32[8]{0:T(128)} %right_sizes.1) | copy-start | bytes 100
  106.1 35.3 %copy-start.9 = (s32[2,8]{1,0:T(2,128)S(1)}, s32[2,8]{1,0:T(2,128)}, u32[]{:S(2)}) copy-start(s32[2,8]{1,0:T(2,128)} %param.32) | copy-start | bytes 196
  114.4 6.8 %collective-permute-start = (f32[100,8,128]{2,1,0:T(8,128)S(1)}, f32[100,8,128]{2,1,0:T(8,128)S(1)}, u32[]{:S(2)}, u32[]{:S(2)}) collective-permute-start(f32[100,8,128]{2,1,0:T(8,128)S(1)} %get-tuple-element.44), channel_id=1, source_target_pairs={{0,1},{1,0},{2,3},{3,2},{4,5},{5,4},{6,7},{7,6},{8,9},{9,8},{10,11... | collective-permute-start | bytes 1228808 | tf_op jit(solution)/shard_map/ppermute | solution.py:629
  121.3 4.5 %collective-permute-start.1 = (f32[25,8,128]{2,1,0:T(8,128)S(1)}, f32[25,8,128]{2,1,0:T(8,128)S(1)}, u32[]{:S(2)}, u32[]{:S(2)}) collective-permute-start(f32[25,8,128]{2,1,0:T(8,128)S(1)} %get-tuple-element.119), channel_id=1, source_target_pairs={{0,2},{1,3},{2,0},{3,1},{4,6},{5,7},{6,4},{7,5},{8,10},{9,11},{10,... | collective-permute-start | bytes 307208 | tf_op jit(solution)/shard_map/ppermute | solution.py:629
  123.0 4.7 %collective-permute-start.3 = (f32[25,8,128]{2,1,0:T(8,128)S(1)}, f32[25,8,128]{2,1,0:T(8,128)S(1)}, u32[]{:S(2)}, u32[]{:S(2)}) collective-permute-start(f32[25,8,128]{2,1,0:T(8,128)S(1)} %get-tuple-element.120), channel_id=1, source_target_pairs={{0,6},{1,7},{2,4},{3,5},{4,2},{5,3},{6,0},{7,1},{8,14},{9,15},{10,... | collective-permute-start | bytes 307208 | tf_op jit(solution)/shard_map/ppermute | solution.py:629
  124.6 5.1 %collective-permute-start.2 = (f32[25,8,128]{2,1,0:T(8,128)S(1)}, f32[25,8,128]{2,1,0:T(8,128)S(1)}, u32[]{:S(2)}, u32[]{:S(2)}) collective-permute-start(f32[25,8,128]{2,1,0:T(8,128)S(1)} %get-tuple-element.121), channel_id=1, source_target_pairs={{0,4},{1,5},{2,6},{3,7},{4,0},{5,1},{6,2},{7,3},{8,12},{9,13},{10,... | collective-permute-start | bytes 307208 | tf_op jit(solution)/shard_map/ppermute | solution.py:629
  129.8 4.8 %collective-permute-start.6 = (f32[25,8,128]{2,1,0:T(8,128)S(1)}, f32[25,8,128]{2,1,0:T(8,128)S(1)}, u32[]{:S(2)}, u32[]{:S(2)}) collective-permute-start(f32[25,8,128]{2,1,0:T(8,128)S(1)} %fusion.24), channel_id=1, source_target_pairs={{0,6},{1,7},{2,4},{3,5},{4,2},{5,3},{6,0},{7,1},{8,14},{9,15},{10,... | collective-permute-start | bytes 307208 | tf_op jit(solution)/shard_map/ppermute | solution.py:629
  130.9 5.0 %collective-permute-start.5 = (f32[25,8,128]{2,1,0:T(8,128)S(1)}, f32[25,8,128]{2,1,0:T(8,128)S(1)}, u32[]{:S(2)}, u32[]{:S(2)}) collective-permute-start(f32[25,8,128]{2,1,0:T(8,128)S(1)} %fusion.24), channel_id=1, source_target_pairs={{0,4},{1,5},{2,6},{3,7},{4,0},{5,1},{6,2},{7,3},{8,12},{9,13},{10,... | collective-permute-start | bytes 307208 | tf_op jit(solution)/shard_map/ppermute | solution.py:629
  131.4 5.2 %collective-permute-start.4 = (f32[25,8,128]{2,1,0:T(8,128)S(1)}, f32[25,8,128]{2,1,0:T(8,128)S(1)}, u32[]{:S(2)}, u32[]{:S(2)}) collective-permute-start(f32[25,8,128]{2,1,0:T(8,128)S(1)} %fusion.24), channel_id=1, source_target_pairs={{0,2},{1,3},{2,0},{3,1},{4,6},{5,7},{6,4},{7,5},{8,10},{9,11},{10,... | collective-permute-start | bytes 307208 | tf_op jit(solution)/shard_map/ppermute | solution.py:629
  136.6 4.8 %collective-permute-start.7 = (f32[100,8,128]{2,1,0:T(8,128)S(1)}, f32[100,8,128]{2,1,0:T(8,128)S(1)}, u32[]{:S(2)}, u32[]{:S(2)}) collective-permute-start(f32[100,8,128]{2,1,0:T(8,128)S(1)} %pad_maximum_fusion), channel_id=1, source_target_pairs={{0,1},{1,0},{2,3},{3,2},{4,5},{5,4},{6,7},{7,6},{8,9},{9,8},{10,11... | collective-permute-start | bytes 1228808 | tf_op jit(solution)/shard_map/ppermute | solution.py:629

commit v5 on v4

--- a/solution.py
+++ b/solution.py
@@ -14,8 +14,7 @@
 MEMBERS = 8
 HELD = 8
 PAIRS = 16
-ROWS_OUT = 64
-ROWS_IN = 64
+SLOT_ROWS = (64, 104)
 PIECE = 24
 VMEM_BYTES = 24 * 1024 * 1024
 WIDE_BYTES = 56 * 1024 * 1024
@@ -168,7 +167,7 @@
             put(i, S_TURN + 2 * t, product.T)
 
 
-def send_kernel(source, rows, first, strip_ref, buf_ref, held_ref, sems):
+def send_kernel(slot, source, rows, first, strip_ref, buf_ref, held_ref, sems):
     def copy(p, c):
         e = 4 * p + c
         return pltpu.make_async_copy(strip_ref.at[source[p, c]], held_ref.at[e], sems.at[e])
@@ -188,18 +187,18 @@
             def four(i, inner):
                 for k in range(4):
                     a = i * 4 + k
-                    at = tile_rows(begin + a, ROWS_OUT)
+                    at = tile_rows(begin + a, slot)
                     tile = held_ref[4 * p + c, tile_at(a), :]
-                    buf_ref[pl.ds(at, ROWS, stride=ROWS_OUT), :] = tile
+                    buf_ref[pl.ds(at, ROWS, stride=slot), :] = tile
                 return inner
 
             lax.fori_loop(0, (rows[p, c] + 3) >> 2, four, 0)
 
 
-def relay_kernel(idx, count, in_ref, out_ref):
-    def slot(peer, carry):
+def relay_kernel(slot, idx, count, in_ref, out_ref):
+    def fill(peer, carry):
         def some(i, inner):
-            at = peer * ROWS_IN + i * ROWS
+            at = peer * slot + i * ROWS
             for k in range(ROWS):
                 out_ref[pl.ds(at + k, 1), :] = in_ref[pl.ds(idx[at + k], 1), :]
             return inner
@@ -207,7 +206,7 @@
         lax.fori_loop(0, (count[peer] + ROWS - 1) >> 3, some, 0)
         return carry
 
-    lax.fori_loop(0, PEERS, slot, 0)
+    lax.fori_loop(0, PEERS, fill, 0)
 
 
 STREAM = MEMBERS * PIECE
@@ -220,7 +219,7 @@
 
 
 def land_kernel(
-    tbl, out_tbl, buf_ref, left_ref, keep_ref, send_ref, x_ref, y_ref, z_ref, sum_ref, stream_ref
+    slot, tbl, out_tbl, buf_ref, left_ref, keep_ref, send_ref, x_ref, y_ref, z_ref, sum_ref, stream_ref
 ):
     z_ref[...] = jnp.zeros_like(z_ref)
 
@@ -231,14 +230,14 @@
         for k in range(4):
             kind = (start + k) & 3
             rank = tbl[at + T_BASE + kind] + ((before + k) >> 2)
-            begin.append((kind * (ROWS * ROWS_IN), rank))
+            begin.append((kind * (ROWS * slot), rank))
 
         def four(i, carry):
             for k in range(4):
                 first, rank = begin[k]
-                row = first + jnp.minimum(rank + i, ROWS_IN - 1)
+                row = first + jnp.minimum(rank + i, slot - 1)
                 dst_ref[u, tile_at(i * 4 + k), strip_at(strip)] = buf_ref[
-                    pl.ds(row, ROWS, stride=ROWS_IN), :
+                    pl.ds(row, ROWS, stride=slot), :
                 ]
             return carry
 
@@ -428,10 +427,10 @@
     )(left_sizes, right_sizes, psi, right)
 
 
-def send_call(tables, strips):
+def send_call(slot, tables, strips):
     return pl.pallas_call(
-        send_kernel,
-        out_shape=floats(PEERS * ROWS_OUT, LANES),
+        functools.partial(send_kernel, slot),
+        out_shape=floats(PEERS * slot, LANES),
         in_specs=[SMEM, SMEM, SMEM, pl.BlockSpec(memory_space=pl.ANY)],
         out_specs=VMEM,
         scratch_shapes=[
@@ -442,19 +441,19 @@
     )(*tables, strips)
 
 
-def relay_call(idx, count, received):
+def relay_call(slot, idx, count, received):
     return pl.pallas_call(
-        relay_kernel,
-        out_shape=floats(PEERS * ROWS_IN, LANES),
+        functools.partial(relay_kernel, slot),
+        out_shape=floats(PEERS * slot, LANES),
         in_specs=[SMEM, SMEM, VMEM],
         out_specs=VMEM,
         compiler_params=PARAMS,
     )(idx, count, received)
 
 
-def land_call(tbl, out_tbl, received, left):
+def land_call(slot, tbl, out_tbl, received, left):
     return pl.pallas_call(
-        land_kernel,
+        functools.partial(land_kernel, slot),
         out_shape=[floats(4 * SENT, ROWS, LANES)] * 2,
         in_specs=[SMEM, SMEM, VMEM, VMEM],
         out_specs=[VMEM, VMEM],
@@ -535,11 +534,10 @@
     out_strips = jnp.where(flip > 0, high, wide)
     out_tiles = out_rows * out_strips
     out_first = before(out_tiles, 1)
-    spilled = (
-        jnp.any(total > 4 * (ROWS_OUT - 1))
-        | jnp.any(filled > ROWS_IN)
-        | jnp.any(jnp.sum(out_tiles, axis=1) > MEMBERS * PIECE)
-    )
+    crowded = jnp.any(jnp.sum(out_tiles, axis=1) > MEMBERS * PIECE)
+
+    def spilled(slot):
+        return jnp.any(total > 4 * (slot - 1)) | jnp.any(filled > slot) | crowded
 
     def own(values, axis=0):
         return lax.dynamic_index_in_dim(values, me, axis, keepdims=False)
@@ -569,12 +567,13 @@
     first_k = lax.dynamic_index_in_dim(first_row, kind, 0, keepdims=False)
     filled_k = lax.dynamic_index_in_dim(filled, kind, 0, keepdims=False)
     first_to = jnp.sum(jnp.where(hit_dev, first_k[:, :, None], 0), axis=1)
-    rank = np.arange(ROWS_IN, dtype=np.int32)[None, None, :]
-    here = (rank >= base_k[:, :, None]) & (rank < (base_k + onto_k)[:, :, None])
-    origin = np.arange(PEERS, dtype=np.int32)[:, None] * ROWS_OUT + first_to - base_k
-    relay_idx = jnp.sum(jnp.where(here, origin[:, :, None] + rank, 0), axis=0)
-    relay_idx = jnp.clip(relay_idx, 0, PEERS * ROWS_OUT - 1).reshape(-1)
-    relay_count = jnp.minimum(filled_k, ROWS_IN)
+
+    def relay_tbl(slot):
+        rank = np.arange(slot, dtype=np.int32)[None, None, :]
+        here = (rank >= base_k[:, :, None]) & (rank < (base_k + onto_k)[:, :, None])
+        origin = np.arange(PEERS, dtype=np.int32)[:, None] * slot + first_to - base_k
+        idx = jnp.sum(jnp.where(here, origin[:, :, None] + rank, 0), axis=0)
+        return jnp.clip(idx, 0, PEERS * slot - 1).reshape(-1), jnp.minimum(filled_k, slot)
 
     unit = np.arange(PAIRS, dtype=np.int32)[:, None, None]
     reach = (dest[None] == me * HELD + unit % HELD) & (
@@ -591,15 +590,12 @@
         axis=1,
     ).reshape(-1)
 
-    out_tbl = jnp.concatenate(
-        [
-            jnp.stack(
-                [own(v) for v in (out_first, out_rows, out_strips, flip, high, wide)], axis=1
-            ).reshape(-1),
-            jnp.stack([core, chip, spilled.astype(jnp.int32)]).astype(jnp.int32),
-        ]
-    )
-    return send_tbl, relay_idx, relay_count, land_tbl, out_tbl
+    def out_tbl(slot):
+        lines = [own(v) for v in (out_first, out_rows, out_strips, flip, high, wide)]
+        last = jnp.stack([core, chip, spilled(slot).astype(jnp.int32)]).astype(jnp.int32)
+        return jnp.concatenate([jnp.stack(lines, axis=1).reshape(-1), last])
+
+    return send_tbl, relay_tbl, land_tbl, out_tbl
 
 
 def per_device(psi_blocks, left_env, right_env, left_sizes, right_sizes, dest_sector):
@@ -612,34 +608,39 @@
     mine = jnp.broadcast_to(mine[None], (PEERS, 4, HELD))
     facts = lax.all_to_all(mine, "sec", 0, 0, tiled=True)
     tables = make_tables(facts, me, core, chip)
-    send_tbl, relay_idx, relay_count, land_tbl, out_tbl = tables
-
-    sent = send_call(send_tbl, strips)
-    hop = lax.all_to_all(sent.reshape(PEERS, ROWS_OUT, LANES), "sec", 0, 0, tiled=True)
-    passed = relay_call(relay_idx, relay_count, hop.reshape(PEERS * ROWS_OUT, LANES))
-    hop = lax.all_to_all(passed.reshape(PEERS, ROWS_IN, LANES), "sec", 0, 0, tiled=True)
-    keep, give = land_call(
-        land_tbl,
-        out_tbl,
-        hop.reshape(PEERS * ROWS_IN, LANES),
-        left_env.reshape(PAIRS, BLK, BLK),
-    )
+    send_tbl, relay_tbl, land_tbl, out_tbl = tables
 
     def swap(values, bits):
         return lax.ppermute(values, "term", [(i, i ^ bits) for i in range(MEMBERS)])
 
-    half = (keep + swap(give, 1)).reshape(4, SENT, ROWS, LANES)
-    piece = half[0] + swap(half[1], 2) + swap(half[2], 4) + swap(half[3], 6)
-    whole = jnp.concatenate([piece, swap(piece, 2), swap(piece, 4), swap(piece, 6)])
-    other = swap(whole, 1)
-
-    return lax.cond(
-        piece[PIECE, 0, 0] > 0.5,
-        lambda: dense_program(
+    def packed_program(slot, otherwise):
+        def exchange(rows):
+            there = lax.all_to_all(rows.reshape(PEERS, slot, LANES), "sec", 0, 0, tiled=True)
+            return there.reshape(PEERS * slot, LANES)
+
+        arrived = exchange(send_call(slot, send_tbl, strips))
+        idx, count = relay_tbl(slot)
+        arrived = exchange(relay_call(slot, idx, count, arrived))
+        left = left_env.reshape(PAIRS, BLK, BLK)
+        lines = out_tbl(slot)
+        keep, give = land_call(slot, land_tbl, lines, arrived, left)
+        half = (keep + swap(give, 1)).reshape(4, SENT, ROWS, LANES)
+        piece = half[0] + swap(half[1], 2) + swap(half[2], 4) + swap(half[3], 6)
+        whole = jnp.concatenate([piece, swap(piece, 2), swap(piece, 4), swap(piece, 6)])
+        other = swap(whole, 1)
+        return lax.cond(
+            piece[PIECE, 0, 0] > 0.5,
+            otherwise,
+            lambda: spread_call(lines, left_sizes, right_sizes, whole, other),
+        )
+
+    def dense():
+        return dense_program(
             psi_blocks, left_env, right_env, left_sizes, right_sizes, dest_sector
-        ),
-        lambda: spread_call(out_tbl, left_sizes, right_sizes, whole, other),
-    )
+        )
+
+    usual, tall = SLOT_ROWS
+    return packed_program(usual, lambda: packed_program(tall, dense))
 
 
 def solution(mesh):

time: 151 us -> 152 us (level)
  transfers between devices with their start and end apart: 11 -> 11, of which waited for: 10 -> 9; matrix products, arithmetic and copies ran while one was open for 7% -> 7% of each run, Pallas kernels for 6% -> 6%
where the time goes in v5:
time: 152 us
  waiting for transfers between devices  47.1 us (31%)
  starting transfers between devices  44.9 us (30%)
  Pallas kernels  28.4 us (19%)
  between operations  16.4 us (11%)
  other arithmetic  10.5 us (7%)
  local copies, waits for them, and re-layouts  4.08 us (3%)
    all_to_all x2, waiting for transfers between devices, exchange(): lax.all_to_all(rows.reshape(PEERS, slot, LANES), 'sec', 0, 0, tiled=True)  36.3 us
    all_to_all x2, starting transfers between devices, exchange(): lax.all_to_all(rows.reshape(PEERS, slot, LANES), 'sec', 0, 0, tiled=True)  18.3 us
    ppermute x8, starting transfers between devices, swap(): return lax.ppermute(values, 'term', [(i, i ^ bits) for i in range(MEMBERS)])  14.8 us
    all_to_all x1, starting transfers between devices, per_device(): facts = lax.all_to_all(mine, 'sec', 0, 0, tiled=True)  11.9 us
    ppermute x8, waiting for transfers between devices, swap(): return lax.ppermute(values, 'term', [(i, i ^ bits) for i in range(MEMBERS)])  10.8 us
    pallas_call x1, Pallas kernels, carry_call(): pl.pallas_call(carry_kernel, grid=(HELD // TOGETHER,), out_shape=floats(H...  9.42 us
    pallas_call x1, Pallas kernels, land_call(): pl.pallas_call(functools.partial(land_kernel, slot), out_shape=[floats(4...  9.08 us
    pallas_call x1, Pallas kernels, send_call(): pl.pallas_call(functools.partial(send_kernel, slot), out_shape=floats(PEE...  4.56 us
  transfers between devices with their start and end apart: 11, of which 9 were waited for; matrix products, arithmetic and copies ran while one was open for 7% of the time, Pallas kernels for 6%

profile of v5, /device:TPU:1, one launch (start us, length us, event | category | flops | bytes accessed | tf_op | source)
XLA Modules:
  0.0 151.6 jit_solution(9632847014473625146)
XLA Ops:
  6.5 0.7 pad_add_fusion.3
  7.2 0.6 broadcast_in_dim.364
  7.9 11.9 %all-to-all-start.4 = ((s32[32,4,8]{2,1,0:T(4,128)}), s32[32,4,8]{2,1,0:T(4,128)S(1)}, u32[]{:S(2)}, u32[]{:S(2)}) async-start(s32[32,4,8]{2,1,0:T(4,128)} %broadcast_in_dim.364), calls=%async_computation.4 | async-start | bytes 131072 | tf_op jit(solution)/shard_map/all_to_all | solution.py:609
  19.8 9.4 %shard_map.260 = f32[8,14,256,128]{3,2,1,0:T(8,128)} custom-call(s32[8]{0:T(128)} %left_sizes.1, s32[8]{0:T(128)} %right_sizes.1, f32[8,256,256]{2,1,0:T(8,128)} %psi_ref.1, f32[2,8,256,256]{3,2,1,0:T(8,128)} %right_ref.1), custom_call_target="tpu_custom_call" | custom-call | flops 1610612736 | bytes 25165824 | tf_op jit(solution)/shard_map/pallas_call | solution.py:412
  29.3 0.1 eq.113
  29.6 0.1 broadcast_in_dim.366
  29.9 0.2 select_reduce_fusion.5
  30.2 0.1 iota_compare_fusion.11
  30.4 0.1 select_reduce_fusion.17
  30.5 0.2 dynamic-slice_reduce_fusion
  30.7 0.2 dynamic-slice_reduce_fusion.2
  30.9 0.2 select_reduce_fusion.19
  31.2 4.6 %shard_map.261 = f32[2048,128]{1,0:T(8,128)} custom-call(s32[16,4]{1,0:T(8,128)S(1)} %get-tuple-element.428.source, s32[16,4]{1,0:T(8,128)S(1)} %get-tuple-element.427.rows, s32[16,4]{1,0:T(8,128)S(1)} %get-tuple-element.426.first, f32[112,256,128]{2,1,0:T(8,128)} %bitcast.131), custom_call_target="tpu_custom_call" | custom-call | tf_op jit(solution)/shard_map/pallas_call | solution.py:431
  35.8 9.4 %all-to-all-start.5 = ((f32[32,64,128]{2,1,0:T(8,128)}), f32[32,64,128]{2,1,0:T(8,128)S(1)}, u32[]{:S(2)}, u32[]{:S(2)}) async-start(f32[32,64,128]{2,1,0:T(8,128)} %bitcast.61), calls=%async_computation.5 | async-start | bytes 2097152 | tf_op jit(solution)/shard_map/all_to_all | solution.py:618
  45.4 0.4 select_reduce_fusion.3
  46.0 0.2 select_reduce_fusion.6
  46.3 2.2 %select_reduce_fusion.2 = s32[4,32,32]{2,1,0:T(8,128)S(1)} fusion(s32[4,32,32]{2,1,0:T(8,128)S(1)} %copy.237, pred[32,32]{1,0:T(8,128)(4,1)S(1)} %bitcast.146), kind=kLoop, calls=%fused_computation.83 | loop fusion | flops 258048 | bytes 33792 | tf_op jit(solution)/shard_map/reduce_sum | solution.py:494
  48.8 0.6 fusion.32
  49.5 20.3 %all-to-all-done.5 = f32[32,64,128]{2,1,0:T(8,128)S(1)} async-done(((f32[32,64,128]{2,1,0:T(8,128)}), f32[32,64,128]{2,1,0:T(8,128)S(1)}, u32[]{:S(2)}, u32[]{:S(2)}) %all-to-all-start.5) | async-done | bytes 1048608 | tf_op jit(solution)/shard_map/all_to_all | solution.py:618
  69.8 3.0 %shard_map.262 = f32[2048,128]{1,0:T(8,128)} custom-call(s32[2048]{0:T(1024)S(1)} %min.31.idx, s32[32]{0:T(128)S(1)} %get-tuple-element.385.count, f32[2048,128]{1,0:T(8,128)S(1)} %bitcast.129), custom_call_target="tpu_custom_call" | custom-call | tf_op jit(solution)/shard_map/pallas_call | solution.py:445
  72.9 8.9 %all-to-all-start.6 = ((f32[32,64,128]{2,1,0:T(8,128)}), f32[32,64,128]{2,1,0:T(8,128)S(1)}, u32[]{:S(2)}, u32[]{:S(2)}) async-start(f32[32,64,128]{2,1,0:T(8,128)} %bitcast.63), calls=%async_computation.6 | async-start | bytes 2097152 | tf_op jit(solution)/shard_map/all_to_all | solution.py:618
  81.8 0.2 fusion.47
  82.2 0.2 fusion.45
  82.4 0.2 fusion.49
  82.8 0.7 compare_reduce_fusion.4
  83.5 0.7 compare_reduce_fusion.3
  85.6 0.7 compare_reduce_fusion.2
  86.9 3.1 %select_reduce_fusion.7 = (s32[16]{0:T(128)S(1)}, s32[16]{0:T(128)S(1)}, s32[16]{0:T(128)S(1)}, s32[16]{0:T(128)S(1)}, s32[16]{0:T(128)S(1)}, /*index=5*/s32[16]...) fusion(s32[32]{0:T(128)S(1)} %get-tuple-element.413, s32[32,16]{0,1:T(8,128)S(1)} %bitcast.142, ...), kind=kLoop, calls=%fused_computation.97 | loop fusion | flops 180064 | bytes 15808 | tf_op jit(solution)/shard_map/reduce_sum | solution.py:584
  90.1 0.1 reshape.816.tbl
  90.3 16.0 %all-to-all-done.6 = f32[32,64,128]{2,1,0:T(8,128)S(1)} async-done(((f32[32,64,128]{2,1,0:T(8,128)}), f32[32,64,128]{2,1,0:T(8,128)S(1)}, u32[]{:S(2)}, u32[]{:S(2)}) %all-to-all-start.6) | async-done | bytes 1048608 | tf_op jit(solution)/shard_map/all_to_all | solution.py:618
  106.3 9.1 %shard_map.263 = (f32[100,8,128]{2,1,0:T(8,128)S(1)}, f32[100,8,128]{2,1,0:T(8,128)S(1)}) custom-call(s32[160]{0:T(256)S(1)} %reshape.816.tbl, s32[51]{0:T(128)S(1)} %pad_add_fusion.4.out_tbl, f32[2048,128]{1,0:T(8,128)S(1)} %bitcast.130, f32[16,256,256]{2,1,0:T(8,128)} %bitcast.133), custom_call_target="tpu_custom_call" | custom-call | tf_op jit(solution)/shard_map/pallas_call | solution.py:455
  115.4 4.6 %collective-permute-start.8 = (f32[100,8,128]{2,1,0:T(8,128)S(1)}, f32[100,8,128]{2,1,0:T(8,128)S(1)}, u32[]{:S(2)}, u32[]{:S(2)}) collective-permute-start(f32[100,8,128]{2,1,0:T(8,128)S(1)} %get-tuple-element.152), channel_id=1, source_target_pairs={{0,1},{1,0},{2,3},{3,2},{4,5},{5,4},{6,7},{7,6},{8,9},{9,8},{10,11... | collective-permute-start | bytes 1228808 | tf_op jit(solution)/shard_map/ppermute | solution.py:614
  120.0 1.4 collective-permute-done.8
  121.5 0.5 collective-permute-start.9
  122.0 2.8 %collective-permute-start.11 = (f32[25,8,128]{2,1,0:T(8,128)S(1)}, f32[25,8,128]{2,1,0:T(8,128)S(1)}, u32[]{:S(2)}, u32[]{:S(2)}) collective-permute-start(f32[25,8,128]{2,1,0:T(8,128)S(1)} %get-tuple-element.408), channel_id=1, source_target_pairs={{0,6},{1,7},{2,4},{3,5},{4,2},{5,3},{6,0},{7,1},{8,14},{9,15},{10,... | collective-permute-start | bytes 307208 | tf_op jit(solution)/shard_map/ppermute | solution.py:614
  124.8 0.2 collective-permute-start.10
  125.1 0.6 collective-permute-done.9
  125.7 3.5 %collective-permute-done.11 = f32[25,8,128]{2,1,0:T(8,128)S(1)} collective-permute-done((f32[25,8,128]{2,1,0:T(8,128)S(1)}, f32[25,8,128]{2,1,0:T(8,128)S(1)}, u32[]{:S(2)}, u32[]{:S(2)}) %collective-permute-start.11) | collective-permute-done | bytes 102432 | tf_op jit(solution)/shard_map/ppermute | solution.py:614
  129.2 0.7 collective-permute-done.10
  129.9 3.0 %collective-permute-start.14 = (f32[25,8,128]{2,1,0:T(8,128)S(1)}, f32[25,8,128]{2,1,0:T(8,128)S(1)}, u32[]{:S(2)}, u32[]{:S(2)}) collective-permute-start(f32[25,8,128]{2,1,0:T(8,128)S(1)} %fusion.35), channel_id=1, source_target_pairs={{0,6},{1,7},{2,4},{3,5},{4,2},{5,3},{6,0},{7,1},{8,14},{9,15},{10,... | collective-permute-start | bytes 307208 | tf_op jit(solution)/shard_map/ppermute | solution.py:614
  132.8 0.7 collective-permute-start.12
  133.5 2.5 %collective-permute-done.14 = f32[25,8,128]{2,1,0:T(8,128)S(1)} collective-permute-done((f32[25,8,128]{2,1,0:T(8,128)S(1)}, f32[25,8,128]{2,1,0:T(8,128)S(1)}, u32[]{:S(2)}, u32[]{:S(2)}) %collective-permute-start.14) | collective-permute-done | bytes 102432 | tf_op jit(solution)/shard_map/ppermute | solution.py:614
  136.0 2.0 %collective-permute-done.13 = f32[25,8,128]{2,1,0:T(8,128)S(1)} collective-permute-done((f32[25,8,128]{2,1,0:T(8,128)S(1)}, f32[25,8,128]{2,1,0:T(8,128)S(1)}, u32[]{:S(2)}, u32[]{:S(2)}) %collective-permute-start.13) | collective-permute-done | bytes 102432 | tf_op jit(solution)/shard_map/ppermute | solution.py:614
  138.0 2.9 %collective-permute-start.15 = (f32[100,8,128]{2,1,0:T(8,128)S(1)}, f32[100,8,128]{2,1,0:T(8,128)S(1)}, u32[]{:S(2)}, u32[]{:S(2)}) collective-permute-start(f32[100,8,128]{2,1,0:T(8,128)S(1)} %pad_maximum_fusion.1), channel_id=1, source_target_pairs={{0,1},{1,0},{2,3},{3,2},{4,5},{5,4},{6,7},{7,6},{8,9},{9,8},{10,11... | collective-permute-start | bytes 1228808 | tf_op jit(solution)/shard_map/ppermute | solution.py:614
  140.9 0.5 slice.101
  142.1 0.2 collective-permute-done.15
  142.3 2.4 %conditional.2 = (f32[8,256,256]{2,1,0:T(8,128)}) conditional(s32[]{:T(128)} %bitcast.66, (s32[51]{0:T(128)S(1)}, s32[8]{0:T(128)S(1)}, s32[8]{0:T(128)S(1)}, f32[100,8,128]{2,1,0:T(8,128)S(1)}, f32[100,8,128]{2,1,0:T(8,128)S(1)}) %tuple.94, (s32[]{:T(128)}, s32[32,8]{0,1:T(8,128)S(1)}, s32[32,8]{0,1:T(8,128)S(1)}, s32[32,8]{0,1:T(8,128)S(1)}, ...), branch_computations={%region_23.24_spmd, %region_24.36_spmd} | conditional | flops 6548976128 | bytes 174507776 | solution.py:631
  142.3 2.3 %branch_0_fun.2 = f32[8,256,256]{2,1,0:T(8,128)} custom-call(s32[51]{0:T(128)S(1)} %get-tuple-element.102.out_tbl, s32[8]{0:T(128)S(1)} %get-tuple-element.103.left_sizes, s32[8]{0:T(128)S(1)} %get-tuple-element.104.right_sizes, f32[100,8,128]{2,1,0:T(8,128)S(1)} %get-tuple-element.105.own_ref, f32[100,8,128]{2,1,0:T(8,128)S(1)} %get-tuple-element.106.other_ref), custom_call_target="tpu_custom_call" | custom-call | tf_op jit(solution)/shard_map/cond/branch_0_fun/pallas_call | solution.py:472
  (78 shorter events, 2.2 us)
Async XLA Ops:
  7.9 21.4 %all-to-all-start.4 = ((s32[32,4,8]{2,1,0:T(4,128)}), s32[32,4,8]{2,1,0:T(4,128)S(1)}, u32[]{:S(2)}, u32[]{:S(2)}) async-start(s32[32,4,8]{2,1,0:T(4,128)} %broadcast_in_dim.364), calls=%async_computation.4 | async-start | bytes 131072 | tf_op jit(solution)/shard_map/all_to_all | solution.py:609
  19.8 10.6 %copy-start.7 = (pred[16,16]{1,0:T(8,128)(4,1)S(1)}, pred[16,16]{1,0:T(8,128)(4,1)}, u32[]{:S(2)}) copy-start(pred[16,16]{1,0:T(8,128)(4,1)} %constant.215.clone) | copy-start | bytes 772
  19.8 11.1 %copy-start.3 = (s32[1,16]{0,1:T(8,128)S(1)}, s32[1,16]{0,1:T(8,128)}, u32[]{:S(2)}) copy-start(s32[1,16]{0,1:T(8,128)} %constant.254) | copy-start | bytes 196
  19.8 11.1 %copy-start.4 = (s32[1,16]{0,1:T(8,128)S(1)}, s32[1,16]{0,1:T(8,128)}, u32[]{:S(2)}) copy-start(s32[1,16]{0,1:T(8,128)} %constant.253) | copy-start | bytes 196
  19.8 11.3 %copy-start.10 = (s32[4]{0:T(128)S(1)}, s32[4]{0:T(128)}, u32[]{:S(2)}) copy-start(s32[4]{0:T(128)} %constant.248) | copy-start | bytes 52
  19.8 11.3 %copy-start.11 = (s32[4]{0:T(128)S(1)}, s32[4]{0:T(128)}, u32[]{:S(2)}) copy-start(s32[4]{0:T(128)} %constant.246) | copy-start | bytes 52
  19.8 11.3 %copy-start.12 = (pred[4]{0:T(512)(128)(4,1)S(1)}, pred[4]{0:T(512)(128)(4,1)}, u32[]{:S(2)}) copy-start(pred[4]{0:T(512)(128)(4,1)} %constant.245) | copy-start | bytes 16
  19.8 11.3 %copy-start.13 = (s32[16]{0:T(128)S(1)}, s32[16]{0:T(128)}, u32[]{:S(2)}) copy-start(s32[16]{0:T(128)} %constant.244) | copy-start | bytes 196
  31.2 15.1 %copy-start.5 = (pred[32,32]{1,0:T(32,128)(4,1)S(1)}, pred[32,32]{1,0:T(32,128)(4,1)}, u32[]{:S(2)}) copy-start(pred[32,32]{1,0:T(32,128)(4,1)} %constant.217.clone) | copy-start | bytes 3076
  35.8 46.0 %copy-start.14 = (s32[16,1,1]{0,2,1:T(1,128)S(1)}, s32[16,1,1]{0,2,1:T(1,128)}, u32[]{:S(2)}) copy-start(s32[16,1,1]{0,2,1:T(1,128)} %constant.226.clone) | copy-start | bytes 196
  35.8 46.3 %copy-start.8 = (pred[8,8]{1,0:T(8,128)(4,1)S(1)}, pred[8,8]{1,0:T(8,128)(4,1)}, u32[]{:S(2)}) copy-start(pred[8,8]{1,0:T(8,128)(4,1)} %constant.218.clone) | copy-start | bytes 196
  35.8 51.1 %copy-start.6 = (pred[16,16]{1,0:T(8,128)(4,1)S(1)}, pred[16,16]{1,0:T(8,128)(4,1)}, u32[]{:S(2)}) copy-start(pred[16,16]{1,0:T(8,128)(4,1)} %constant.238) | copy-start | bytes 772
  35.8 34.0 %all-to-all-start.5 = ((f32[32,64,128]{2,1,0:T(8,128)}), f32[32,64,128]{2,1,0:T(8,128)S(1)}, u32[]{:S(2)}, u32[]{:S(2)}) async-start(f32[32,64,128]{2,1,0:T(8,128)} %bitcast.61), calls=%async_computation.5 | async-start | bytes 2097152 | tf_op jit(solution)/shard_map/all_to_all | solution.py:618
  72.9 33.4 %all-to-all-start.6 = ((f32[32,64,128]{2,1,0:T(8,128)}), f32[32,64,128]{2,1,0:T(8,128)S(1)}, u32[]{:S(2)}, u32[]{:S(2)}) async-start(f32[32,64,128]{2,1,0:T(8,128)} %bitcast.63), calls=%async_computation.6 | async-start | bytes 2097152 | tf_op jit(solution)/shard_map/all_to_all | solution.py:618
  106.3 36.0 %copy-start.1 = (s32[8]{0:T(128)S(1)}, s32[8]{0:T(128)}, u32[]{:S(2)}) copy-start(s32[8]{0:T(128)} %left_sizes.1) | copy-start | bytes 100
  106.3 36.0 %copy-start.2 = (s32[8]{0:T(128)S(1)}, s32[8]{0:T(128)}, u32[]{:S(2)}) copy-start(s32[8]{0:T(128)} %right_sizes.1) | copy-start | bytes 100
  106.3 36.0 %copy-start.9 = (s32[2,8]{1,0:T(2,128)S(1)}, s32[2,8]{1,0:T(2,128)}, u32[]{:S(2)}) copy-start(s32[2,8]{1,0:T(2,128)} %param.36) | copy-start | bytes 196
  115.4 6.0 %collective-permute-start.8 = (f32[100,8,128]{2,1,0:T(8,128)S(1)}, f32[100,8,128]{2,1,0:T(8,128)S(1)}, u32[]{:S(2)}, u32[]{:S(2)}) collective-permute-start(f32[100,8,128]{2,1,0:T(8,128)S(1)} %get-tuple-element.152), channel_id=1, source_target_pairs={{0,1},{1,0},{2,3},{3,2},{4,5},{5,4},{6,7},{7,6},{8,9},{9,8},{10,11... | collective-permute-start | bytes 1228808 | tf_op jit(solution)/shard_map/ppermute | solution.py:614
  121.5 4.2 %collective-permute-start.9 = (f32[25,8,128]{2,1,0:T(8,128)S(1)}, f32[25,8,128]{2,1,0:T(8,128)S(1)}, u32[]{:S(2)}, u32[]{:S(2)}) collective-permute-start(f32[25,8,128]{2,1,0:T(8,128)S(1)} %get-tuple-element.407), channel_id=1, source_target_pairs={{0,2},{1,3},{2,0},{3,1},{4,6},{5,7},{6,4},{7,5},{8,10},{9,11},{10,... | collective-permute-start | bytes 307208 | tf_op jit(solution)/shard_map/ppermute | solution.py:614
  122.0 7.2 %collective-permute-start.11 = (f32[25,8,128]{2,1,0:T(8,128)S(1)}, f32[25,8,128]{2,1,0:T(8,128)S(1)}, u32[]{:S(2)}, u32[]{:S(2)}) collective-permute-start(f32[25,8,128]{2,1,0:T(8,128)S(1)} %get-tuple-element.408), channel_id=1, source_target_pairs={{0,6},{1,7},{2,4},{3,5},{4,2},{5,3},{6,0},{7,1},{8,14},{9,15},{10,... | collective-permute-start | bytes 307208 | tf_op jit(solution)/shard_map/ppermute | solution.py:614
  124.8 5.0 %collective-permute-start.10 = (f32[25,8,128]{2,1,0:T(8,128)S(1)}, f32[25,8,128]{2,1,0:T(8,128)S(1)}, u32[]{:S(2)}, u32[]{:S(2)}) collective-permute-start(f32[25,8,128]{2,1,0:T(8,128)S(1)} %get-tuple-element.409), channel_id=1, source_target_pairs={{0,4},{1,5},{2,6},{3,7},{4,0},{5,1},{6,2},{7,3},{8,12},{9,13},{10,... | collective-permute-start | bytes 307208 | tf_op jit(solution)/shard_map/ppermute | solution.py:614
  129.9 6.1 %collective-permute-start.14 = (f32[25,8,128]{2,1,0:T(8,128)S(1)}, f32[25,8,128]{2,1,0:T(8,128)S(1)}, u32[]{:S(2)}, u32[]{:S(2)}) collective-permute-start(f32[25,8,128]{2,1,0:T(8,128)S(1)} %fusion.35), channel_id=1, source_target_pairs={{0,6},{1,7},{2,4},{3,5},{4,2},{5,3},{6,0},{7,1},{8,14},{9,15},{10,... | collective-permute-start | bytes 307208 | tf_op jit(solution)/shard_map/ppermute | solution.py:614
  132.8 5.1 %collective-permute-start.13 = (f32[25,8,128]{2,1,0:T(8,128)S(1)}, f32[25,8,128]{2,1,0:T(8,128)S(1)}, u32[]{:S(2)}, u32[]{:S(2)}) collective-permute-start(f32[25,8,128]{2,1,0:T(8,128)S(1)} %fusion.35), channel_id=1, source_target_pairs={{0,4},{1,5},{2,6},{3,7},{4,0},{5,1},{6,2},{7,3},{8,12},{9,13},{10,... | collective-permute-start | bytes 307208 | tf_op jit(solution)/shard_map/ppermute | solution.py:614
  132.8 5.1 %collective-permute-start.12 = (f32[25,8,128]{2,1,0:T(8,128)S(1)}, f32[25,8,128]{2,1,0:T(8,128)S(1)}, u32[]{:S(2)}, u32[]{:S(2)}) collective-permute-start(f32[25,8,128]{2,1,0:T(8,128)S(1)} %fusion.35), channel_id=1, source_target_pairs={{0,2},{1,3},{2,0},{3,1},{4,6},{5,7},{6,4},{7,5},{8,10},{9,11},{10,... | collective-permute-start | bytes 307208 | tf_op jit(solution)/shard_map/ppermute | solution.py:614
  138.0 4.3 %collective-permute-start.15 = (f32[100,8,128]{2,1,0:T(8,128)S(1)}, f32[100,8,128]{2,1,0:T(8,128)S(1)}, u32[]{:S(2)}, u32[]{:S(2)}) collective-permute-start(f32[100,8,128]{2,1,0:T(8,128)S(1)} %pad_maximum_fusion.1), channel_id=1, source_target_pairs={{0,1},{1,0},{2,3},{3,2},{4,5},{5,4},{6,7},{7,6},{8,9},{9,8},{10,11... | collective-permute-start | bytes 1228808 | tf_op jit(solution)/shard_map/ppermute | solution.py:614

commit v6 on v5

--- a/solution.py
+++ b/solution.py
@@ -604,8 +604,10 @@
     core, chip = member & 1, member >> 1
     strips = carry_call(left_sizes, right_sizes, psi_blocks, right_env)
     strips = strips.reshape(HELD * STRIPS, BLK, LANES)
-    mine = jnp.concatenate([left_sizes[None], right_sizes[None], dest_sector])
-    mine = jnp.broadcast_to(mine[None], (PEERS, 4, HELD))
+    facts = [left_sizes[None], right_sizes[None], dest_sector]
+    mine = jnp.concatenate(
+        [jnp.broadcast_to(v[None], (PEERS,) + v.shape) for v in facts], axis=1
+    )
     facts = lax.all_to_all(mine, "sec", 0, 0, tiled=True)
     tables = make_tables(facts, me, core, chip)
     send_tbl, relay_tbl, land_tbl, out_tbl = tables

time: 152 us -> 153 us (level)
  local copies, waits for them, and re-layouts: 4.08 us -> 6.35 us
    broadcast_in_dim x1 -> x3, local copies, waits for them, and re-layouts: 0.64 us -> 2.19 us  [per_device(): jnp.broadcast_to(v[None], (PEERS,) + v.shape)]
where the time goes in v6:
time: 153 us
  waiting for transfers between devices  46.9 us (31%)
  starting transfers between devices  44.5 us (29%)
  Pallas kernels  29.1 us (19%)
  between operations  16.4 us (11%)
  other arithmetic  9.76 us (6%)
  local copies, waits for them, and re-layouts  6.35 us (4%)
    all_to_all x2, waiting for transfers between devices, exchange(): lax.all_to_all(rows.reshape(PEERS, slot, LANES), 'sec', 0, 0, tiled=True)  36.3 us
    all_to_all x2, starting transfers between devices, exchange(): lax.all_to_all(rows.reshape(PEERS, slot, LANES), 'sec', 0, 0, tiled=True)  18.1 us
    ppermute x8, starting transfers between devices, swap(): return lax.ppermute(values, 'term', [(i, i ^ bits) for i in range(MEMBERS)])  14.5 us
    all_to_all x1, starting transfers between devices, per_device(): facts = lax.all_to_all(mine, 'sec', 0, 0, tiled=True)  11.9 us
    ppermute x8, waiting for transfers between devices, swap(): return lax.ppermute(values, 'term', [(i, i ^ bits) for i in range(MEMBERS)])  10.6 us
    pallas_call x1, Pallas kernels, land_call(): pl.pallas_call(functools.partial(land_kernel, slot), out_shape=[floats(4...  9.63 us
    pallas_call x1, Pallas kernels, carry_call(): pl.pallas_call(carry_kernel, grid=(HELD // TOGETHER,), out_shape=floats(H...  9.43 us
    pallas_call x1, Pallas kernels, send_call(): pl.pallas_call(functools.partial(send_kernel, slot), out_shape=floats(PEE...  4.54 us
  transfers between devices with their start and end apart: 11, of which 9 were waited for; matrix products, arithmetic and copies ran while one was open for 7% of the time, Pallas kernels for 6%

profile of v6, /device:TPU:1, one launch (start us, length us, event | category | flops | bytes accessed | tf_op | source)
XLA Modules:
  0.0 153.2 jit_solution(6091484339726667259)
XLA Ops:
  6.5 0.7 broadcast_in_dim.366
  7.3 0.7 broadcast_in_dim.367
  8.0 0.7 broadcast_in_dim.368
  8.7 0.7 copy.265
  9.5 11.9 %all-to-all-start.4 = ((s32[32,4,8]{2,1,0:T(4,128)}), s32[32,4,8]{2,1,0:T(4,128)S(1)}, u32[]{:S(2)}, u32[]{:S(2)}) async-start(s32[32,4,8]{2,1,0:T(4,128)} %copy.265), calls=%async_computation.4 | async-start | bytes 131072 | tf_op jit(solution)/shard_map/all_to_all | solution.py:611
  21.4 9.4 %shard_map.260 = f32[8,14,256,128]{3,2,1,0:T(8,128)} custom-call(s32[8]{0:T(128)} %left_sizes.1, s32[8]{0:T(128)} %right_sizes.1, f32[8,256,256]{2,1,0:T(8,128)} %psi_ref.1, f32[2,8,256,256]{3,2,1,0:T(8,128)} %right_ref.1), custom_call_target="tpu_custom_call" | custom-call | flops 1610612736 | bytes 25165824 | tf_op jit(solution)/shard_map/pallas_call | solution.py:412
  30.9 0.1 eq.113
  31.4 0.2 select_reduce_fusion.5
  31.7 0.1 iota_compare_fusion.11
  31.9 0.1 select_reduce_fusion.17
  32.0 0.2 dynamic-slice_reduce_fusion
  32.2 0.2 dynamic-slice_reduce_fusion.2
  32.4 0.2 select_reduce_fusion.19
  32.8 4.5 %shard_map.261 = f32[2048,128]{1,0:T(8,128)} custom-call(s32[16,4]{1,0:T(8,128)S(1)} %get-tuple-element.458.source, s32[16,4]{1,0:T(8,128)S(1)} %get-tuple-element.457.rows, s32[16,4]{1,0:T(8,128)S(1)} %get-tuple-element.456.first, f32[112,256,128]{2,1,0:T(8,128)} %bitcast.129), custom_call_target="tpu_custom_call" | custom-call | tf_op jit(solution)/shard_map/pallas_call | solution.py:431
  37.4 9.3 %all-to-all-start.5 = ((f32[32,64,128]{2,1,0:T(8,128)}), f32[32,64,128]{2,1,0:T(8,128)S(1)}, u32[]{:S(2)}, u32[]{:S(2)}) async-start(f32[32,64,128]{2,1,0:T(8,128)} %bitcast.59), calls=%async_computation.5 | async-start | bytes 2097152 | tf_op jit(solution)/shard_map/all_to_all | solution.py:620
  46.9 0.4 select_reduce_fusion.3
  47.4 0.2 select_reduce_fusion.6
  47.8 2.2 %select_reduce_fusion.2 = s32[4,32,32]{2,1,0:T(8,128)S(1)} fusion(s32[4,32,32]{2,1,0:T(8,128)S(1)} %copy.277, pred[32,32]{1,0:T(8,128)(4,1)S(1)} %bitcast.142), kind=kLoop, calls=%fused_computation.83 | loop fusion | flops 258048 | bytes 33792 | tf_op jit(solution)/shard_map/reduce_sum | solution.py:494
  50.3 0.6 fusion.32
  50.9 20.4 %all-to-all-done.5 = f32[32,64,128]{2,1,0:T(8,128)S(1)} async-done(((f32[32,64,128]{2,1,0:T(8,128)}), f32[32,64,128]{2,1,0:T(8,128)S(1)}, u32[]{:S(2)}, u32[]{:S(2)}) %all-to-all-start.5) | async-done | bytes 1048608 | tf_op jit(solution)/shard_map/all_to_all | solution.py:620
  71.4 3.1 %shard_map.262 = f32[2048,128]{1,0:T(8,128)} custom-call(s32[2048]{0:T(1024)S(1)} %min.31.idx, s32[32]{0:T(128)S(1)} %get-tuple-element.415.count, f32[2048,128]{1,0:T(8,128)S(1)} %bitcast.127), custom_call_target="tpu_custom_call" | custom-call | tf_op jit(solution)/shard_map/pallas_call | solution.py:445
  74.4 8.8 %all-to-all-start.6 = ((f32[32,64,128]{2,1,0:T(8,128)}), f32[32,64,128]{2,1,0:T(8,128)S(1)}, u32[]{:S(2)}, u32[]{:S(2)}) async-start(f32[32,64,128]{2,1,0:T(8,128)} %bitcast.61), calls=%async_computation.6 | async-start | bytes 2097152 | tf_op jit(solution)/shard_map/all_to_all | solution.py:620
  83.3 0.2 fusion.47
  83.6 0.2 fusion.45
  83.8 0.2 fusion.49
  84.2 0.7 compare_reduce_fusion.4
  84.9 0.7 compare_reduce_fusion.3
  87.0 0.7 compare_reduce_fusion.2
  88.3 3.1 %select_reduce_fusion.7 = (s32[16]{0:T(128)S(1)}, s32[16]{0:T(128)S(1)}, s32[16]{0:T(128)S(1)}, s32[16]{0:T(128)S(1)}, s32[16]{0:T(128)S(1)}, /*index=5*/s32[16]...) fusion(s32[32]{0:T(128)S(1)} %get-tuple-element.443, s32[32,16]{0,1:T(8,128)S(1)} %bitcast.140, ...), kind=kLoop, calls=%fused_computation.97 | loop fusion | flops 180064 | bytes 15808 | tf_op jit(solution)/shard_map/reduce_sum | solution.py:584
  91.8 15.9 %all-to-all-done.6 = f32[32,64,128]{2,1,0:T(8,128)S(1)} async-done(((f32[32,64,128]{2,1,0:T(8,128)}), f32[32,64,128]{2,1,0:T(8,128)S(1)}, u32[]{:S(2)}, u32[]{:S(2)}) %all-to-all-start.6) | async-done | bytes 1048608 | tf_op jit(solution)/shard_map/all_to_all | solution.py:620
  107.6 9.6 %shard_map.263 = (f32[100,8,128]{2,1,0:T(8,128)S(1)}, f32[100,8,128]{2,1,0:T(8,128)S(1)}) custom-call(s32[160]{0:T(256)S(1)} %reshape.822.tbl, s32[51]{0:T(128)S(1)} %pad_add_fusion.4.out_tbl, f32[2048,128]{1,0:T(8,128)S(1)} %bitcast.128, f32[16,256,256]{2,1,0:T(8,128)} %bitcast.131), custom_call_target="tpu_custom_call" | custom-call | tf_op jit(solution)/shard_map/pallas_call | solution.py:455
  117.2 4.9 %collective-permute-start.8 = (f32[100,8,128]{2,1,0:T(8,128)S(1)}, f32[100,8,128]{2,1,0:T(8,128)S(1)}, u32[]{:S(2)}, u32[]{:S(2)}) collective-permute-start(f32[100,8,128]{2,1,0:T(8,128)S(1)} %get-tuple-element.152), channel_id=1, source_target_pairs={{0,1},{1,0},{2,3},{3,2},{4,5},{5,4},{6,7},{7,6},{8,9},{9,8},{10,11... | collective-permute-start | bytes 1228808 | tf_op jit(solution)/shard_map/ppermute | solution.py:616
  122.2 1.4 collective-permute-done.8
  123.6 0.6 collective-permute-start.9
  124.2 2.4 %collective-permute-start.11 = (f32[25,8,128]{2,1,0:T(8,128)S(1)}, f32[25,8,128]{2,1,0:T(8,128)S(1)}, u32[]{:S(2)}, u32[]{:S(2)}) collective-permute-start(f32[25,8,128]{2,1,0:T(8,128)S(1)} %get-tuple-element.438), channel_id=1, source_target_pairs={{0,6},{1,7},{2,4},{3,5},{4,2},{5,3},{6,0},{7,1},{8,14},{9,15},{10,... | collective-permute-start | bytes 307208 | tf_op jit(solution)/shard_map/ppermute | solution.py:616
  126.6 0.4 collective-permute-start.10
  127.0 0.8 collective-permute-done.9
  127.8 2.8 %collective-permute-done.11 = f32[25,8,128]{2,1,0:T(8,128)S(1)} collective-permute-done((f32[25,8,128]{2,1,0:T(8,128)S(1)}, f32[25,8,128]{2,1,0:T(8,128)S(1)}, u32[]{:S(2)}, u32[]{:S(2)}) %collective-permute-start.11) | collective-permute-done | bytes 102432 | tf_op jit(solution)/shard_map/ppermute | solution.py:616
  130.6 1.0 collective-permute-done.10
  131.6 2.7 %collective-permute-start.14 = (f32[25,8,128]{2,1,0:T(8,128)S(1)}, f32[25,8,128]{2,1,0:T(8,128)S(1)}, u32[]{:S(2)}, u32[]{:S(2)}) collective-permute-start(f32[25,8,128]{2,1,0:T(8,128)S(1)} %fusion.35), channel_id=1, source_target_pairs={{0,6},{1,7},{2,4},{3,5},{4,2},{5,3},{6,0},{7,1},{8,14},{9,15},{10,... | collective-permute-start | bytes 307208 | tf_op jit(solution)/shard_map/ppermute | solution.py:616
  134.3 0.7 collective-permute-start.12
  135.0 2.4 %collective-permute-done.14 = f32[25,8,128]{2,1,0:T(8,128)S(1)} collective-permute-done((f32[25,8,128]{2,1,0:T(8,128)S(1)}, f32[25,8,128]{2,1,0:T(8,128)S(1)}, u32[]{:S(2)}, u32[]{:S(2)}) %collective-permute-start.14) | collective-permute-done | bytes 102432 | tf_op jit(solution)/shard_map/ppermute | solution.py:616
  137.4 2.0 %collective-permute-done.13 = f32[25,8,128]{2,1,0:T(8,128)S(1)} collective-permute-done((f32[25,8,128]{2,1,0:T(8,128)S(1)}, f32[25,8,128]{2,1,0:T(8,128)S(1)}, u32[]{:S(2)}, u32[]{:S(2)}) %collective-permute-start.13) | collective-permute-done | bytes 102432 | tf_op jit(solution)/shard_map/ppermute | solution.py:616
  139.5 2.9 %collective-permute-start.15 = (f32[100,8,128]{2,1,0:T(8,128)S(1)}, f32[100,8,128]{2,1,0:T(8,128)S(1)}, u32[]{:S(2)}, u32[]{:S(2)}) collective-permute-start(f32[100,8,128]{2,1,0:T(8,128)S(1)} %pad_maximum_fusion.1), channel_id=1, source_target_pairs={{0,1},{1,0},{2,3},{3,2},{4,5},{5,4},{6,7},{7,6},{8,9},{9,8},{10,11... | collective-permute-start | bytes 1228808 | tf_op jit(solution)/shard_map/ppermute | solution.py:616
  142.4 0.5 slice.101
  143.5 0.2 collective-permute-done.15
  143.8 2.6 %conditional.2 = (f32[8,256,256]{2,1,0:T(8,128)}) conditional(s32[]{:T(128)} %bitcast.64, (s32[51]{0:T(128)S(1)}, s32[8]{0:T(128)S(1)}, s32[8]{0:T(128)S(1)}, f32[100,8,128]{2,1,0:T(8,128)S(1)}, f32[100,8,128]{2,1,0:T(8,128)S(1)}) %tuple.96, (s32[]{:T(128)}, s32[32,8]{0,1:T(8,128)S(1)}, s32[32,8]{0,1:T(8,128)S(1)}, s32[32,8]{0,1:T(8,128)S(1)}, ...), branch_computations={%region_23.24_spmd, %region_24.36_spmd} | conditional | flops 6548976128 | bytes 174507776 | solution.py:633
  143.8 2.4 %branch_0_fun.2 = f32[8,256,256]{2,1,0:T(8,128)} custom-call(s32[51]{0:T(128)S(1)} %get-tuple-element.102.out_tbl, s32[8]{0:T(128)S(1)} %get-tuple-element.103.left_sizes, s32[8]{0:T(128)S(1)} %get-tuple-element.104.right_sizes, f32[100,8,128]{2,1,0:T(8,128)S(1)} %get-tuple-element.105.own_ref, f32[100,8,128]{2,1,0:T(8,128)S(1)} %get-tuple-element.106.other_ref), custom_call_target="tpu_custom_call" | custom-call | tf_op jit(solution)/shard_map/cond/branch_0_fun/pallas_call | solution.py:472
  (81 shorter events, 2.3 us)
Async XLA Ops:
  9.5 21.4 %all-to-all-start.4 = ((s32[32,4,8]{2,1,0:T(4,128)}), s32[32,4,8]{2,1,0:T(4,128)S(1)}, u32[]{:S(2)}, u32[]{:S(2)}) async-start(s32[32,4,8]{2,1,0:T(4,128)} %copy.265), calls=%async_computation.4 | async-start | bytes 131072 | tf_op jit(solution)/shard_map/all_to_all | solution.py:611
  21.3 10.6 %copy-start.7 = (pred[16,16]{1,0:T(8,128)(4,1)S(1)}, pred[16,16]{1,0:T(8,128)(4,1)}, u32[]{:S(2)}) copy-start(pred[16,16]{1,0:T(8,128)(4,1)} %constant.215.clone) | copy-start | bytes 772
  21.3 11.1 %copy-start.3 = (s32[1,16]{0,1:T(8,128)S(1)}, s32[1,16]{0,1:T(8,128)}, u32[]{:S(2)}) copy-start(s32[1,16]{0,1:T(8,128)} %constant.254) | copy-start | bytes 196
  21.4 11.1 %copy-start.4 = (s32[1,16]{0,1:T(8,128)S(1)}, s32[1,16]{0,1:T(8,128)}, u32[]{:S(2)}) copy-start(s32[1,16]{0,1:T(8,128)} %constant.253) | copy-start | bytes 196
  21.4 11.3 %copy-start.10 = (s32[4]{0:T(128)S(1)}, s32[4]{0:T(128)}, u32[]{:S(2)}) copy-start(s32[4]{0:T(128)} %constant.248) | copy-start | bytes 52
  21.4 11.3 %copy-start.11 = (s32[4]{0:T(128)S(1)}, s32[4]{0:T(128)}, u32[]{:S(2)}) copy-start(s32[4]{0:T(128)} %constant.246) | copy-start | bytes 52
  21.4 11.3 %copy-start.12 = (pred[4]{0:T(512)(128)(4,1)S(1)}, pred[4]{0:T(512)(128)(4,1)}, u32[]{:S(2)}) copy-start(pred[4]{0:T(512)(128)(4,1)} %constant.245) | copy-start | bytes 16
  21.4 11.3 %copy-start.13 = (s32[16]{0:T(128)S(1)}, s32[16]{0:T(128)}, u32[]{:S(2)}) copy-start(s32[16]{0:T(128)} %constant.244) | copy-start | bytes 196
  32.8 15.0 %copy-start.5 = (pred[32,32]{1,0:T(32,128)(4,1)S(1)}, pred[32,32]{1,0:T(32,128)(4,1)}, u32[]{:S(2)}) copy-start(pred[32,32]{1,0:T(32,128)(4,1)} %constant.217.clone) | copy-start | bytes 3076
  37.3 45.9 %copy-start.14 = (s32[16,1,1]{0,2,1:T(1,128)S(1)}, s32[16,1,1]{0,2,1:T(1,128)}, u32[]{:S(2)}) copy-start(s32[16,1,1]{0,2,1:T(1,128)} %constant.226.clone) | copy-start | bytes 196
  37.4 46.1 %copy-start.9 = (pred[8,8]{1,0:T(8,128)(4,1)S(1)}, pred[8,8]{1,0:T(8,128)(4,1)}, u32[]{:S(2)}) copy-start(pred[8,8]{1,0:T(8,128)(4,1)} %constant.218.clone) | copy-start | bytes 196
  37.4 51.0 %copy-start.6 = (pred[16,16]{1,0:T(8,128)(4,1)S(1)}, pred[16,16]{1,0:T(8,128)(4,1)}, u32[]{:S(2)}) copy-start(pred[16,16]{1,0:T(8,128)(4,1)} %constant.238) | copy-start | bytes 772
  37.4 34.0 %all-to-all-start.5 = ((f32[32,64,128]{2,1,0:T(8,128)}), f32[32,64,128]{2,1,0:T(8,128)S(1)}, u32[]{:S(2)}, u32[]{:S(2)}) async-start(f32[32,64,128]{2,1,0:T(8,128)} %bitcast.59), calls=%async_computation.5 | async-start | bytes 2097152 | tf_op jit(solution)/shard_map/all_to_all | solution.py:620
  74.4 33.2 %all-to-all-start.6 = ((f32[32,64,128]{2,1,0:T(8,128)}), f32[32,64,128]{2,1,0:T(8,128)S(1)}, u32[]{:S(2)}, u32[]{:S(2)}) async-start(f32[32,64,128]{2,1,0:T(8,128)} %bitcast.61), calls=%async_computation.6 | async-start | bytes 2097152 | tf_op jit(solution)/shard_map/all_to_all | solution.py:620
  107.6 36.2 %copy-start.1 = (s32[8]{0:T(128)S(1)}, s32[8]{0:T(128)}, u32[]{:S(2)}) copy-start(s32[8]{0:T(128)} %left_sizes.1) | copy-start | bytes 100
  107.6 36.2 %copy-start.2 = (s32[8]{0:T(128)S(1)}, s32[8]{0:T(128)}, u32[]{:S(2)}) copy-start(s32[8]{0:T(128)} %right_sizes.1) | copy-start | bytes 100
  107.6 36.2 %copy-start.8 = (s32[2,8]{1,0:T(2,128)S(1)}, s32[2,8]{1,0:T(2,128)}, u32[]{:S(2)}) copy-start(s32[2,8]{1,0:T(2,128)} %param.36) | copy-start | bytes 196
  117.2 6.3 %collective-permute-start.8 = (f32[100,8,128]{2,1,0:T(8,128)S(1)}, f32[100,8,128]{2,1,0:T(8,128)S(1)}, u32[]{:S(2)}, u32[]{:S(2)}) collective-permute-start(f32[100,8,128]{2,1,0:T(8,128)S(1)} %get-tuple-element.152), channel_id=1, source_target_pairs={{0,1},{1,0},{2,3},{3,2},{4,5},{5,4},{6,7},{7,6},{8,9},{9,8},{10,11... | collective-permute-start | bytes 1228808 | tf_op jit(solution)/shard_map/ppermute | solution.py:616
  123.6 4.2 %collective-permute-start.9 = (f32[25,8,128]{2,1,0:T(8,128)S(1)}, f32[25,8,128]{2,1,0:T(8,128)S(1)}, u32[]{:S(2)}, u32[]{:S(2)}) collective-permute-start(f32[25,8,128]{2,1,0:T(8,128)S(1)} %get-tuple-element.437), channel_id=1, source_target_pairs={{0,2},{1,3},{2,0},{3,1},{4,6},{5,7},{6,4},{7,5},{8,10},{9,11},{10,... | collective-permute-start | bytes 307208 | tf_op jit(solution)/shard_map/ppermute | solution.py:616
  124.2 6.4 %collective-permute-start.11 = (f32[25,8,128]{2,1,0:T(8,128)S(1)}, f32[25,8,128]{2,1,0:T(8,128)S(1)}, u32[]{:S(2)}, u32[]{:S(2)}) collective-permute-start(f32[25,8,128]{2,1,0:T(8,128)S(1)} %get-tuple-element.438), channel_id=1, source_target_pairs={{0,6},{1,7},{2,4},{3,5},{4,2},{5,3},{6,0},{7,1},{8,14},{9,15},{10,... | collective-permute-start | bytes 307208 | tf_op jit(solution)/shard_map/ppermute | solution.py:616
  126.6 5.0 %collective-permute-start.10 = (f32[25,8,128]{2,1,0:T(8,128)S(1)}, f32[25,8,128]{2,1,0:T(8,128)S(1)}, u32[]{:S(2)}, u32[]{:S(2)}) collective-permute-start(f32[25,8,128]{2,1,0:T(8,128)S(1)} %get-tuple-element.439), channel_id=1, source_target_pairs={{0,4},{1,5},{2,6},{3,7},{4,0},{5,1},{6,2},{7,3},{8,12},{9,13},{10,... | collective-permute-start | bytes 307208 | tf_op jit(solution)/shard_map/ppermute | solution.py:616
  131.6 5.8 %collective-permute-start.14 = (f32[25,8,128]{2,1,0:T(8,128)S(1)}, f32[25,8,128]{2,1,0:T(8,128)S(1)}, u32[]{:S(2)}, u32[]{:S(2)}) collective-permute-start(f32[25,8,128]{2,1,0:T(8,128)S(1)} %fusion.35), channel_id=1, source_target_pairs={{0,6},{1,7},{2,4},{3,5},{4,2},{5,3},{6,0},{7,1},{8,14},{9,15},{10,... | collective-permute-start | bytes 307208 | tf_op jit(solution)/shard_map/ppermute | solution.py:616
  134.3 5.1 %collective-permute-start.13 = (f32[25,8,128]{2,1,0:T(8,128)S(1)}, f32[25,8,128]{2,1,0:T(8,128)S(1)}, u32[]{:S(2)}, u32[]{:S(2)}) collective-permute-start(f32[25,8,128]{2,1,0:T(8,128)S(1)} %fusion.35), channel_id=1, source_target_pairs={{0,4},{1,5},{2,6},{3,7},{4,0},{5,1},{6,2},{7,3},{8,12},{9,13},{10,... | collective-permute-start | bytes 307208 | tf_op jit(solution)/shard_map/ppermute | solution.py:616
  134.3 5.1 %collective-permute-start.12 = (f32[25,8,128]{2,1,0:T(8,128)S(1)}, f32[25,8,128]{2,1,0:T(8,128)S(1)}, u32[]{:S(2)}, u32[]{:S(2)}) collective-permute-start(f32[25,8,128]{2,1,0:T(8,128)S(1)} %fusion.35), channel_id=1, source_target_pairs={{0,2},{1,3},{2,0},{3,1},{4,6},{5,7},{6,4},{7,5},{8,10},{9,11},{10,... | collective-permute-start | bytes 307208 | tf_op jit(solution)/shard_map/ppermute | solution.py:616
  139.5 4.3 %collective-permute-start.15 = (f32[100,8,128]{2,1,0:T(8,128)S(1)}, f32[100,8,128]{2,1,0:T(8,128)S(1)}, u32[]{:S(2)}, u32[]{:S(2)}) collective-permute-start(f32[100,8,128]{2,1,0:T(8,128)S(1)} %pad_maximum_fusion.1), channel_id=1, source_target_pairs={{0,1},{1,0},{2,3},{3,2},{4,5},{5,4},{6,7},{7,6},{8,9},{9,8},{10,11... | collective-permute-start | bytes 1228808 | tf_op jit(solution)/shard_map/ppermute | solution.py:616
